TPU v7x, 32 devices: a whole 2x2x4 slice. The times are simulated.
32 devices in a mesh: tm: 4 (over y, core), sta: 8 (over z, x).
Axes of the slice: x: 2, y: 2, z: 4, core: 2. Of those that a mesh axis runs over, the one named last changes fastest.
Arguments:
- spectra: bfloat16 [4, 512, 2048], P('tm', 'sta'), may hold values from -5 to 5
- pair_list: int32 [4, 8, 256], P('tm', 'sta'), may hold values from 0 to 511, as said below
- pair_stations: int32 [2, 4096], P(None, 'sta'), may hold values from 0 to 511
- owner_code: int32 [4096], P('sta'), may hold values from 0 to 1023, as said below
Outputs:
- stack: float32 [8192, 1024], P(('tm', 'sta'))
Inputs may be any that keep to these rules, and one draw needn't show every extreme that they name: `pair_list`: within each (g, s) the entries are distinct catalogue numbers below 512. `owner_code`: within each catalogue of 512 pairs the codes are distinct; each owner (code // 256) holds at most 256 pairs of a catalogue, and in every catalogue one owner holds exactly 256.
All inputs are finite; a program needn't handle non-finite values.
Results may differ from a plain program's by a relative error of at most 0.0003.
Values may be sent and summed in bfloat16 or wider, within the bound.
No kernel may reach another device: no remote copies, remote signals or barrier semaphores. Data moves between devices by JAX's collectives and lax.ppermute only.
A program may use at most 64 MiB of HBM per device.

v0:
```python
import jax
import jax.numpy as jnp
from jax import lax
from jax.sharding import PartitionSpec as P

LAGS = 1024


def lag_table(bins, lags):
    bin_index = jnp.arange(bins, dtype=jnp.int32)[:, None]
    lag_index = jnp.arange(lags, dtype=jnp.int32)[None, :] - lags // 2
    phase = (bin_index * lag_index % (2 * bins)).astype(jnp.float32) * (jnp.pi / bins)
    scale = 1.0 / bins**0.5
    return jnp.concatenate([jnp.cos(phase) * scale, -jnp.sin(phase) * scale], axis=0)


def cross_spectra(first, second, bins):
    first = first.astype(jnp.float32)
    second = second.astype(jnp.float32)
    real_a, imag_a = (first[..., :bins], first[..., bins:])
    real_b, imag_b = (second[..., :bins], second[..., bins:])
    real_c = real_a * real_b + imag_a * imag_b
    imag_c = real_a * imag_b - imag_a * real_b
    return jnp.concatenate([real_c, imag_c], axis=-1)


def local(spectra, pair_list, pair_stations, owner_code):
    local_spectra = spectra[0]
    width = local_spectra.shape[1]
    bins = width // 2
    catalogue = pair_stations.shape[1]
    groups = lax.axis_size("tm")
    capacity = 2 * catalogue // groups
    listed = pair_list[0, 0]
    first_station = pair_stations[0][listed]
    second_station = pair_stations[1][listed]
    codes = owner_code[listed]
    table = lag_table(bins, LAGS)
    all_spectra = lax.all_gather(local_spectra, "sta", axis=0, tiled=True)
    first = all_spectra[first_station]
    second = all_spectra[second_station]
    cross = cross_spectra(first, second, bins)
    partial_lags = jnp.dot(
        cross, table, precision=lax.Precision.HIGHEST, preferred_element_type=jnp.float32
    )
    slots = jnp.arange(capacity * lax.axis_size("tm"), dtype=jnp.int32)
    select = (slots[:, None] == codes[None, :]).astype(jnp.float32)
    return lax.psum_scatter(
        jnp.dot(
            select,
            partial_lags,
            precision=lax.Precision.HIGHEST,
            preferred_element_type=jnp.float32,
        ),
        "tm",
        scatter_dimension=0,
        tiled=True,
    )


def solution(mesh):
    return jax.shard_map(
        local,
        mesh=mesh,
        in_specs=(P("tm", "sta", None), P("tm", "sta", None), P(None, "sta"), P("sta")),
        out_specs=P(("tm", "sta"), None),
        check_vma=False,
    )
```

profile of v0, /device:TPU:0, one launch (start us, length us, event | category | flops | bytes accessed | tf_op | source)
XLA Modules:
  0.0 134.3 jit_solution(16364569250833107021)
XLA Ops:
  6.5 0.0 copy-start
  6.5 0.0 all-gather.3.cloned.1.call-start
  6.5 0.7 all-gather.3.cloned.1.call-update
  7.3 0.0 reduce-scatter.2.cloned.1.call-start
  7.3 0.7 compare_select_fusion.2
  8.0 0.0 copy-done
  8.0 1.9 %gather_fusion = s32[256]{0:T(256)S(1)} fusion(s32[512]{0:T(512)S(1)} %copy-done, s32[1024]{0:T(1024)S(1)} %pad_clamp_fusion.2), kind=kCustom, calls=%fused_computation | custom fusion | bytes 3072 | tf_op jit(solution)/shard_map/gather | solution.py:37
  10.0 0.8 fusion.16
  10.7 1.9 %gather_fusion.1 = s32[256]{0:T(256)S(1)} fusion(s32[512]{0:T(512)S(1)} %bitcast.12, s32[1024]{0:T(1024)S(1)} %pad_clamp_fusion.2), kind=kCustom, calls=%fused_computation.1 | custom fusion | bytes 3072 | tf_op jit(solution)/shard_map/gather | solution.py:35
  12.7 1.9 %gather_fusion.3 = s32[256]{0:T(256)S(1)} fusion(s32[512]{0:T(512)S(1)} %bitcast.11, s32[1024]{0:T(1024)S(1)} %pad_clamp_fusion.2), kind=kCustom, calls=%fused_computation.3 | custom fusion | bytes 3072 | tf_op jit(solution)/shard_map/gather | solution.py:36
  14.7 18.2 %cosine_multiply_fusion = (f32[1024,1024]{1,0:T(8,128)}, f32[1024,1024]{1,0:T(8,128)}) fusion(s32[1024]{0:T(1024)S(1)} %iota_add_fusion), kind=kLoop, calls=%fused_computation.16 | loop fusion | flops 17825792 | bytes 8392704 | tf_op jit(solution)/shard_map/mul | solution.py:14
  32.9 28.7 %all-gather.3.cloned.1.call-done = bf16[1,512,2048]{2,1,0:T(8,128)(2,1)} async-done(((bf16[1,64,2048]{2,1,0:T(8,128)(2,1)}), bf16[1,512,2048]{2,1,0:T(8,128)(2,1)}) %all-gather.3.cloned.1.call-update) | async-done | bytes 2097168 | tf_op jit(solution)/shard_map/all_gather | solution.py:39
  61.5 0.0 copy-start.1
  61.5 4.4 %gather_fusion.2 = bf16[256,2048]{1,0:T(8,128)(2,1)S(1)} fusion(bf16[512,2048]{1,0:T(8,128)(2,1)} %bitcast.13, s32[1024]{0:T(1024)S(1)} %pad_clamp_fusion.1), kind=kCustom, calls=%fused_computation.2 | custom fusion | bytes 2098176 | tf_op jit(solution)/shard_map/gather | solution.py:40
  65.9 0.0 copy-done.1
  65.9 2.3 %gather_fusion.4 = bf16[256,2048]{1,0:T(8,128)(2,1)} fusion(bf16[512,2048]{1,0:T(8,128)(2,1)S(1)} %bitcast.14, s32[1024]{0:T(1024)S(1)} %pad_clamp_fusion), kind=kCustom, calls=%fused_computation.4 | custom fusion | bytes 2098176 | tf_op jit(solution)/shard_map/gather | solution.py:41
  68.2 1.4 %convert_element_type.13 = f32[256,2048]{1,0:T(8,128)S(1)} convert(bf16[256,2048]{1,0:T(8,128)(2,1)} %gather_fusion.4) | non-fusion elementwise | flops 524288 | bytes 3145728 | tf_op jit(solution)/shard_map/convert_element_type | solution.py:19
  69.7 0.0 copy-start.2
  69.7 0.0 copy-start.3
  69.7 0.2 convert_element_type.12
  70.0 0.6 multiply_add_fusion
  70.6 1.3 copy-done.2
  71.9 1.3 copy-done.3
  73.2 7.3 %fusion = f32[256,1024]{1,0:T(8,128)S(1)} fusion(f32[1024,1024]{1,0:T(8,128)S(1)} %copy-done.3, f32[1024,1024]{1,0:T(8,128)S(1)} %copy-done.2, f32[256,1024]{1,0:T(8,128)S(1)} %get-tuple-element.6, f32[256,1024]{1,0:T(8,128)S(1)} %get-tuple-element.5), kind=kOutput, calls=%fused_computation.5 | convolution fusion | flops 6445072384 | bytes 11534336 | tf_op jit(solution)/shard_map/dot_general | solution.py:43
  80.5 3.8 %fusion.13 = f32[1024,1024]{1,0:T(8,128)} fusion(f32[256,1024]{1,0:T(8,128)S(1)} %fusion, s32[256]{0:T(256)S(1)} %gather_fusion), kind=kOutput, calls=%fused_computation.26 | convolution fusion | flops 3221487616 | bytes 5243904 | tf_op jit(solution)/shard_map/dot_general | solution.py:49
  84.3 0.0 reduce-scatter.2.cloned.1.call-update
  84.3 43.1 %reduce-scatter.2.cloned.1.call-done = f32[256,1024]{1,0:T(8,128)} async-done(((f32[1024,1024]{1,0:T(8,128)}), f32[256,1024]{1,0:T(8,128)}) %reduce-scatter.2.cloned.1.call-update) | async-done | bytes 1048592 | tf_op jit(solution)/shard_map/reduce_scatter | solution.py:48
  (6 shorter events, 0.0 us)
Async XLA Ops:
  6.5 1.5 %copy-start = (s32[512]{0:T(512)S(1)}, s32[512]{0:T(512)}, u32[]{:S(2)}) copy-start(s32[512]{0:T(512)} %param.7) | copy-start | bytes 6148
  6.5 55.0 %all-gather.3.cloned.1.call-start = ((), (), s32[]{:S(2)}) async-start(), calls=%async_computation.2 | async-start | bytes 2359296 | tf_op jit(solution)/shard_map/all_gather | solution.py:39
  7.3 120.2 %reduce-scatter.2.cloned.1.call-start = ((), (), s32[]{:S(2)}) async-start(), calls=%async_computation.1 | async-start | bytes 5242880 | tf_op jit(solution)/shard_map/reduce_scatter | solution.py:48
  61.5 4.4 %copy-start.1 = (bf16[1,512,2048]{2,1,0:T(8,128)(2,1)S(1)}, bf16[1,512,2048]{2,1,0:T(8,128)(2,1)}, u32[]{:S(2)}) copy-start(bf16[1,512,2048]{2,1,0:T(8,128)(2,1)} %all-gather.3.cloned.1.call-done) | copy-start | bytes 6291460
  69.7 2.2 %copy-start.2 = (f32[1024,1024]{1,0:T(8,128)S(1)}, f32[1024,1024]{1,0:T(8,128)}, u32[]{:S(2)}) copy-start(f32[1024,1024]{1,0:T(8,128)} %get-tuple-element.9) | copy-start | bytes 12582916
  69.7 3.5 %copy-start.3 = (f32[1024,1024]{1,0:T(8,128)S(1)}, f32[1024,1024]{1,0:T(8,128)}, u32[]{:S(2)}) copy-start(f32[1024,1024]{1,0:T(8,128)} %get-tuple-element.10) | copy-start | bytes 12582916
Sparse Core Ops, SparseCore 0:
  9.5 51.9 all-gather.2
  84.5 42.9 reduce-scatter.1
where the time goes:
time: 135 us; the launch traced here: 134 us
  waiting for transfers between devices  72.5 us (54%)
  other arithmetic  21.2 us (16%)
  local copies, waits for them, and re-layouts  15.9 us (12%)
  between operations  13.5 us (10%)
  matrix products  11.1 us (8%)
    reduce_scatter x1, waiting for transfers between devices, local(): lax.psum_scatter(jnp.dot(select, partial_lags, precision=lax.Precision.HI...  43.1 us
    all_gather x1, waiting for transfers between devices, local(): all_spectra = lax.all_gather(local_spectra, 'sta', axis=0, tiled=True)  28.7 us
    mul x1, other arithmetic, lag_table(): jnp.cos(phase) * scale  18.2 us
    dot_general x1, matrix products, local(): jnp.dot(cross, table, precision=lax.Precision.HIGHEST, preferred_element_...  7.31 us
    gather x1, local copies, waits for them, and re-layouts, local(): first = all_spectra[first_station]  4.38 us
    dot_general x1, matrix products, local(): jnp.dot(select, partial_lags, precision=lax.Precision.HIGHEST, preferred_...  3.83 us
  transfers between devices with their start and end apart: 2, of which 2 were waited for; matrix products, arithmetic and copies ran while one was open for 19% of the time, Pallas kernels for 0%

commit v1 on v0

--- a/solution.py
+++ b/solution.py
@@ -1,9 +1,18 @@
+import functools
+
 import jax
 import jax.numpy as jnp
+import numpy as np
 from jax import lax
+from jax.experimental import pallas as pl
+from jax.experimental.pallas import tpu as pltpu
 from jax.sharding import PartitionSpec as P
 
 LAGS = 1024
+AXES = ("tm", "sta")
+ROWS, CORES, LAYERS, COLUMNS = 2, 2, 4, 2
+BLOCK = 128
+FIRST_BINS = 512
 
 
 def lag_table(bins, lags):
@@ -24,7 +33,7 @@
     return jnp.concatenate([real_c, imag_c], axis=-1)
 
 
-def local(spectra, pair_list, pair_stations, owner_code):
+def local_any_size(spectra, pair_list, pair_stations, owner_code):
     local_spectra = spectra[0]
     width = local_spectra.shape[1]
     bins = width // 2
@@ -58,9 +67,207 @@
     )
 
 
+def moves(target):
+    def place(row, core, layer, column):
+        return (row * CORES + core) * LAYERS * COLUMNS + layer * COLUMNS + column
+
+    return [
+        (place(row, core, layer, column), place(*target(row, core, layer, column)))
+        for row in range(ROWS)
+        for core in range(CORES)
+        for layer in range(LAYERS)
+        for column in range(COLUMNS)
+    ]
+
+
+OTHER_ROW = moves(lambda r, c, z, x: (1 - r, c, z, x))
+OTHER_CORE = moves(lambda r, c, z, x: (r, 1 - c, z, x))
+FIRST_SIDE = moves(lambda r, c, z, x: (r, c, z, 1 - x) if c == 0 else (1 - r, c, z, x))
+SECOND_SIDE = moves(lambda r, c, z, x: (1 - r, c, z, x) if c == 0 else (r, c, z, 1 - x))
+
+
+def layer_turn(step):
+    return moves(lambda r, c, z, x: (r, c, (z + step) % LAYERS, x))
+
+
+def send(value, pairs):
+    return lax.ppermute(value, AXES, pairs)
+
+
+def split_table(bins, start, stop):
+    index = np.arange(bins)[:, None] * (np.arange(LAGS)[None, :] - LAGS // 2) % (2 * bins)
+    angle = index * (np.pi / bins)
+    both = np.stack([np.cos(angle), -np.sin(angle)]) / np.sqrt(bins)
+    rows = both[:, start:stop].reshape(2, -1, BLOCK, LAGS).transpose(1, 0, 2, 3).reshape(-1, LAGS)
+    rows = rows.astype(np.float32)
+    high = rows.astype(jnp.bfloat16)
+    low = (rows - high.astype(np.float32)).astype(jnp.bfloat16)
+    return jnp.asarray(high), jnp.asarray(low)
+
+
+def chunk_kernel(final, core_ref, picks_ref, *refs):
+    tops, rests, refs = refs[:8], refs[8:12], refs[12:]
+    high_ref, low_ref, refs = refs[0], refs[1], refs[2:]
+    if final:
+        earlier_ref, select_ref, theirs_ref, ours_ref, high_cross, low_cross, total_ref = refs
+    else:
+        total_ref, high_cross, low_cross = refs
+    step = pl.program_id(0)
+    entries = picks_ref.shape[1] // 2
+
+    def block(side):
+        top = jnp.concatenate([tops[2 * side][...], tops[2 * side + 1][...]], axis=1)
+        return jnp.concatenate([top, rests[side][...]], axis=0)
+
+    def cross(order):
+        for segment in range(2):
+            same, other = order[2 * segment], order[2 * segment + 1]
+            stations = jnp.concatenate([block(same), block(other)], axis=0)
+            both = jnp.dot(picks_ref[segment], stations, preferred_element_type=jnp.float32)
+            real_a, imag_a = both[:entries, :BLOCK], both[:entries, BLOCK:]
+            real_b, imag_b = both[entries:, :BLOCK], both[entries:, BLOCK:]
+            value = jnp.concatenate(
+                [real_a * real_b + imag_a * imag_b, real_a * imag_b - imag_a * real_b], axis=1
+            )
+            high = value.astype(jnp.bfloat16)
+            rows = pl.ds(segment * entries, entries)
+            high_cross[rows, :] = high
+            low_cross[rows, :] = (value - high.astype(jnp.float32)).astype(jnp.bfloat16)
+
+    @pl.when(core_ref[0] == 0)
+    def _():
+        cross((0, 1, 2, 3))
+
+    @pl.when(core_ref[0] == 1)
+    def _():
+        cross((0, 2, 1, 3))
+
+    lags = jnp.dot(high_cross[...], high_ref[...], preferred_element_type=jnp.float32)
+    lags += jnp.dot(low_cross[...], high_ref[...], preferred_element_type=jnp.float32)
+    lags += jnp.dot(high_cross[...], low_ref[...], preferred_element_type=jnp.float32)
+
+    @pl.when(step == 0)
+    def _():
+        total_ref[...] = (earlier_ref[...] + lags) if final else lags
+
+    @pl.when(step > 0)
+    def _():
+        total_ref[...] += lags
+
+    if final:
+
+        @pl.when(step == pl.num_programs(0) - 1)
+        def _():
+            total = total_ref[...]
+            high = total.astype(jnp.bfloat16)
+            low = (total - high.astype(jnp.float32)).astype(jnp.bfloat16)
+            for part, out_ref in enumerate((theirs_ref, ours_ref)):
+                out_ref[...] = jnp.dot(
+                    select_ref[part], high, preferred_element_type=jnp.float32
+                ) + jnp.dot(select_ref[part], low, preferred_element_type=jnp.float32)
+
+
+def correlate_chunk(core, picks, own, tops, rests, start, stop, bins, earlier=None, select=None):
+    final = earlier is not None
+    steps = (stop - start) // BLOCK
+    first_block = start // BLOCK
+    stations = own.shape[0]
+    entries = picks.shape[1]
+    high, low = split_table(bins, start, stop)
+    whole = lambda shape: pl.BlockSpec(shape, lambda j, c: (0,) * len(shape))
+    real = pl.BlockSpec((stations, BLOCK), lambda j, c: (0, first_block + j))
+    imag = pl.BlockSpec((stations, BLOCK), lambda j, c: (0, bins // BLOCK + first_block + j))
+    rest = pl.BlockSpec((rests[0].shape[0], 2 * BLOCK), lambda j, c: (0, j))
+    table = pl.BlockSpec((2 * BLOCK, LAGS), lambda j, c: (j, 0))
+    operands = [picks, *(t for t in tops for _ in range(2)), *rests, high, low]
+    in_specs = [whole(picks.shape), *([real, imag] * 4), *([rest] * 4), table, table]
+    scratch = [
+        pltpu.VMEM((entries, 2 * BLOCK), jnp.bfloat16),
+        pltpu.VMEM((entries, 2 * BLOCK), jnp.bfloat16),
+    ]
+    out_shape = [jax.ShapeDtypeStruct((entries, LAGS), jnp.float32)]
+    if final:
+        operands += [earlier, select]
+        in_specs += [whole(earlier.shape), whole(select.shape)]
+        out_shape = [jax.ShapeDtypeStruct((select.shape[1], LAGS), jnp.float32)] * 2
+        scratch.append(pltpu.VMEM((entries, LAGS), jnp.float32))
+    result = pl.pallas_call(
+        functools.partial(chunk_kernel, final),
+        out_shape=out_shape,
+        grid_spec=pltpu.PrefetchScalarGridSpec(
+            num_scalar_prefetch=1,
+            grid=(steps,),
+            in_specs=in_specs,
+            out_specs=[whole(o.shape) for o in out_shape],
+            scratch_shapes=scratch,
+        ),
+        compiler_params=pltpu.CompilerParams(vmem_limit_bytes=40 * 1024 * 1024),
+        cost_estimate=pl.CostEstimate(
+            flops=2 * entries * (stop - start) * 2 * (3 * LAGS + entries),
+            bytes_accessed=(stop - start) * 2 * (4 * LAGS + 16 * stations * 2),
+            transcendentals=0,
+        ),
+        name="correlate_last" if final else "correlate",
+    )(core, *operands)
+    return result
+
+
+def local_grid(spectra, pair_list, pair_stations, owner_code):
+    own = spectra[0]
+    stations, width = own.shape
+    bins = width // 2
+    catalogue = pair_stations.shape[1]
+    capacity = 2 * catalogue // (ROWS * CORES)
+    row, core = lax.axis_index("tm") // CORES, lax.axis_index("tm") % CORES
+    layer, column = lax.axis_index("sta") // COLUMNS, lax.axis_index("sta") % COLUMNS
+
+    listed_here = pair_list[0, 0]
+    first_own = send(own, FIRST_SIDE)
+    second_own = send(own, SECOND_SIDE)
+    listed_there = send(listed_here, OTHER_ROW)
+    cuts = [(0, FIRST_BINS), (FIRST_BINS, bins)]
+    turned = []
+    for start, stop in cuts:
+        blocks = own.reshape(stations, 2, bins // BLOCK, BLOCK)[:, :, start // BLOCK : stop // BLOCK]
+        part = blocks.transpose(0, 2, 1, 3).reshape(stations, 2 * (stop - start))
+        turned.append(
+            jnp.concatenate([send(part, layer_turn(step)) for step in range(1, LAYERS)], axis=0)
+        )
+    diagonal_own = send(first_own, SECOND_SIDE)
+    tops = (own, first_own, second_own, diagonal_own)
+    rests = []
+    for part in turned:
+        first, second = send(part, FIRST_SIDE), send(part, SECOND_SIDE)
+        rests.append((part, first, second, send(first, SECOND_SIDE)))
+
+    listed = jnp.stack([listed_here, listed_there])
+    hit = listed[:, :, None] == jnp.arange(catalogue, dtype=jnp.int32)
+    look_up = lambda values: jnp.sum(jnp.where(hit, values, 0), axis=-1)
+    pair = jnp.concatenate([look_up(pair_stations[0]), look_up(pair_stations[1])], axis=1)
+    holder, place = pair // stations, pair % stations
+    turn = (layer - holder // COLUMNS) % LAYERS
+    beside = (holder % COLUMNS) ^ column
+    position = (beside * LAYERS + turn) * stations + place
+    spots = jnp.arange(COLUMNS * LAYERS * stations, dtype=jnp.int32)
+    picks = (position[:, :, None] == spots).astype(jnp.bfloat16)
+    codes = look_up(owner_code).reshape(-1)
+    owner = row * CORES + jnp.stack([1 - core, core])
+    slots = owner[:, None] * capacity + jnp.arange(capacity, dtype=jnp.int32)
+    select = (slots[:, :, None] == codes).astype(jnp.bfloat16)
+
+    core = core.astype(jnp.int32).reshape(1)
+    (early,) = correlate_chunk(core, picks, own, tops, rests[0], *cuts[0], bins)
+    theirs, ours = correlate_chunk(
+        core, picks, own, tops, rests[1], *cuts[1], bins, earlier=early, select=select
+    )
+    return ours + send(theirs, OTHER_CORE)
+
+
 def solution(mesh):
+    sizes = (mesh.shape["tm"], mesh.shape["sta"])
+    fits = sizes == (ROWS * CORES, LAYERS * COLUMNS)
     return jax.shard_map(
-        local,
+        local_grid if fits else local_any_size,
         mesh=mesh,
         in_specs=(P("tm", "sta", None), P("tm", "sta", None), P(None, "sta"), P("sta")),
         out_specs=P(("tm", "sta"), None),

time: 135 us -> 80.6 us (0.60)
  waiting for transfers between devices: 72.5 us -> 33.1 us
  starting transfers between devices: 0.04 us -> 25.1 us
  other arithmetic: 21.2 us -> 2.4 us
  Pallas kernels: 0 us -> 16.1 us
  between operations: 13.5 us -> 0.26 us
  local copies, waits for them, and re-layouts: 15.9 us -> 3.34 us
  matrix products: 11.1 us -> 0 us
    reduce_scatter x1 -> x0, waiting for transfers between devices: 43.1 us -> none  [local(): lax.psum_scatter(jnp.dot(select, partial_lags, precision=lax.Precision.HI...]
    ppermute x0 -> x17, waiting for transfers between devices: none -> 33.1 us  [send(): return lax.ppermute(value, AXES, pairs)]
    all_gather x1 -> x0, waiting for transfers between devices: 28.7 us -> none  [local(): all_spectra = lax.all_gather(local_spectra, 'sta', axis=0, tiled=True)]
    ppermute x0 -> x17, starting transfers between devices: none -> 25.1 us  [send(): return lax.ppermute(value, AXES, pairs)]
    mul x1, other arithmetic: 18.2 us -> 0.08 us  [local_grid(): slots = owner[:, None] * capacity + jnp.arange(capacity, dtype=jnp.int32)]
    pallas_call x0 -> x2, Pallas kernels: none -> 16.1 us  [correlate_chunk(): pl.pallas_call(functools.partial(chunk_kernel, final), out_shape=out_shap...]
    gather x5 -> x0, local copies, waits for them, and re-layouts: 12.5 us -> none  [the longest x1 4.38 us: local(): first = all_spectra[first_station]]
    dot_general x2 -> x0, matrix products: 11.1 us -> none  [the longest x1 7.31 us: local(): jnp.dot(cross, table, precision=lax.Precision.HIGHEST, preferred_element_...]
  transfers between devices with their start and end apart: 2 -> 17, of which waited for: 2 -> 7; matrix products, arithmetic and copies ran while one was open for 19% -> 2% of each run, Pallas kernels for 0% -> 9%
where the time goes in v1:
time: 80.6 us; the launch traced here: 80.3 us
  waiting for transfers between devices  33.1 us (41%)
  starting transfers between devices  25.1 us (31%)
  Pallas kernels  16.1 us (20%)
  local copies, waits for them, and re-layouts  3.34 us (4%)
  other arithmetic  2.4 us (3%)
    ppermute x17, waiting for transfers between devices, send(): return lax.ppermute(value, AXES, pairs)  33.1 us
    ppermute x17, starting transfers between devices, send(): return lax.ppermute(value, AXES, pairs)  25.1 us
    pallas_call x2, Pallas kernels, correlate_chunk(): pl.pallas_call(functools.partial(chunk_kernel, final), out_shape=out_shap...  16.1 us
    unnamed x24, local copies, waits for them, and re-layouts  3.08 us
  transfers between devices with their start and end apart: 17, of which 7 were waited for; matrix products, arithmetic and copies ran while one was open for 2% of the time, Pallas kernels for 9%

profile of v1, /device:TPU:0, one launch (start us, length us, event | category | flops | bytes accessed | tf_op | source)
XLA Modules:
  0.0 80.3 jit_solution(1186846762320099609)
XLA Ops:
  0.0 1.1 %copy.15 = bf16[8,8,16,128]{3,2,1,0:T(8,128)(2,1)S(1)} copy(bf16[8,8,16,128]{3,1,2,0:T(8,128)(2,1)} %bitcast.20) | data formatting | bytes 524288
  1.1 0.1 fusion.6
  1.2 0.1 copy.20
  1.3 0.0 copy-start.3
  1.3 0.1 reshape.206
  1.4 5.1 %collective-permute-start.6 = (bf16[64,1024]{1,0:T(8,128)(2,1)S(1)}, bf16[64,1024]{1,0:T(8,128)(2,1)S(1)}, u32[]{:S(2)}, u32[]{:S(2)}) collective-permute-start(bf16[64,1024]{1,0:T(8,128)(2,1)S(1)} %reshape.206), channel_id=1, source_target_pairs={{0,6},{1,7},{2,0},{3,1},{4,2},{5,3},{6,4},{7,5},{8,14},{9,15},{10,... | collective-permute-start | bytes 393224 | tf_op jit(solution)/shard_map/ppermute | solution.py:94
  6.5 0.0 collective-permute-start.5
  6.5 1.0 %collective-permute-start.4 = (bf16[64,1024]{1,0:T(8,128)(2,1)S(1)}, bf16[64,1024]{1,0:T(8,128)(2,1)S(1)}, u32[]{:S(2)}, u32[]{:S(2)}) collective-permute-start(bf16[64,1024]{1,0:T(8,128)(2,1)S(1)} %reshape.206), channel_id=1, source_target_pairs={{0,2},{1,3},{2,4},{3,5},{4,6},{5,7},{6,0},{7,1},{8,10},{9,11},{10,... | collective-permute-start | bytes 393224 | tf_op jit(solution)/shard_map/ppermute | solution.py:94
  7.5 1.5 %collective-permute-start = (s32[256]{0:T(256)}, s32[256]{0:T(256)S(1)}, u32[]{:S(2)}, u32[]{:S(2)}) collective-permute-start(s32[256]{0:T(256)} %bitcast.34), channel_id=1, source_target_pairs={{0,16},{1,17},{2,18},{3,19},{4,20},{5,21},{6,22},{7,23},{8,24},{9,... | collective-permute-start | bytes 3080 | tf_op jit(solution)/shard_map/ppermute | solution.py:94
  9.0 0.1 copy.19
  9.1 0.1 reshape.207
  9.2 2.5 %collective-permute-start.10 = (bf16[64,1024]{1,0:T(8,128)(2,1)S(1)}, bf16[64,1024]{1,0:T(8,128)(2,1)S(1)}, u32[]{:S(2)}, u32[]{:S(2)}) collective-permute-start(bf16[64,1024]{1,0:T(8,128)(2,1)S(1)} %reshape.207), channel_id=1, source_target_pairs={{0,2},{1,3},{2,4},{3,5},{4,6},{5,7},{6,0},{7,1},{8,10},{9,11},{10,... | collective-permute-start | bytes 393224 | tf_op jit(solution)/shard_map/ppermute | solution.py:94
  11.7 0.1 fusion.5
  11.8 0.1 iota_add_fusion
  11.9 0.0 collective-permute-done
  11.9 1.3 %collective-permute-start.11 = (bf16[64,1024]{1,0:T(8,128)(2,1)S(1)}, bf16[64,1024]{1,0:T(8,128)(2,1)S(1)}, u32[]{:S(2)}, u32[]{:S(2)}) collective-permute-start(bf16[64,1024]{1,0:T(8,128)(2,1)S(1)} %reshape.207), channel_id=1, source_target_pairs={{0,4},{1,5},{2,6},{3,7},{4,0},{5,1},{6,2},{7,3},{8,12},{9,13},{10,... | collective-permute-start | bytes 393224 | tf_op jit(solution)/shard_map/ppermute | solution.py:94
  13.2 6.6 %collective-permute-done.10 = bf16[64,1024]{1,0:T(8,128)(2,1)S(1)} collective-permute-done((bf16[64,1024]{1,0:T(8,128)(2,1)S(1)}, bf16[64,1024]{1,0:T(8,128)(2,1)S(1)}, u32[]{:S(2)}, u32[]{:S(2)}) %collective-permute-start.10) | collective-permute-done | bytes 131104 | tf_op jit(solution)/shard_map/ppermute | solution.py:94
  19.8 1.4 %collective-permute-start.12 = (bf16[64,1024]{1,0:T(8,128)(2,1)S(1)}, bf16[64,1024]{1,0:T(8,128)(2,1)S(1)}, u32[]{:S(2)}, u32[]{:S(2)}) collective-permute-start(bf16[64,1024]{1,0:T(8,128)(2,1)S(1)} %reshape.207), channel_id=1, source_target_pairs={{0,6},{1,7},{2,0},{3,1},{4,2},{5,3},{6,4},{7,5},{8,14},{9,15},{10,... | collective-permute-start | bytes 393224 | tf_op jit(solution)/shard_map/ppermute | solution.py:94
  21.2 5.0 %collective-permute-done.11 = bf16[64,1024]{1,0:T(8,128)(2,1)S(1)} collective-permute-done((bf16[64,1024]{1,0:T(8,128)(2,1)S(1)}, bf16[64,1024]{1,0:T(8,128)(2,1)S(1)}, u32[]{:S(2)}, u32[]{:S(2)}) %collective-permute-start.11) | collective-permute-done | bytes 131104 | tf_op jit(solution)/shard_map/ppermute | solution.py:94
  26.2 1.5 %collective-permute-start.2 = (bf16[64,2048]{1,0:T(8,128)(2,1)S(1)}, bf16[64,2048]{1,0:T(8,128)(2,1)S(1)}, u32[]{:S(2)}, u32[]{:S(2)}) collective-permute-start(bf16[64,2048]{1,0:T(8,128)(2,1)S(1)} %bitcast.21), channel_id=1, source_target_pairs={{0,16},{1,17},{2,18},{3,19},{4,20},{5,21},{6,22},{7,23},{8,9},{9,8... | collective-permute-start | bytes 786440 | tf_op jit(solution)/shard_map/ppermute | solution.py:94
  27.7 2.9 %collective-permute-done.12 = bf16[64,1024]{1,0:T(8,128)(2,1)S(1)} collective-permute-done((bf16[64,1024]{1,0:T(8,128)(2,1)S(1)}, bf16[64,1024]{1,0:T(8,128)(2,1)S(1)}, u32[]{:S(2)}, u32[]{:S(2)}) %collective-permute-start.12) | collective-permute-done | bytes 131104 | tf_op jit(solution)/shard_map/ppermute | solution.py:94
  30.6 1.5 %collective-permute-start.1 = (bf16[64,2048]{1,0:T(8,128)(2,1)S(1)}, bf16[64,2048]{1,0:T(8,128)(2,1)S(1)}, u32[]{:S(2)}, u32[]{:S(2)}) collective-permute-start(bf16[64,2048]{1,0:T(8,128)(2,1)S(1)} %bitcast.22), channel_id=1, source_target_pairs={{0,1},{1,0},{2,3},{3,2},{4,5},{5,4},{6,7},{7,6},{8,24},{9,25},{10,... | collective-permute-start | bytes 786440 | tf_op jit(solution)/shard_map/ppermute | solution.py:94
  32.1 0.0 collective-permute-done.4
  32.2 0.6 collective-permute-start.13
  32.8 0.0 collective-permute-done.5
  32.8 0.0 collective-permute-done.6
  32.8 1.6 %collective-permute-start.7 = (bf16[192,1024]{1,0:T(8,128)(2,1)S(1)}, bf16[192,1024]{1,0:T(8,128)(2,1)S(1)}, u32[]{:S(2)}, u32[]{:S(2)}) collective-permute-start(bf16[192,1024]{1,0:T(8,128)(2,1)S(1)} %constant_dynamic-update-slice_fusion.refs_8_), channel_id=1, source_target_pairs={{0,1},{1,0},{2,3},{3,2},{4,5},{5,4},{6,7},{7,6},{8,24},{9,25},{10,... | collective-permute-start | bytes 1179656 | tf_op jit(solution)/shard_map/ppermute | solution.py:94
  34.4 0.7 select_reduce_fusion
  35.1 0.1 fusion.3
  35.1 1.6 %collective-permute-start.14 = (bf16[192,1024]{1,0:T(8,128)(2,1)S(1)}, bf16[192,1024]{1,0:T(8,128)(2,1)S(1)}, u32[]{:S(2)}, u32[]{:S(2)}) collective-permute-start(bf16[192,1024]{1,0:T(8,128)(2,1)S(1)} %constant_dynamic-update-slice_fusion.3.refs_8_), channel_id=1, source_target_pairs={{0,16},{1,17},{2,18},{3,19},{4,20},{5,21},{6,22},{7,23},{8,9},{9,8... | collective-permute-start | bytes 1179656 | tf_op jit(solution)/shard_map/ppermute | solution.py:94
  36.7 3.0 %collective-permute-done.1.refs_2_.refs_3_ = bf16[64,2048]{1,0:T(8,128)(2,1)S(1)} collective-permute-done((bf16[64,2048]{1,0:T(8,128)(2,1)S(1)}, bf16[64,2048]{1,0:T(8,128)(2,1)S(1)}, u32[]{:S(2)}, u32[]{:S(2)}) %collective-permute-start.1) | collective-permute-done | bytes 262176 | tf_op jit(solution)/shard_map/ppermute | solution.py:94
  39.8 1.7 %collective-permute-start.3 = (bf16[64,2048]{1,0:T(8,128)(2,1)S(1)}, bf16[64,2048]{1,0:T(8,128)(2,1)S(1)}, u32[]{:S(2)}, u32[]{:S(2)}) collective-permute-start(bf16[64,2048]{1,0:T(8,128)(2,1)S(1)} %collective-permute-done.1.refs_2_.refs_3_), channel_id=1, source_target_pairs={{0,16},{1,17},{2,18},{3,19},{4,20},{5,21},{6,22},{7,23},{8,9},{9,8... | collective-permute-start | bytes 786440 | tf_op jit(solution)/shard_map/ppermute | solution.py:94
  41.4 6.8 %collective-permute-done.13.refs_9_ = bf16[192,1024]{1,0:T(8,128)(2,1)S(1)} collective-permute-done((bf16[192,1024]{1,0:T(8,128)(2,1)S(1)}, bf16[192,1024]{1,0:T(8,128)(2,1)S(1)}, u32[]{:S(2)}, u32[]{:S(2)}) %collective-permute-start.13) | collective-permute-done | bytes 393248 | tf_op jit(solution)/shard_map/ppermute | solution.py:94
  48.2 1.7 %collective-permute-start.15 = (bf16[192,1024]{1,0:T(8,128)(2,1)S(1)}, bf16[192,1024]{1,0:T(8,128)(2,1)S(1)}, u32[]{:S(2)}, u32[]{:S(2)}) collective-permute-start(bf16[192,1024]{1,0:T(8,128)(2,1)S(1)} %collective-permute-done.13.refs_9_), channel_id=1, source_target_pairs={{0,16},{1,17},{2,18},{3,19},{4,20},{5,21},{6,22},{7,23},{8,9},{9,8... | collective-permute-start | bytes 1179656 | tf_op jit(solution)/shard_map/ppermute | solution.py:94
  49.8 0.2 fusion.picks_ref
  50.1 0.4 collective-permute-start.8
  50.5 6.1 %collective-permute-done.7.refs_9_ = bf16[192,1024]{1,0:T(8,128)(2,1)S(1)} collective-permute-done((bf16[192,1024]{1,0:T(8,128)(2,1)S(1)}, bf16[192,1024]{1,0:T(8,128)(2,1)S(1)}, u32[]{:S(2)}, u32[]{:S(2)}) %collective-permute-start.7) | collective-permute-done | bytes 393248 | tf_op jit(solution)/shard_map/ppermute | solution.py:94
  56.6 1.7 %collective-permute-start.9 = (bf16[192,1024]{1,0:T(8,128)(2,1)S(1)}, bf16[192,1024]{1,0:T(8,128)(2,1)S(1)}, u32[]{:S(2)}, u32[]{:S(2)}) collective-permute-start(bf16[192,1024]{1,0:T(8,128)(2,1)S(1)} %collective-permute-done.7.refs_9_), channel_id=1, source_target_pairs={{0,16},{1,17},{2,18},{3,19},{4,20},{5,21},{6,22},{7,23},{8,9},{9,8... | collective-permute-start | bytes 1179656 | tf_op jit(solution)/shard_map/ppermute | solution.py:94
  58.3 0.1 compare_convert_fusion.refs_15_
  58.4 0.0 copy-start.1
  58.4 0.0 copy-start.2
  58.5 0.0 copy-start.4
  58.5 1.7 %copy-done.4 = bf16[1024,1024]{1,0:T(8,128)(2,1)S(1)} copy-done((bf16[1024,1024]{1,0:T(8,128)(2,1)S(1)}, bf16[1024,1024]{1,0:T(8,128)(2,1)}, u32[]{:S(2)}) %copy-start.4) | copy-done | bytes 2097176
  60.2 7.3 %correlate.1.refs_14_ = f32[512,1024]{1,0:T(8,128)S(1)} custom-call(s32[1]{0:T(128)} %bitcast.core_ref, bf16[2,512,512]{2,1,0:T(8,128)(2,1)S(1)} %fusion.picks_ref, bf16[64,2048]{1,0:T(8,128)(2,1)S(1)} %bitcast.23, bf16[64,2048]{1,0:T(8,128)(2,1)S(1)} %bitcast.24, bf16[64,2048]{1,0:T(8,128)(2,1)S(1)} %collective-permute-done.1.refs_2_.refs_3_, ...), custom_call_target="tpu_custom_call" | custom-call | flops 3758096384 | bytes 6291456 | tf_op jit(solution)/shard_map/correlate/pallas_call | solution.py:194
  67.6 8.8 %correlate_last.1 = (f32[256,1024]{1,0:T(8,128)S(1)}, f32[256,1024]{1,0:T(8,128)S(1)}) custom-call(s32[1]{0:T(128)} %bitcast.core_ref, bf16[2,512,512]{2,1,0:T(8,128)(2,1)S(1)} %fusion.picks_ref, bf16[64,2048]{1,0:T(8,128)(2,1)S(1)} %bitcast.25, bf16[64,2048]{1,0:T(8,128)(2,1)S(1)} %bitcast.26, bf16[64,2048]{1,0:T(8,128)(2,1)S(1)} %collective-permute-done.1.refs_2_.refs_3_, ...), custom_call_target="tpu_custom_call" | custom-call | flops 3758096384 | bytes 6291456 | tf_op jit(solution)/shard_map/correlate_last/pallas_call | solution.py:194
  76.4 0.1 collective-permute-start.16
  76.5 2.6 %collective-permute-done.16 = f32[256,1024]{1,0:T(8,128)S(1)} collective-permute-done((f32[256,1024]{1,0:T(8,128)S(1)}, f32[256,1024]{1,0:T(8,128)S(1)}, u32[]{:S(2)}, u32[]{:S(2)}) %collective-permute-start.16) | collective-permute-done | bytes 1048608 | tf_op jit(solution)/shard_map/ppermute | solution.py:94
  79.2 1.1 %add.101 = f32[256,1024]{1,0:T(8,128)} add(f32[256,1024]{1,0:T(8,128)S(1)} %get-tuple-element.7, f32[256,1024]{1,0:T(8,128)S(1)} %collective-permute-done.16) | non-fusion elementwise | flops 262144 | bytes 3145728 | tf_op jit(solution)/shard_map/add | solution.py:263
  (26 shorter events, 0.1 us)
Async XLA Ops:
  0.0 26.2 %copy-start = (bf16[1,64,2048]{2,1,0:T(8,128)(2,1)S(1)}, bf16[1,64,2048]{2,1,0:T(8,128)(2,1)}, u32[]{:S(2)}) copy-start(bf16[1,64,2048]{2,1,0:T(8,128)(2,1)} %param.8) | copy-start | bytes 786436
  0.0 13.2 %copy-start.7 = (s32[1,1,256]{2,1,0:T(1,128)S(1)}, s32[1,1,256]{2,1,0:T(1,128)}, u32[]{:S(2)}) copy-start(s32[1,1,256]{2,1,0:T(1,128)} %param.9) | copy-start | bytes 3076
  0.0 11.7 %copy-start.5 = (s32[2,512]{1,0:T(2,128)S(1)}, s32[2,512]{1,0:T(2,128)}, u32[]{:S(2)}) copy-start(s32[2,512]{1,0:T(2,128)} %param.10) | copy-start | bytes 12292
  0.0 34.4 %copy-start.6 = (s32[512]{0:T(512)S(1)}, s32[512]{0:T(512)}, u32[]{:S(2)}) copy-start(s32[512]{0:T(512)} %param.11) | copy-start | bytes 6148
  1.3 57.2 %copy-start.3 = (bf16[1024,1024]{1,0:T(8,128)(2,1)S(1)}, bf16[1024,1024]{1,0:T(8,128)(2,1)}, u32[]{:S(2)}) copy-start(bf16[1024,1024]{1,0:T(8,128)(2,1)} %constant.106.clone.refs_13_) | copy-start | bytes 6291460
  1.4 31.4 %collective-permute-start.6 = (bf16[64,1024]{1,0:T(8,128)(2,1)S(1)}, bf16[64,1024]{1,0:T(8,128)(2,1)S(1)}, u32[]{:S(2)}, u32[]{:S(2)}) collective-permute-start(bf16[64,1024]{1,0:T(8,128)(2,1)S(1)} %reshape.206), channel_id=1, source_target_pairs={{0,6},{1,7},{2,0},{3,1},{4,2},{5,3},{6,4},{7,5},{8,14},{9,15},{10,... | collective-permute-start | bytes 393224 | tf_op jit(solution)/shard_map/ppermute | solution.py:94
  6.5 26.3 %collective-permute-start.5 = (bf16[64,1024]{1,0:T(8,128)(2,1)S(1)}, bf16[64,1024]{1,0:T(8,128)(2,1)S(1)}, u32[]{:S(2)}, u32[]{:S(2)}) collective-permute-start(bf16[64,1024]{1,0:T(8,128)(2,1)S(1)} %reshape.206), channel_id=1, source_target_pairs={{0,4},{1,5},{2,6},{3,7},{4,0},{5,1},{6,2},{7,3},{8,12},{9,13},{10,... | collective-permute-start | bytes 393224 | tf_op jit(solution)/shard_map/ppermute | solution.py:94
  6.5 25.7 %collective-permute-start.4 = (bf16[64,1024]{1,0:T(8,128)(2,1)S(1)}, bf16[64,1024]{1,0:T(8,128)(2,1)S(1)}, u32[]{:S(2)}, u32[]{:S(2)}) collective-permute-start(bf16[64,1024]{1,0:T(8,128)(2,1)S(1)} %reshape.206), channel_id=1, source_target_pairs={{0,2},{1,3},{2,4},{3,5},{4,6},{5,7},{6,0},{7,1},{8,10},{9,11},{10,... | collective-permute-start | bytes 393224 | tf_op jit(solution)/shard_map/ppermute | solution.py:94
  7.5 4.4 %collective-permute-start = (s32[256]{0:T(256)}, s32[256]{0:T(256)S(1)}, u32[]{:S(2)}, u32[]{:S(2)}) collective-permute-start(s32[256]{0:T(256)} %bitcast.34), channel_id=1, source_target_pairs={{0,16},{1,17},{2,18},{3,19},{4,20},{5,21},{6,22},{7,23},{8,24},{9,... | collective-permute-start | bytes 3080 | tf_op jit(solution)/shard_map/ppermute | solution.py:94
  9.2 10.6 %collective-permute-start.10 = (bf16[64,1024]{1,0:T(8,128)(2,1)S(1)}, bf16[64,1024]{1,0:T(8,128)(2,1)S(1)}, u32[]{:S(2)}, u32[]{:S(2)}) collective-permute-start(bf16[64,1024]{1,0:T(8,128)(2,1)S(1)} %reshape.207), channel_id=1, source_target_pairs={{0,2},{1,3},{2,4},{3,5},{4,6},{5,7},{6,0},{7,1},{8,10},{9,11},{10,... | collective-permute-start | bytes 393224 | tf_op jit(solution)/shard_map/ppermute | solution.py:94
  11.9 14.3 %collective-permute-start.11 = (bf16[64,1024]{1,0:T(8,128)(2,1)S(1)}, bf16[64,1024]{1,0:T(8,128)(2,1)S(1)}, u32[]{:S(2)}, u32[]{:S(2)}) collective-permute-start(bf16[64,1024]{1,0:T(8,128)(2,1)S(1)} %reshape.207), channel_id=1, source_target_pairs={{0,4},{1,5},{2,6},{3,7},{4,0},{5,1},{6,2},{7,3},{8,12},{9,13},{10,... | collective-permute-start | bytes 393224 | tf_op jit(solution)/shard_map/ppermute | solution.py:94
  19.8 10.8 %collective-permute-start.12 = (bf16[64,1024]{1,0:T(8,128)(2,1)S(1)}, bf16[64,1024]{1,0:T(8,128)(2,1)S(1)}, u32[]{:S(2)}, u32[]{:S(2)}) collective-permute-start(bf16[64,1024]{1,0:T(8,128)(2,1)S(1)} %reshape.207), channel_id=1, source_target_pairs={{0,6},{1,7},{2,0},{3,1},{4,2},{5,3},{6,4},{7,5},{8,14},{9,15},{10,... | collective-permute-start | bytes 393224 | tf_op jit(solution)/shard_map/ppermute | solution.py:94
  26.2 23.9 %collective-permute-start.2 = (bf16[64,2048]{1,0:T(8,128)(2,1)S(1)}, bf16[64,2048]{1,0:T(8,128)(2,1)S(1)}, u32[]{:S(2)}, u32[]{:S(2)}) collective-permute-start(bf16[64,2048]{1,0:T(8,128)(2,1)S(1)} %bitcast.21), channel_id=1, source_target_pairs={{0,16},{1,17},{2,18},{3,19},{4,20},{5,21},{6,22},{7,23},{8,9},{9,8... | collective-permute-start | bytes 786440 | tf_op jit(solution)/shard_map/ppermute | solution.py:94
  30.6 9.1 %collective-permute-start.1 = (bf16[64,2048]{1,0:T(8,128)(2,1)S(1)}, bf16[64,2048]{1,0:T(8,128)(2,1)S(1)}, u32[]{:S(2)}, u32[]{:S(2)}) collective-permute-start(bf16[64,2048]{1,0:T(8,128)(2,1)S(1)} %bitcast.22), channel_id=1, source_target_pairs={{0,1},{1,0},{2,3},{3,2},{4,5},{5,4},{6,7},{7,6},{8,24},{9,25},{10,... | collective-permute-start | bytes 786440 | tf_op jit(solution)/shard_map/ppermute | solution.py:94
  32.2 16.0 %collective-permute-start.13 = (bf16[192,1024]{1,0:T(8,128)(2,1)S(1)}, bf16[192,1024]{1,0:T(8,128)(2,1)S(1)}, u32[]{:S(2)}, u32[]{:S(2)}) collective-permute-start(bf16[192,1024]{1,0:T(8,128)(2,1)S(1)} %constant_dynamic-update-slice_fusion.3.refs_8_), channel_id=1, source_target_pairs={{0,1},{1,0},{2,3},{3,2},{4,5},{5,4},{6,7},{7,6},{8,24},{9,25},{10,... | collective-permute-start | bytes 1179656 | tf_op jit(solution)/shard_map/ppermute | solution.py:94
  32.8 23.8 %collective-permute-start.7 = (bf16[192,1024]{1,0:T(8,128)(2,1)S(1)}, bf16[192,1024]{1,0:T(8,128)(2,1)S(1)}, u32[]{:S(2)}, u32[]{:S(2)}) collective-permute-start(bf16[192,1024]{1,0:T(8,128)(2,1)S(1)} %constant_dynamic-update-slice_fusion.refs_8_), channel_id=1, source_target_pairs={{0,1},{1,0},{2,3},{3,2},{4,5},{5,4},{6,7},{7,6},{8,24},{9,25},{10,... | collective-permute-start | bytes 1179656 | tf_op jit(solution)/shard_map/ppermute | solution.py:94
  35.1 23.3 %collective-permute-start.14 = (bf16[192,1024]{1,0:T(8,128)(2,1)S(1)}, bf16[192,1024]{1,0:T(8,128)(2,1)S(1)}, u32[]{:S(2)}, u32[]{:S(2)}) collective-permute-start(bf16[192,1024]{1,0:T(8,128)(2,1)S(1)} %constant_dynamic-update-slice_fusion.3.refs_8_), channel_id=1, source_target_pairs={{0,16},{1,17},{2,18},{3,19},{4,20},{5,21},{6,22},{7,23},{8,9},{9,8... | collective-permute-start | bytes 1179656 | tf_op jit(solution)/shard_map/ppermute | solution.py:94
  39.8 18.7 %collective-permute-start.3 = (bf16[64,2048]{1,0:T(8,128)(2,1)S(1)}, bf16[64,2048]{1,0:T(8,128)(2,1)S(1)}, u32[]{:S(2)}, u32[]{:S(2)}) collective-permute-start(bf16[64,2048]{1,0:T(8,128)(2,1)S(1)} %collective-permute-done.1.refs_2_.refs_3_), channel_id=1, source_target_pairs={{0,16},{1,17},{2,18},{3,19},{4,20},{5,21},{6,22},{7,23},{8,9},{9,8... | collective-permute-start | bytes 786440 | tf_op jit(solution)/shard_map/ppermute | solution.py:94
  48.2 10.3 %collective-permute-start.15 = (bf16[192,1024]{1,0:T(8,128)(2,1)S(1)}, bf16[192,1024]{1,0:T(8,128)(2,1)S(1)}, u32[]{:S(2)}, u32[]{:S(2)}) collective-permute-start(bf16[192,1024]{1,0:T(8,128)(2,1)S(1)} %collective-permute-done.13.refs_9_), channel_id=1, source_target_pairs={{0,16},{1,17},{2,18},{3,19},{4,20},{5,21},{6,22},{7,23},{8,9},{9,8... | collective-permute-start | bytes 1179656 | tf_op jit(solution)/shard_map/ppermute | solution.py:94
  50.1 17.5 %collective-permute-start.8 = (bf16[192,1024]{1,0:T(8,128)(2,1)S(1)}, bf16[192,1024]{1,0:T(8,128)(2,1)S(1)}, u32[]{:S(2)}, u32[]{:S(2)}) collective-permute-start(bf16[192,1024]{1,0:T(8,128)(2,1)S(1)} %constant_dynamic-update-slice_fusion.refs_8_), channel_id=1, source_target_pairs={{0,16},{1,17},{2,18},{3,19},{4,20},{5,21},{6,22},{7,23},{8,9},{9,8... | collective-permute-start | bytes 1179656 | tf_op jit(solution)/shard_map/ppermute | solution.py:94
  56.6 11.0 %collective-permute-start.9 = (bf16[192,1024]{1,0:T(8,128)(2,1)S(1)}, bf16[192,1024]{1,0:T(8,128)(2,1)S(1)}, u32[]{:S(2)}, u32[]{:S(2)}) collective-permute-start(bf16[192,1024]{1,0:T(8,128)(2,1)S(1)} %collective-permute-done.7.refs_9_), channel_id=1, source_target_pairs={{0,16},{1,17},{2,18},{3,19},{4,20},{5,21},{6,22},{7,23},{8,9},{9,8... | collective-permute-start | bytes 1179656 | tf_op jit(solution)/shard_map/ppermute | solution.py:94
  58.4 9.2 %copy-start.1 = (bf16[1024,1024]{1,0:T(8,128)(2,1)S(1)}, bf16[1024,1024]{1,0:T(8,128)(2,1)}, u32[]{:S(2)}) copy-start(bf16[1024,1024]{1,0:T(8,128)(2,1)} %constant.108.clone.refs_13_) | copy-start | bytes 6291460
  58.4 9.2 %copy-start.2 = (bf16[1024,1024]{1,0:T(8,128)(2,1)S(1)}, bf16[1024,1024]{1,0:T(8,128)(2,1)}, u32[]{:S(2)}) copy-start(bf16[1024,1024]{1,0:T(8,128)(2,1)} %constant.107.clone.refs_12_) | copy-start | bytes 6291460
  58.5 1.7 %copy-start.4 = (bf16[1024,1024]{1,0:T(8,128)(2,1)S(1)}, bf16[1024,1024]{1,0:T(8,128)(2,1)}, u32[]{:S(2)}) copy-start(bf16[1024,1024]{1,0:T(8,128)(2,1)} %constant.105.clone.refs_12_) | copy-start | bytes 6291460
  76.4 2.7 %collective-permute-start.16 = (f32[256,1024]{1,0:T(8,128)S(1)}, f32[256,1024]{1,0:T(8,128)S(1)}, u32[]{:S(2)}, u32[]{:S(2)}) collective-permute-start(f32[256,1024]{1,0:T(8,128)S(1)} %get-tuple-element.8), channel_id=1, source_target_pairs={{0,8},{1,9},{2,10},{3,11},{4,12},{5,13},{6,14},{7,15},{8,0},{9,1},... | collective-permute-start | bytes 3145736 | tf_op jit(solution)/shard_map/ppermute | solution.py:94

commit v2 on v0

--- a/solution.py
+++ b/solution.py
@@ -1,9 +1,18 @@
+import functools
+
 import jax
 import jax.numpy as jnp
+import numpy as np
 from jax import lax
+from jax.experimental import pallas as pl
+from jax.experimental.pallas import tpu as pltpu
 from jax.sharding import PartitionSpec as P
 
 LAGS = 1024
+AXES = ("tm", "sta")
+ROWS, CORES, LAYERS, COLUMNS = 2, 2, 4, 2
+BLOCK = 256
+FIRST_BINS = 512
 
 
 def lag_table(bins, lags):
@@ -24,7 +33,7 @@
     return jnp.concatenate([real_c, imag_c], axis=-1)
 
 
-def local(spectra, pair_list, pair_stations, owner_code):
+def local_any_size(spectra, pair_list, pair_stations, owner_code):
     local_spectra = spectra[0]
     width = local_spectra.shape[1]
     bins = width // 2
@@ -58,9 +67,186 @@
     )
 
 
+def moves(target):
+    def place(row, core, layer, column):
+        return (row * CORES + core) * LAYERS * COLUMNS + layer * COLUMNS + column
+
+    return [
+        (place(row, core, layer, column), place(*target(row, core, layer, column)))
+        for row in range(ROWS)
+        for core in range(CORES)
+        for layer in range(LAYERS)
+        for column in range(COLUMNS)
+    ]
+
+
+OTHER_ROW = moves(lambda r, c, z, x: (1 - r, c, z, x))
+OTHER_CORE = moves(lambda r, c, z, x: (r, 1 - c, z, x))
+OTHER_COLUMN = moves(lambda r, c, z, x: (r, c, z, 1 - x))
+DIAGONAL = moves(lambda r, c, z, x: (1 - r, c, z, x) if c == 0 else (r, c, z, 1 - x))
+
+
+def layer_turn(step):
+    return moves(lambda r, c, z, x: (r, c, (z + step) % LAYERS, x))
+
+
+def send(value, pairs):
+    return lax.ppermute(value, AXES, pairs)
+
+
+def split_table(bins, start, stop):
+    index = np.arange(bins)[:, None] * (np.arange(LAGS)[None, :] - LAGS // 2) % (2 * bins)
+    angle = index * (np.pi / bins)
+    both = np.stack([np.cos(angle), -np.sin(angle)]) / np.sqrt(bins)
+    rows = both[:, start:stop].reshape(-1, LAGS).astype(np.float32)
+    high = rows.astype(jnp.bfloat16)
+    low = (rows - high.astype(np.float32)).astype(jnp.bfloat16)
+    return jnp.asarray(high), jnp.asarray(low)
+
+
+def two_parts(value):
+    high = value.astype(jnp.bfloat16)
+    return high, (value - high.astype(jnp.float32)).astype(jnp.bfloat16)
+
+
+def chunk_kernel(final, start, bins, picks_ref, *refs):
+    tops, rests, refs = refs[:4], refs[4:8], refs[8:]
+    table_high, table_low, refs = refs[0], refs[1], refs[2:]
+    if final:
+        earlier_ref, select_ref, theirs_ref, ours_ref, high_cross, low_cross = refs
+    else:
+        total_ref, high_cross, low_cross = refs
+    entries = picks_ref.shape[1] // 2
+    chunk = rests[0].shape[1] // 2
+
+    for segment in range(2):
+        rows = slice(segment * entries, (segment + 1) * entries)
+        for at in range(0, chunk, BLOCK):
+            blocks = []
+            for side in (2 * segment, 2 * segment + 1):
+                for ref, real in ((tops[side], start + at), (rests[side], at)):
+                    imag = real + (bins if ref is tops[side] else chunk)
+                    blocks.append(
+                        jnp.concatenate(
+                            [ref[:, real : real + BLOCK], ref[:, imag : imag + BLOCK]], axis=1
+                        )
+                    )
+            stations = jnp.concatenate(blocks, axis=0)
+            both = jnp.dot(picks_ref[segment], stations, preferred_element_type=jnp.float32)
+            real_a, imag_a = both[:entries, :BLOCK], both[:entries, BLOCK:]
+            real_b, imag_b = both[entries:, :BLOCK], both[entries:, BLOCK:]
+            for value, column in (
+                (real_a * real_b + imag_a * imag_b, at),
+                (real_a * imag_b - imag_a * real_b, chunk + at),
+            ):
+                columns = slice(column, column + BLOCK)
+                high_cross[rows, columns], low_cross[rows, columns] = two_parts(value)
+
+    dot = functools.partial(jnp.dot, preferred_element_type=jnp.float32)
+    lags = dot(high_cross[...], table_high[...])
+    lags += dot(low_cross[...], table_high[...])
+    lags += dot(high_cross[...], table_low[...])
+    if final:
+        high, low = two_parts(earlier_ref[...] + lags)
+        for part, out_ref in enumerate((theirs_ref, ours_ref)):
+            out_ref[...] = dot(select_ref[part], high) + dot(select_ref[part], low)
+    else:
+        total_ref[...] = lags
+
+
+def correlate_chunk(picks, tops, rests, start, stop, bins, earlier=None, select=None):
+    final = earlier is not None
+    entries = picks.shape[1]
+    operands = [picks, *tops, *rests, *split_table(bins, start, stop)]
+    out_shape = [jax.ShapeDtypeStruct((entries, LAGS), jnp.float32)]
+    if final:
+        operands += [earlier, select]
+        out_shape = [jax.ShapeDtypeStruct((select.shape[1], LAGS), jnp.float32)] * 2
+    in_vmem = pl.BlockSpec(memory_space=pltpu.VMEM)
+    return pl.pallas_call(
+        functools.partial(chunk_kernel, final, start, bins),
+        out_shape=out_shape,
+        in_specs=[in_vmem] * len(operands),
+        out_specs=[in_vmem] * len(out_shape),
+        scratch_shapes=[pltpu.VMEM((entries, 2 * (stop - start)), jnp.bfloat16)] * 2,
+        compiler_params=pltpu.CompilerParams(vmem_limit_bytes=24 * 1024 * 1024),
+        cost_estimate=pl.CostEstimate(
+            flops=2 * entries * (stop - start) * 2 * (3 * LAGS + entries),
+            bytes_accessed=(stop - start) * 2 * (4 * LAGS + 16 * tops[0].shape[0] * 2),
+            transcendentals=0,
+        ),
+        name="correlate_last" if final else "correlate",
+    )(*operands)
+
+
+def local_grid(spectra, pair_list, pair_stations, owner_code):
+    own = spectra[0]
+    stations, width = own.shape
+    bins = width // 2
+    catalogue = pair_stations.shape[1]
+    capacity = 2 * catalogue // (ROWS * CORES)
+    row, core = lax.axis_index("tm") // CORES, lax.axis_index("tm") % CORES
+    layer, column = lax.axis_index("sta") // COLUMNS, lax.axis_index("sta") % COLUMNS
+    after = lambda value, *others: lax.optimization_barrier((value, *others))[0]
+
+    def around(value, *others):
+        side = send(value, OTHER_COLUMN)
+        ahead = send(value, OTHER_ROW)
+        return side, ahead
+
+    def diagonal(side, ahead, *others):
+        forwarded = after(jnp.where(core == 0, side, ahead), *others)
+        return send(forwarded, DIAGONAL)
+
+    def turn(value):
+        return [send(value, layer_turn(step)) for step in (2, 1, 3)]
+
+    def chunk(start, stop):
+        return jnp.concatenate([own[:, start:stop], own[:, bins + start : bins + stop]], axis=1)
+
+    listed_here = pair_list[0, 0]
+    cuts = [(0, FIRST_BINS), (FIRST_BINS, bins)]
+    side_own, ahead_own = around(own)
+    turned_first = turn(chunk(*cuts[0]))
+    diagonal_own = diagonal(side_own, ahead_own)
+    listed_there = send(after(listed_here, side_own, ahead_own), OTHER_ROW)
+    turned_last = turn(after(chunk(*cuts[1]), side_own, ahead_own))
+    rest = after(jnp.concatenate(turned_first, axis=0), diagonal_own)
+    side, ahead = around(rest)
+    first_rests = (rest, side, ahead, diagonal(side, ahead))
+    rest = after(jnp.concatenate(turned_last, axis=0), side, ahead)
+    side, ahead = around(rest)
+    tops = (own, side_own, ahead_own, diagonal_own)
+
+    listed = jnp.stack([listed_here, listed_there])
+    hit = listed[:, :, None] == jnp.arange(catalogue, dtype=jnp.int32)
+    look_up = lambda values: jnp.sum(jnp.where(hit, values, 0), axis=-1)
+    pair = jnp.concatenate([look_up(pair_stations[0]), look_up(pair_stations[1])], axis=1)
+    holder, place = pair // stations, pair % stations
+    turns = (layer - holder // COLUMNS) % LAYERS
+    turns = jnp.where(turns == 2, 1, jnp.where(turns == 1, 2, turns))
+    beside = (holder % COLUMNS) ^ column
+    position = (beside * LAYERS + turns) * stations + place
+    spots = jnp.arange(COLUMNS * LAYERS * stations, dtype=jnp.int32)
+    picks = (position[:, :, None] == spots).astype(jnp.bfloat16)
+    codes = look_up(owner_code).reshape(-1)
+    owner = row * CORES + jnp.stack([1 - core, core])
+    slots = owner[:, None] * capacity + jnp.arange(capacity, dtype=jnp.int32)
+    select = (slots[:, :, None] == codes).astype(jnp.bfloat16)
+
+    (early,) = correlate_chunk(picks, tops, first_rests, *cuts[0], bins)
+    last_rests = (rest, side, ahead, diagonal(side, ahead))
+    theirs, ours = correlate_chunk(
+        picks, tops, last_rests, *cuts[1], bins, earlier=early, select=select
+    )
+    return ours + send(theirs, OTHER_CORE)
+
+
 def solution(mesh):
+    sizes = (mesh.shape["tm"], mesh.shape["sta"])
+    fits = sizes == (ROWS * CORES, LAYERS * COLUMNS)
     return jax.shard_map(
-        local,
+        local_grid if fits else local_any_size,
         mesh=mesh,
         in_specs=(P("tm", "sta", None), P("tm", "sta", None), P(None, "sta"), P("sta")),
         out_specs=P(("tm", "sta"), None),

time: 135 us -> 63.7 us (0.47)
  waiting for transfers between devices: 72.5 us -> 26.2 us
  starting transfers between devices: 0.04 us -> 22.5 us
  other arithmetic: 21.2 us -> 2.57 us
  local copies, waits for them, and re-layouts: 15.9 us -> 1.79 us
  between operations: 13.5 us -> 0.22 us
  matrix products: 11.1 us -> 0 us
  Pallas kernels: 0 us -> 10.2 us
    reduce_scatter x1 -> x0, waiting for transfers between devices: 43.1 us -> none  [local(): lax.psum_scatter(jnp.dot(select, partial_lags, precision=lax.Precision.HI...]
    all_gather x1 -> x0, waiting for transfers between devices: 28.7 us -> none  [local(): all_spectra = lax.all_gather(local_spectra, 'sta', axis=0, tiled=True)]
    ppermute x0 -> x17, waiting for transfers between devices: none -> 26.2 us  [send(): return lax.ppermute(value, AXES, pairs)]
    ppermute x0 -> x17, starting transfers between devices: none -> 22.5 us  [send(): return lax.ppermute(value, AXES, pairs)]
    mul x1, other arithmetic: 18.2 us -> 0.08 us  [local_grid(): slots = owner[:, None] * capacity + jnp.arange(capacity, dtype=jnp.int32)]
    gather x5 -> x0, local copies, waits for them, and re-layouts: 12.5 us -> none  [the longest x1 4.38 us: local(): first = all_spectra[first_station]]
    dot_general x2 -> x0, matrix products: 11.1 us -> none  [the longest x1 7.31 us: local(): jnp.dot(cross, table, precision=lax.Precision.HIGHEST, preferred_element_...]
    pallas_call x0 -> x2, Pallas kernels: none -> 10.2 us  [correlate_chunk(): pl.pallas_call(functools.partial(chunk_kernel, final, start, bins), out_s...]
  transfers between devices with their start and end apart: 2 -> 17, of which waited for: 2 -> 9; matrix products, arithmetic and copies ran while one was open for 19% -> 3% of each run, Pallas kernels for 0% -> 7%
where the time goes in v2:
time: 63.7 us; the launch traced here: 63.5 us
  waiting for transfers between devices  26.2 us (41%)
  starting transfers between devices  22.5 us (35%)
  Pallas kernels  10.2 us (16%)
  other arithmetic  2.57 us (4%)
  local copies, waits for them, and re-layouts  1.79 us (3%)
    ppermute x17, waiting for transfers between devices, send(): return lax.ppermute(value, AXES, pairs)  26.2 us
    ppermute x17, starting transfers between devices, send(): return lax.ppermute(value, AXES, pairs)  22.5 us
    pallas_call x2, Pallas kernels, correlate_chunk(): pl.pallas_call(functools.partial(chunk_kernel, final, start, bins), out_s...  10.2 us
  transfers between devices with their start and end apart: 17, of which 9 were waited for; matrix products, arithmetic and copies ran while one was open for 3% of the time, Pallas kernels for 7%

profile of v2, /device:TPU:0, one launch (start us, length us, event | category | flops | bytes accessed | tf_op | source)
XLA Modules:
  0.0 63.5 jit_solution(7797213029934064808)
XLA Ops:
  0.0 1.0 %fusion.7 = (bf16[64,512]{1,0:T(8,128)(2,1)S(1)}, bf16[64,512]{1,0:T(8,128)(2,1)S(1)}, bf16[64,512]{1,0:T(8,128)(2,1)S(1)}, bf16[64,512]{1,0:T(8,128)(2,1)S(1)}) fusion(bf16[64,2048]{1,0:T(8,128)(2,1)} %bitcast.10), kind=kLoop, calls=%fused_computation.39 | loop fusion | bytes 524288 | tf_op jit(solution)/shard_map/slice | solution.py:205
  1.0 5.1 %collective-permute-start.9 = (bf16[64,1024]{1,0:T(8,128)(2,1)S(1)}, bf16[64,1024]{1,0:T(8,128)(2,1)S(1)}, u32[]{:S(2)}, u32[]{:S(2)}) collective-permute-start(bf16[64,1024]{1,0:T(8,128)(2,1)S(1)} %pad_maximum_fusion.3), channel_id=1, source_target_pairs={{0,6},{1,7},{2,0},{3,1},{4,2},{5,3},{6,4},{7,5},{8,14},{9,15},{10,... | collective-permute-start | bytes 393224 | tf_op jit(solution)/shard_map/ppermute | solution.py:94
  6.1 1.0 %collective-permute-start.7 = (bf16[64,1024]{1,0:T(8,128)(2,1)S(1)}, bf16[64,1024]{1,0:T(8,128)(2,1)S(1)}, u32[]{:S(2)}, u32[]{:S(2)}) collective-permute-start(bf16[64,1024]{1,0:T(8,128)(2,1)S(1)} %pad_maximum_fusion.3), channel_id=1, source_target_pairs={{0,4},{1,5},{2,6},{3,7},{4,0},{5,1},{6,2},{7,3},{8,12},{9,13},{10,... | collective-permute-start | bytes 393224 | tf_op jit(solution)/shard_map/ppermute | solution.py:94
  7.1 1.5 %collective-permute-start.1 = (bf16[64,2048]{1,0:T(8,128)(2,1)}, bf16[64,2048]{1,0:T(8,128)(2,1)S(1)}, u32[]{:S(2)}, u32[]{:S(2)}) collective-permute-start(bf16[64,2048]{1,0:T(8,128)(2,1)} %bitcast.11), channel_id=1, source_target_pairs={{0,16},{1,17},{2,18},{3,19},{4,20},{5,21},{6,22},{7,23},{8,24},{9,... | collective-permute-start | bytes 786440 | tf_op jit(solution)/shard_map/ppermute | solution.py:94
  8.6 1.5 %collective-permute-start = (bf16[64,2048]{1,0:T(8,128)(2,1)}, bf16[64,2048]{1,0:T(8,128)(2,1)S(1)}, u32[]{:S(2)}, u32[]{:S(2)}) collective-permute-start(bf16[64,2048]{1,0:T(8,128)(2,1)} %bitcast.12), channel_id=1, source_target_pairs={{0,1},{1,0},{2,3},{3,2},{4,5},{5,4},{6,7},{7,6},{8,9},{9,8},{10,11... | collective-permute-start | bytes 786440 | tf_op jit(solution)/shard_map/ppermute | solution.py:94
  10.1 0.1 fusion.6
  10.2 0.1 iota_add_fusion
  10.3 0.8 %fusion.8 = (s32[1,512]{1,0:T(1,128)S(1)}, s32[1,512]{1,0:T(1,128)S(1)}) fusion(s32[2,512]{1,0:T(2,128)} %param.10), kind=kLoop, calls=%fused_computation.40 | loop fusion | bytes 8192 | tf_op jit(solution)/shard_map/slice | solution.py:224
  11.1 3.5 %collective-permute-done.1.refs_2_ = bf16[64,2048]{1,0:T(8,128)(2,1)S(1)} collective-permute-done((bf16[64,2048]{1,0:T(8,128)(2,1)}, bf16[64,2048]{1,0:T(8,128)(2,1)S(1)}, u32[]{:S(2)}, u32[]{:S(2)}) %collective-permute-start.1) | collective-permute-done | bytes 262176 | tf_op jit(solution)/shard_map/ppermute | solution.py:94
  14.5 1.2 %collective-permute-done.refs_1_ = bf16[64,2048]{1,0:T(8,128)(2,1)S(1)} collective-permute-done((bf16[64,2048]{1,0:T(8,128)(2,1)}, bf16[64,2048]{1,0:T(8,128)(2,1)S(1)}, u32[]{:S(2)}, u32[]{:S(2)}) %collective-permute-start) | collective-permute-done | bytes 262176 | tf_op jit(solution)/shard_map/ppermute | solution.py:94
  15.8 0.6 collective-permute-start.3
  16.4 1.6 %collective-permute-start.2 = (s32[256]{0:T(256)}, s32[256]{0:T(256)S(1)}, u32[]{:S(2)}, u32[]{:S(2)}) collective-permute-start(s32[256]{0:T(256)} %bitcast.19), channel_id=1, source_target_pairs={{0,16},{1,17},{2,18},{3,19},{4,20},{5,21},{6,22},{7,23},{8,24},{9,... | collective-permute-start | bytes 3080 | tf_op jit(solution)/shard_map/ppermute | solution.py:94
  18.0 0.0 collective-permute-done.9
  18.0 0.0 collective-permute-done.8
  18.0 0.0 collective-permute-done.7
  18.0 3.1 %collective-permute-start.6 = (bf16[64,1024]{1,0:T(8,128)(2,1)S(1)}, bf16[64,1024]{1,0:T(8,128)(2,1)S(1)}, u32[]{:S(2)}, u32[]{:S(2)}) collective-permute-start(bf16[64,1024]{1,0:T(8,128)(2,1)S(1)} %pad_maximum_fusion.2), channel_id=1, source_target_pairs={{0,6},{1,7},{2,0},{3,1},{4,2},{5,3},{6,4},{7,5},{8,14},{9,15},{10,... | collective-permute-start | bytes 393224 | tf_op jit(solution)/shard_map/ppermute | solution.py:94
  21.2 0.3 collective-permute-start.5
  21.5 1.4 %collective-permute-start.4 = (bf16[64,1024]{1,0:T(8,128)(2,1)S(1)}, bf16[64,1024]{1,0:T(8,128)(2,1)S(1)}, u32[]{:S(2)}, u32[]{:S(2)}) collective-permute-start(bf16[64,1024]{1,0:T(8,128)(2,1)S(1)} %pad_maximum_fusion.2), channel_id=1, source_target_pairs={{0,4},{1,5},{2,6},{3,7},{4,0},{5,1},{6,2},{7,3},{8,12},{9,13},{10,... | collective-permute-start | bytes 393224 | tf_op jit(solution)/shard_map/ppermute | solution.py:94
  22.9 0.0 collective-permute-done.2
  23.0 0.0 collective-permute-done.3.refs_3_
  23.0 0.6 collective-permute-start.11
  23.5 1.5 %collective-permute-start.10 = (bf16[192,1024]{1,0:T(8,128)(2,1)S(1)}, bf16[192,1024]{1,0:T(8,128)(2,1)S(1)}, u32[]{:S(2)}, u32[]{:S(2)}) collective-permute-start(bf16[192,1024]{1,0:T(8,128)(2,1)S(1)} %pad_maximum_fusion.1.refs_4_), channel_id=1, source_target_pairs={{0,1},{1,0},{2,3},{3,2},{4,5},{5,4},{6,7},{7,6},{8,9},{9,8},{10,11... | collective-permute-start | bytes 1179656 | tf_op jit(solution)/shard_map/ppermute | solution.py:94
  25.0 0.7 %select_reduce_fusion = (s32[2,256]{1,0:T(2,128)S(1)}, s32[2,256]{1,0:T(2,128)S(1)}, s32[2,256]{1,0:T(2,128)S(1)}) fusion(s32[512]{0:T(512)S(1)} %copy-done.5, s32[2,256]{1,0:T(2,128)S(1)} %pad_add_fusion.1, s32[512]{0:T(512)S(1)} %bitcast.18, s32[512]{0:T(512)S(1)} %bitcast.17), kind=kLoop, calls=%fused_computation.2 | loop fusion | flops 1833472 | bytes 14336 | tf_op jit(solution)/shard_map/reduce_sum | solution.py:223
  25.7 0.1 fusion.4
  25.8 1.1 %collective-permute-done.6 = bf16[64,1024]{1,0:T(8,128)(2,1)S(1)} collective-permute-done((bf16[64,1024]{1,0:T(8,128)(2,1)S(1)}, bf16[64,1024]{1,0:T(8,128)(2,1)S(1)}, u32[]{:S(2)}, u32[]{:S(2)}) %collective-permute-start.6) | collective-permute-done | bytes 131104 | tf_op jit(solution)/shard_map/ppermute | solution.py:94
  26.9 2.1 %collective-permute-done.5 = bf16[64,1024]{1,0:T(8,128)(2,1)S(1)} collective-permute-done((bf16[64,1024]{1,0:T(8,128)(2,1)S(1)}, bf16[64,1024]{1,0:T(8,128)(2,1)S(1)}, u32[]{:S(2)}, u32[]{:S(2)}) %collective-permute-start.5) | collective-permute-done | bytes 131104 | tf_op jit(solution)/shard_map/ppermute | solution.py:94
  29.0 3.4 %collective-permute-done.4 = bf16[64,1024]{1,0:T(8,128)(2,1)S(1)} collective-permute-done((bf16[64,1024]{1,0:T(8,128)(2,1)S(1)}, bf16[64,1024]{1,0:T(8,128)(2,1)S(1)}, u32[]{:S(2)}, u32[]{:S(2)}) %collective-permute-start.4) | collective-permute-done | bytes 131104 | tf_op jit(solution)/shard_map/ppermute | solution.py:94
  32.5 0.0 copy-start
  32.5 0.0 copy-start.3
  32.5 0.0 collective-permute-done.11.refs_6_
  32.5 0.0 collective-permute-done.10.refs_5_
  32.5 1.6 %collective-permute-start.13 = (bf16[192,1024]{1,0:T(8,128)(2,1)S(1)}, bf16[192,1024]{1,0:T(8,128)(2,1)S(1)}, u32[]{:S(2)}, u32[]{:S(2)}) collective-permute-start(bf16[192,1024]{1,0:T(8,128)(2,1)S(1)} %pad_maximum_fusion.refs_4_), channel_id=1, source_target_pairs={{0,16},{1,17},{2,18},{3,19},{4,20},{5,21},{6,22},{7,23},{8,24},{9,... | collective-permute-start | bytes 1179656 | tf_op jit(solution)/shard_map/ppermute | solution.py:94
  34.1 1.5 %collective-permute-start.12 = (bf16[192,1024]{1,0:T(8,128)(2,1)S(1)}, bf16[192,1024]{1,0:T(8,128)(2,1)S(1)}, u32[]{:S(2)}, u32[]{:S(2)}) collective-permute-start(bf16[192,1024]{1,0:T(8,128)(2,1)S(1)} %pad_maximum_fusion.refs_4_), channel_id=1, source_target_pairs={{0,1},{1,0},{2,3},{3,2},{4,5},{5,4},{6,7},{7,6},{8,9},{9,8},{10,11... | collective-permute-start | bytes 1179656 | tf_op jit(solution)/shard_map/ppermute | solution.py:94
  35.6 0.2 fusion.picks_ref
  35.9 0.6 collective-permute-start.15
  36.4 4.5 %collective-permute-done.13.refs_6_ = bf16[192,1024]{1,0:T(8,128)(2,1)S(1)} collective-permute-done((bf16[192,1024]{1,0:T(8,128)(2,1)S(1)}, bf16[192,1024]{1,0:T(8,128)(2,1)S(1)}, u32[]{:S(2)}, u32[]{:S(2)}) %collective-permute-start.13) | collective-permute-done | bytes 393248 | tf_op jit(solution)/shard_map/ppermute | solution.py:94
  40.9 5.2 %collective-permute-done.12.refs_5_ = bf16[192,1024]{1,0:T(8,128)(2,1)S(1)} collective-permute-done((bf16[192,1024]{1,0:T(8,128)(2,1)S(1)}, bf16[192,1024]{1,0:T(8,128)(2,1)S(1)}, u32[]{:S(2)}, u32[]{:S(2)}) %collective-permute-start.12) | collective-permute-done | bytes 393248 | tf_op jit(solution)/shard_map/ppermute | solution.py:94
  46.2 0.6 collective-permute-start.14
  46.8 0.1 compare_convert_fusion.refs_11_
  46.9 0.0 copy-start.1
  46.9 0.0 copy-start.2
  46.9 0.0 collective-permute-done.15.refs_7_
  47.0 4.5 %correlate.1.refs_10_ = f32[512,1024]{1,0:T(8,128)S(1)} custom-call(bf16[2,512,512]{2,1,0:T(8,128)(2,1)S(1)} %fusion.picks_ref, bf16[64,2048]{1,0:T(8,128)(2,1)S(1)} %bitcast.13, bf16[64,2048]{1,0:T(8,128)(2,1)S(1)} %collective-permute-done.refs_1_, bf16[64,2048]{1,0:T(8,128)(2,1)S(1)} %collective-permute-done.1.refs_2_, ...), custom_call_target="tpu_custom_call" | custom-call | flops 3758096384 | bytes 6291456 | tf_op jit(solution)/shard_map/correlate/pallas_call | solution.py:166
  51.5 2.5 %collective-permute-done.14.refs_7_ = bf16[192,1024]{1,0:T(8,128)(2,1)S(1)} collective-permute-done((bf16[192,1024]{1,0:T(8,128)(2,1)S(1)}, bf16[192,1024]{1,0:T(8,128)(2,1)S(1)}, u32[]{:S(2)}, u32[]{:S(2)}) %collective-permute-start.14) | collective-permute-done | bytes 393248 | tf_op jit(solution)/shard_map/ppermute | solution.py:94
  54.0 5.6 %correlate_last.1 = (f32[256,1024]{1,0:T(8,128)S(1)}, f32[256,1024]{1,0:T(8,128)S(1)}) custom-call(bf16[2,512,512]{2,1,0:T(8,128)(2,1)S(1)} %fusion.picks_ref, bf16[64,2048]{1,0:T(8,128)(2,1)S(1)} %bitcast.14, bf16[64,2048]{1,0:T(8,128)(2,1)S(1)} %collective-permute-done.refs_1_, bf16[64,2048]{1,0:T(8,128)(2,1)S(1)} %collective-permute-done.1.refs_2_, ...), custom_call_target="tpu_custom_call" | custom-call | flops 3758096384 | bytes 6291456 | tf_op jit(solution)/shard_map/correlate_last/pallas_call | solution.py:166
  59.7 0.1 collective-permute-start.16
  59.8 2.6 %collective-permute-done.16 = f32[256,1024]{1,0:T(8,128)S(1)} collective-permute-done((f32[256,1024]{1,0:T(8,128)S(1)}, f32[256,1024]{1,0:T(8,128)S(1)}, u32[]{:S(2)}, u32[]{:S(2)}) %collective-permute-start.16) | collective-permute-done | bytes 1048608 | tf_op jit(solution)/shard_map/ppermute | solution.py:94
  62.4 1.1 %add.101 = f32[256,1024]{1,0:T(8,128)} add(f32[256,1024]{1,0:T(8,128)S(1)} %get-tuple-element.15, f32[256,1024]{1,0:T(8,128)S(1)} %collective-permute-done.16) | non-fusion elementwise | flops 262144 | bytes 3145728 | tf_op jit(solution)/shard_map/add | solution.py:242
  (20 shorter events, 0.2 us)
Async XLA Ops:
  0.0 22.9 %copy-start.6 = (s32[1,1,256]{2,1,0:T(1,128)S(1)}, s32[1,1,256]{2,1,0:T(1,128)}, u32[]{:S(2)}) copy-start(s32[1,1,256]{2,1,0:T(1,128)} %param.9) | copy-start | bytes 3076
  0.0 25.0 %copy-start.5 = (s32[512]{0:T(512)S(1)}, s32[512]{0:T(512)}, u32[]{:S(2)}) copy-start(s32[512]{0:T(512)} %param.11) | copy-start | bytes 6148
  1.0 17.0 %collective-permute-start.9 = (bf16[64,1024]{1,0:T(8,128)(2,1)S(1)}, bf16[64,1024]{1,0:T(8,128)(2,1)S(1)}, u32[]{:S(2)}, u32[]{:S(2)}) collective-permute-start(bf16[64,1024]{1,0:T(8,128)(2,1)S(1)} %pad_maximum_fusion.3), channel_id=1, source_target_pairs={{0,6},{1,7},{2,0},{3,1},{4,2},{5,3},{6,4},{7,5},{8,14},{9,15},{10,... | collective-permute-start | bytes 393224 | tf_op jit(solution)/shard_map/ppermute | solution.py:94
  6.1 11.9 %collective-permute-start.8 = (bf16[64,1024]{1,0:T(8,128)(2,1)S(1)}, bf16[64,1024]{1,0:T(8,128)(2,1)S(1)}, u32[]{:S(2)}, u32[]{:S(2)}) collective-permute-start(bf16[64,1024]{1,0:T(8,128)(2,1)S(1)} %pad_maximum_fusion.3), channel_id=1, source_target_pairs={{0,2},{1,3},{2,4},{3,5},{4,6},{5,7},{6,0},{7,1},{8,10},{9,11},{10,... | collective-permute-start | bytes 393224 | tf_op jit(solution)/shard_map/ppermute | solution.py:94
  6.1 11.9 %collective-permute-start.7 = (bf16[64,1024]{1,0:T(8,128)(2,1)S(1)}, bf16[64,1024]{1,0:T(8,128)(2,1)S(1)}, u32[]{:S(2)}, u32[]{:S(2)}) collective-permute-start(bf16[64,1024]{1,0:T(8,128)(2,1)S(1)} %pad_maximum_fusion.3), channel_id=1, source_target_pairs={{0,4},{1,5},{2,6},{3,7},{4,0},{5,1},{6,2},{7,3},{8,12},{9,13},{10,... | collective-permute-start | bytes 393224 | tf_op jit(solution)/shard_map/ppermute | solution.py:94
  7.1 7.4 %collective-permute-start.1 = (bf16[64,2048]{1,0:T(8,128)(2,1)}, bf16[64,2048]{1,0:T(8,128)(2,1)S(1)}, u32[]{:S(2)}, u32[]{:S(2)}) collective-permute-start(bf16[64,2048]{1,0:T(8,128)(2,1)} %bitcast.11), channel_id=1, source_target_pairs={{0,16},{1,17},{2,18},{3,19},{4,20},{5,21},{6,22},{7,23},{8,24},{9,... | collective-permute-start | bytes 786440 | tf_op jit(solution)/shard_map/ppermute | solution.py:94
  8.6 7.1 %collective-permute-start = (bf16[64,2048]{1,0:T(8,128)(2,1)}, bf16[64,2048]{1,0:T(8,128)(2,1)S(1)}, u32[]{:S(2)}, u32[]{:S(2)}) collective-permute-start(bf16[64,2048]{1,0:T(8,128)(2,1)} %bitcast.12), channel_id=1, source_target_pairs={{0,1},{1,0},{2,3},{3,2},{4,5},{5,4},{6,7},{7,6},{8,9},{9,8},{10,11... | collective-permute-start | bytes 786440 | tf_op jit(solution)/shard_map/ppermute | solution.py:94
  15.8 7.1 %collective-permute-start.3 = (bf16[64,2048]{1,0:T(8,128)(2,1)S(1)}, bf16[64,2048]{1,0:T(8,128)(2,1)S(1)}, u32[]{:S(2)}, u32[]{:S(2)}) collective-permute-start(bf16[64,2048]{1,0:T(8,128)(2,1)S(1)} %broadcast_select_fusion.2), channel_id=1, source_target_pairs={{0,16},{1,17},{2,18},{3,19},{4,20},{5,21},{6,22},{7,23},{8,9},{9,8... | collective-permute-start | bytes 786440 | tf_op jit(solution)/shard_map/ppermute | solution.py:94
  16.4 6.5 %collective-permute-start.2 = (s32[256]{0:T(256)}, s32[256]{0:T(256)S(1)}, u32[]{:S(2)}, u32[]{:S(2)}) collective-permute-start(s32[256]{0:T(256)} %bitcast.19), channel_id=1, source_target_pairs={{0,16},{1,17},{2,18},{3,19},{4,20},{5,21},{6,22},{7,23},{8,24},{9,... | collective-permute-start | bytes 3080 | tf_op jit(solution)/shard_map/ppermute | solution.py:94
  18.0 8.8 %collective-permute-start.6 = (bf16[64,1024]{1,0:T(8,128)(2,1)S(1)}, bf16[64,1024]{1,0:T(8,128)(2,1)S(1)}, u32[]{:S(2)}, u32[]{:S(2)}) collective-permute-start(bf16[64,1024]{1,0:T(8,128)(2,1)S(1)} %pad_maximum_fusion.2), channel_id=1, source_target_pairs={{0,6},{1,7},{2,0},{3,1},{4,2},{5,3},{6,4},{7,5},{8,14},{9,15},{10,... | collective-permute-start | bytes 393224 | tf_op jit(solution)/shard_map/ppermute | solution.py:94
  21.2 7.8 %collective-permute-start.5 = (bf16[64,1024]{1,0:T(8,128)(2,1)S(1)}, bf16[64,1024]{1,0:T(8,128)(2,1)S(1)}, u32[]{:S(2)}, u32[]{:S(2)}) collective-permute-start(bf16[64,1024]{1,0:T(8,128)(2,1)S(1)} %pad_maximum_fusion.2), channel_id=1, source_target_pairs={{0,2},{1,3},{2,4},{3,5},{4,6},{5,7},{6,0},{7,1},{8,10},{9,11},{10,... | collective-permute-start | bytes 393224 | tf_op jit(solution)/shard_map/ppermute | solution.py:94
  21.5 10.9 %collective-permute-start.4 = (bf16[64,1024]{1,0:T(8,128)(2,1)S(1)}, bf16[64,1024]{1,0:T(8,128)(2,1)S(1)}, u32[]{:S(2)}, u32[]{:S(2)}) collective-permute-start(bf16[64,1024]{1,0:T(8,128)(2,1)S(1)} %pad_maximum_fusion.2), channel_id=1, source_target_pairs={{0,4},{1,5},{2,6},{3,7},{4,0},{5,1},{6,2},{7,3},{8,12},{9,13},{10,... | collective-permute-start | bytes 393224 | tf_op jit(solution)/shard_map/ppermute | solution.py:94
  23.0 9.5 %collective-permute-start.11 = (bf16[192,1024]{1,0:T(8,128)(2,1)S(1)}, bf16[192,1024]{1,0:T(8,128)(2,1)S(1)}, u32[]{:S(2)}, u32[]{:S(2)}) collective-permute-start(bf16[192,1024]{1,0:T(8,128)(2,1)S(1)} %pad_maximum_fusion.1.refs_4_), channel_id=1, source_target_pairs={{0,16},{1,17},{2,18},{3,19},{4,20},{5,21},{6,22},{7,23},{8,24},{9,... | collective-permute-start | bytes 1179656 | tf_op jit(solution)/shard_map/ppermute | solution.py:94
  23.5 8.9 %collective-permute-start.10 = (bf16[192,1024]{1,0:T(8,128)(2,1)S(1)}, bf16[192,1024]{1,0:T(8,128)(2,1)S(1)}, u32[]{:S(2)}, u32[]{:S(2)}) collective-permute-start(bf16[192,1024]{1,0:T(8,128)(2,1)S(1)} %pad_maximum_fusion.1.refs_4_), channel_id=1, source_target_pairs={{0,1},{1,0},{2,3},{3,2},{4,5},{5,4},{6,7},{7,6},{8,9},{9,8},{10,11... | collective-permute-start | bytes 1179656 | tf_op jit(solution)/shard_map/ppermute | solution.py:94
  32.4 14.5 %copy-start.4 = (bf16[1024,1024]{1,0:T(8,128)(2,1)S(1)}, bf16[1024,1024]{1,0:T(8,128)(2,1)}, u32[]{:S(2)}) copy-start(bf16[1024,1024]{1,0:T(8,128)(2,1)} %constant.107.clone.refs_8_) | copy-start | bytes 6291460
  32.5 14.5 %copy-start = (bf16[1,64,2048]{2,1,0:T(8,128)(2,1)S(1)}, bf16[1,64,2048]{2,1,0:T(8,128)(2,1)}, u32[]{:S(2)}) copy-start(bf16[1,64,2048]{2,1,0:T(8,128)(2,1)} %param.8) | copy-start | bytes 786436
  32.5 14.5 %copy-start.3 = (bf16[1024,1024]{1,0:T(8,128)(2,1)S(1)}, bf16[1024,1024]{1,0:T(8,128)(2,1)}, u32[]{:S(2)}) copy-start(bf16[1024,1024]{1,0:T(8,128)(2,1)} %constant.108.clone.refs_9_) | copy-start | bytes 6291460
  32.5 8.4 %collective-permute-start.13 = (bf16[192,1024]{1,0:T(8,128)(2,1)S(1)}, bf16[192,1024]{1,0:T(8,128)(2,1)S(1)}, u32[]{:S(2)}, u32[]{:S(2)}) collective-permute-start(bf16[192,1024]{1,0:T(8,128)(2,1)S(1)} %pad_maximum_fusion.refs_4_), channel_id=1, source_target_pairs={{0,16},{1,17},{2,18},{3,19},{4,20},{5,21},{6,22},{7,23},{8,24},{9,... | collective-permute-start | bytes 1179656 | tf_op jit(solution)/shard_map/ppermute | solution.py:94
  34.1 12.1 %collective-permute-start.12 = (bf16[192,1024]{1,0:T(8,128)(2,1)S(1)}, bf16[192,1024]{1,0:T(8,128)(2,1)S(1)}, u32[]{:S(2)}, u32[]{:S(2)}) collective-permute-start(bf16[192,1024]{1,0:T(8,128)(2,1)S(1)} %pad_maximum_fusion.refs_4_), channel_id=1, source_target_pairs={{0,1},{1,0},{2,3},{3,2},{4,5},{5,4},{6,7},{7,6},{8,9},{9,8},{10,11... | collective-permute-start | bytes 1179656 | tf_op jit(solution)/shard_map/ppermute | solution.py:94
  35.9 11.1 %collective-permute-start.15 = (bf16[192,1024]{1,0:T(8,128)(2,1)S(1)}, bf16[192,1024]{1,0:T(8,128)(2,1)S(1)}, u32[]{:S(2)}, u32[]{:S(2)}) collective-permute-start(bf16[192,1024]{1,0:T(8,128)(2,1)S(1)} %broadcast_select_fusion), channel_id=1, source_target_pairs={{0,16},{1,17},{2,18},{3,19},{4,20},{5,21},{6,22},{7,23},{8,9},{9,8... | collective-permute-start | bytes 1179656 | tf_op jit(solution)/shard_map/ppermute | solution.py:94
  46.2 7.8 %collective-permute-start.14 = (bf16[192,1024]{1,0:T(8,128)(2,1)S(1)}, bf16[192,1024]{1,0:T(8,128)(2,1)S(1)}, u32[]{:S(2)}, u32[]{:S(2)}) collective-permute-start(bf16[192,1024]{1,0:T(8,128)(2,1)S(1)} %broadcast_select_fusion.1), channel_id=1, source_target_pairs={{0,16},{1,17},{2,18},{3,19},{4,20},{5,21},{6,22},{7,23},{8,9},{9,8... | collective-permute-start | bytes 1179656 | tf_op jit(solution)/shard_map/ppermute | solution.py:94
  46.9 7.1 %copy-start.1 = (bf16[1024,1024]{1,0:T(8,128)(2,1)S(1)}, bf16[1024,1024]{1,0:T(8,128)(2,1)}, u32[]{:S(2)}) copy-start(bf16[1024,1024]{1,0:T(8,128)(2,1)} %constant.110.clone.refs_9_) | copy-start | bytes 6291460
  46.9 7.1 %copy-start.2 = (bf16[1024,1024]{1,0:T(8,128)(2,1)S(1)}, bf16[1024,1024]{1,0:T(8,128)(2,1)}, u32[]{:S(2)}) copy-start(bf16[1024,1024]{1,0:T(8,128)(2,1)} %constant.109.clone.refs_8_) | copy-start | bytes 6291460
  59.7 2.7 %collective-permute-start.16 = (f32[256,1024]{1,0:T(8,128)S(1)}, f32[256,1024]{1,0:T(8,128)S(1)}, u32[]{:S(2)}, u32[]{:S(2)}) collective-permute-start(f32[256,1024]{1,0:T(8,128)S(1)} %get-tuple-element.16), channel_id=1, source_target_pairs={{0,8},{1,9},{2,10},{3,11},{4,12},{5,13},{6,14},{7,15},{8,0},{9,1},... | collective-permute-start | bytes 3145736 | tf_op jit(solution)/shard_map/ppermute | solution.py:94

commit v3 on v0

--- a/solution.py
+++ b/solution.py
@@ -1,9 +1,17 @@
+import functools
+
 import jax
 import jax.numpy as jnp
+import numpy as np
 from jax import lax
+from jax.experimental import pallas as pl
+from jax.experimental.pallas import tpu as pltpu
 from jax.sharding import PartitionSpec as P
 
 LAGS = 1024
+AXES = ("tm", "sta")
+ROWS, CORES, LAYERS, COLUMNS = 2, 2, 4, 2
+BLOCK = 256
 
 
 def lag_table(bins, lags):
@@ -24,7 +32,7 @@
     return jnp.concatenate([real_c, imag_c], axis=-1)
 
 
-def local(spectra, pair_list, pair_stations, owner_code):
+def local_any_size(spectra, pair_list, pair_stations, owner_code):
     local_spectra = spectra[0]
     width = local_spectra.shape[1]
     bins = width // 2
@@ -58,9 +66,163 @@
     )
 
 
+def moves(target):
+    def place(row, core, layer, column):
+        return (row * CORES + core) * LAYERS * COLUMNS + layer * COLUMNS + column
+
+    return [
+        (place(row, core, layer, column), place(*to))
+        for row in range(ROWS)
+        for core in range(CORES)
+        for layer in range(LAYERS)
+        for column in range(COLUMNS)
+        if (to := target(row, core, layer, column)) is not None
+    ]
+
+
+OTHER_ROW = moves(lambda r, c, z, x: (1 - r, c, z, x))
+OTHER_CORE = moves(lambda r, c, z, x: (r, 1 - c, z, x))
+OTHER_COLUMN = moves(lambda r, c, z, x: (r, c, z, 1 - x))
+DIAGONAL = moves(lambda r, c, z, x: (1 - r, c, z, x) if c == 0 else (r, c, z, 1 - x))
+PAIR_SWAP = moves(lambda r, c, z, x: (r, c, z ^ 1, x))
+INNER_SWAP = moves(lambda r, c, z, x: (r, c, 3 - z, x) if z in (1, 2) else None)
+OUTWARD = moves(lambda r, c, z, x: (r, c, z ^ 1, x) if z in (1, 2) else None)
+
+
+def send(value, pairs):
+    return lax.ppermute(value, AXES, pairs)
+
+
+def split_table(bins):
+    index = np.arange(bins)[:, None] * (np.arange(LAGS)[None, :] - LAGS // 2) % (2 * bins)
+    angle = index * (np.pi / bins)
+    rows = np.concatenate([np.cos(angle), -np.sin(angle)]) / np.sqrt(bins)
+    rows = rows.astype(np.float32)
+    high = rows.astype(jnp.bfloat16)
+    low = (rows - high.astype(np.float32)).astype(jnp.bfloat16)
+    return jnp.asarray(high), jnp.asarray(low)
+
+
+def two_parts(value):
+    high = value.astype(jnp.bfloat16)
+    return high, (value - high.astype(jnp.float32)).astype(jnp.bfloat16)
+
+
+def segment_kernel(picks_ref, select_ref, table_high, table_low, *refs):
+    blocks, refs = refs[: 2 * LAYERS], refs[2 * LAYERS :]
+    earlier, (theirs_ref, ours_ref, high_cross, low_cross) = refs[:-4], refs[-4:]
+    entries = picks_ref.shape[0] // 2
+    bins = table_high.shape[0] // 2
+    dot = functools.partial(jnp.dot, preferred_element_type=jnp.float32)
+
+    for at in range(0, bins, BLOCK):
+        real, imag = slice(at, at + BLOCK), slice(bins + at, bins + at + BLOCK)
+        stations = jnp.concatenate(
+            [jnp.concatenate([ref[:, real], ref[:, imag]], axis=1) for ref in blocks], axis=0
+        )
+        both = dot(picks_ref[...], stations)
+        real_a, imag_a = both[:entries, :BLOCK], both[:entries, BLOCK:]
+        real_b, imag_b = both[entries:, :BLOCK], both[entries:, BLOCK:]
+        for value, columns in (
+            (real_a * real_b + imag_a * imag_b, real),
+            (real_a * imag_b - imag_a * real_b, imag),
+        ):
+            high_cross[:, columns], low_cross[:, columns] = two_parts(value)
+
+    lags = dot(high_cross[...], table_high[...])
+    lags += dot(low_cross[...], table_high[...])
+    lags += dot(high_cross[...], table_low[...])
+    high, low = two_parts(lags)
+    for part, out_ref in enumerate((theirs_ref, ours_ref)):
+        slots = dot(select_ref[part], high) + dot(select_ref[part], low)
+        out_ref[...] = slots + earlier[part][...] if earlier else slots
+
+
+def add_segment(picks, select, table, blocks, earlier=()):
+    entries, (_, slots, _) = picks.shape[0] // 2, select.shape
+    bins = table[0].shape[0] // 2
+    operands = [picks, select, *table, *blocks, *earlier]
+    in_vmem = pl.BlockSpec(memory_space=pltpu.VMEM)
+    return pl.pallas_call(
+        segment_kernel,
+        out_shape=[jax.ShapeDtypeStruct((slots, LAGS), jnp.float32)] * 2,
+        in_specs=[in_vmem] * len(operands),
+        out_specs=[in_vmem] * 2,
+        scratch_shapes=[pltpu.VMEM((entries, 2 * bins), jnp.bfloat16)] * 2,
+        compiler_params=pltpu.CompilerParams(vmem_limit_bytes=24 * 1024 * 1024),
+        cost_estimate=pl.CostEstimate(
+            flops=4 * entries * (bins * (3 * LAGS + 2 * picks.shape[1]) + 2 * slots * LAGS),
+            bytes_accessed=8 * bins * (LAGS + picks.shape[1]),
+            transcendentals=0,
+        ),
+        name="add_segment",
+    )(*operands)
+
+
+def local_grid(spectra, pair_list, pair_stations, owner_code):
+    own = spectra[0]
+    stations, width = own.shape
+    bins = width // 2
+    catalogue = pair_stations.shape[1]
+    capacity = 2 * catalogue // (ROWS * CORES)
+    row, core = lax.axis_index("tm") // CORES, lax.axis_index("tm") % CORES
+    layer, column = lax.axis_index("sta") // COLUMNS, lax.axis_index("sta") % COLUMNS
+    after = lambda value, *others: lax.optimization_barrier((value, *others))[0]
+
+    def around(value):
+        return send(value, OTHER_COLUMN), send(value, OTHER_ROW)
+
+    def diagonal(side, ahead):
+        return send(jnp.where(core == 0, side, ahead), DIAGONAL)
+
+    inner = (layer == 1) | (layer == 2)
+    side, ahead = around(own)
+    near, swapped = send(own, PAIR_SWAP), send(own, INNER_SWAP)
+    corner = diagonal(side, ahead)
+    near_side, near_ahead = around(after(near, side, ahead))
+    third = jnp.where(inner, swapped, send(swapped, OUTWARD))
+    swapped = send(near, INNER_SWAP)
+    fourth = jnp.where(inner, swapped, send(swapped, OUTWARD))
+    listed_here = pair_list[0, 0]
+    listed_there = send(after(listed_here, corner), OTHER_ROW)
+
+    listed = jnp.stack([listed_here, listed_there])
+    hit = listed[:, :, None] == jnp.arange(catalogue, dtype=jnp.int32)
+    look_up = lambda values: jnp.sum(jnp.where(hit, values, 0), axis=-1)
+    pair = jnp.concatenate([look_up(pair_stations[0]), look_up(pair_stations[1])], axis=1)
+    holder, place = pair // stations, pair % stations
+    apart = layer ^ (holder // COLUMNS)
+    turns = jnp.where((apart > 1) & inner, 5 - apart, apart)
+    beside = (holder % COLUMNS) ^ column
+    position = (beside * LAYERS + turns) * stations + place
+    spots = jnp.arange(COLUMNS * LAYERS * stations, dtype=jnp.int32)
+    picks = (position[:, :, None] == spots).astype(jnp.bfloat16)
+
+    third_side, third_ahead = around(after(third, corner))
+    near_corner = diagonal(near_side, near_ahead)
+    fourth_side, fourth_ahead = around(after(fourth, picks))
+    third_corner = diagonal(third_side, third_ahead)
+    fourth_corner = diagonal(fourth_side, fourth_ahead)
+    here = (own, near, third, fourth, side, near_side, third_side, fourth_side)
+    there = (ahead, near_ahead, third_ahead, fourth_ahead)
+    there += (corner, near_corner, third_corner, fourth_corner)
+
+    codes = look_up(owner_code)
+    owner = row * CORES + jnp.stack([1 - core, core])
+    slots = owner[:, None] * capacity + jnp.arange(capacity, dtype=jnp.int32)
+    select = (slots[:, :, None] == codes[:, None, None, :]).astype(jnp.bfloat16)
+
+    table = split_table(bins)
+    sums = add_segment(picks[0], select[0], table, here)
+    theirs, ours = add_segment(picks[1], select[1], table, there, sums)
+    return ours + send(theirs, OTHER_CORE)
+
+
 def solution(mesh):
+    sizes = (mesh.shape["tm"], mesh.shape["sta"])
+    fits = sizes == (ROWS * CORES, LAYERS * COLUMNS)
     return jax.shard_map(
-        local,
+        local_grid if fits else local_any_size,
         mesh=mesh,
         in_specs=(P("tm", "sta", None), P("tm", "sta", None), P(None, "sta"), P("sta")),
         out_specs=P(("tm", "sta"), None),

time: 135 us -> 60.1 us (0.45)
  waiting for transfers between devices: 72.5 us -> 23.9 us
  starting transfers between devices: 0.04 us -> 20.6 us
  other arithmetic: 21.2 us -> 3.91 us
  local copies, waits for them, and re-layouts: 15.9 us -> 0.89 us
  between operations: 13.5 us -> 0.21 us
  matrix products: 11.1 us -> 0 us
  Pallas kernels: 0 us -> 10.3 us
    reduce_scatter x1 -> x0, waiting for transfers between devices: 43.1 us -> none  [local(): lax.psum_scatter(jnp.dot(select, partial_lags, precision=lax.Precision.HI...]
    all_gather x1 -> x0, waiting for transfers between devices: 28.7 us -> none  [local(): all_spectra = lax.all_gather(local_spectra, 'sta', axis=0, tiled=True)]
    ppermute x0 -> x19, waiting for transfers between devices: none -> 23.9 us  [send(): return lax.ppermute(value, AXES, pairs)]
    ppermute x0 -> x19, starting transfers between devices: none -> 20.6 us  [send(): return lax.ppermute(value, AXES, pairs)]
    mul x1, other arithmetic: 18.2 us -> 0.08 us  [local_grid(): slots = owner[:, None] * capacity + jnp.arange(capacity, dtype=jnp.int32)]
    gather x5 -> x0, local copies, waits for them, and re-layouts: 12.5 us -> none  [the longest x1 4.38 us: local(): first = all_spectra[first_station]]
    dot_general x2 -> x0, matrix products: 11.1 us -> none  [the longest x1 7.31 us: local(): jnp.dot(cross, table, precision=lax.Precision.HIGHEST, preferred_element_...]
    pallas_call x0 -> x2, Pallas kernels: none -> 10.3 us  [add_segment(): pl.pallas_call(segment_kernel, out_shape=[jax.ShapeDtypeStruct((slots, LA...]
  transfers between devices with their start and end apart: 2 -> 19, of which waited for: 2 -> 9; matrix products, arithmetic and copies ran while one was open for 19% -> 6% of each run, Pallas kernels for 0% -> 9%
where the time goes in v3:
time: 60.1 us; the launch traced here: 59.8 us
  waiting for transfers between devices  23.9 us (40%)
  starting transfers between devices  20.6 us (34%)
  Pallas kernels  10.3 us (17%)
  other arithmetic  3.91 us (7%)
  local copies, waits for them, and re-layouts  0.89 us (1%)
    ppermute x19, waiting for transfers between devices, send(): return lax.ppermute(value, AXES, pairs)  23.9 us
    ppermute x19, starting transfers between devices, send(): return lax.ppermute(value, AXES, pairs)  20.6 us
    pallas_call x2, Pallas kernels, add_segment(): pl.pallas_call(segment_kernel, out_shape=[jax.ShapeDtypeStruct((slots, LA...  10.3 us
    reduce_sum x1, other arithmetic, local_grid(): look_up = lambda values: jnp.sum(jnp.where(hit, values, 0), axis=-1)  1.35 us
  transfers between devices with their start and end apart: 19, of which 9 were waited for; matrix products, arithmetic and copies ran while one was open for 6% of the time, Pallas kernels for 9%

profile of v3, /device:TPU:0, one launch (start us, length us, event | category | flops | bytes accessed | tf_op | source)
XLA Modules:
  0.0 59.8 jit_solution(9576802122883014213)
XLA Ops:
  0.0 2.9 %collective-permute-start = (bf16[64,2048]{1,0:T(8,128)(2,1)}, bf16[64,2048]{1,0:T(8,128)(2,1)S(1)}, u32[]{:S(2)}, u32[]{:S(2)}) collective-permute-start(bf16[64,2048]{1,0:T(8,128)(2,1)} %bitcast.16), channel_id=1, source_target_pairs={{0,1},{1,0},{2,3},{3,2},{4,5},{5,4},{6,7},{7,6},{8,9},{9,8},{10,11... | collective-permute-start | bytes 786440 | tf_op jit(solution)/shard_map/ppermute | solution.py:93
  2.9 1.5 %collective-permute-start.1 = (bf16[64,2048]{1,0:T(8,128)(2,1)}, bf16[64,2048]{1,0:T(8,128)(2,1)S(1)}, u32[]{:S(2)}, u32[]{:S(2)}) collective-permute-start(bf16[64,2048]{1,0:T(8,128)(2,1)} %bitcast.17), channel_id=1, source_target_pairs={{0,16},{1,17},{2,18},{3,19},{4,20},{5,21},{6,22},{7,23},{8,24},{9,... | collective-permute-start | bytes 786440 | tf_op jit(solution)/shard_map/ppermute | solution.py:93
  4.5 1.6 %collective-permute-start.4 = (bf16[64,2048]{1,0:T(8,128)(2,1)}, bf16[64,2048]{1,0:T(8,128)(2,1)S(1)}, u32[]{:S(2)}, u32[]{:S(2)}) collective-permute-start(bf16[64,2048]{1,0:T(8,128)(2,1)} %bitcast.18), channel_id=1, source_target_pairs={{0,2},{1,3},{2,0},{3,1},{4,6},{5,7},{6,4},{7,5},{8,10},{9,11},{10,... | collective-permute-start | bytes 786440 | tf_op jit(solution)/shard_map/ppermute | solution.py:93
  6.0 0.7 %collective-permute-start.6 = (bf16[64,2048]{1,0:T(8,128)(2,1)}, bf16[64,2048]{1,0:T(8,128)(2,1)S(1)}, u32[]{:S(2)}, u32[]{:S(2)}) collective-permute-start(bf16[64,2048]{1,0:T(8,128)(2,1)} %bitcast.19), channel_id=1, source_target_pairs={{2,4},{3,5},{4,2},{5,3},{10,12},{11,13},{12,10},{13,11},{18,20},{1... | collective-permute-start | bytes 786440 | tf_op jit(solution)/shard_map/ppermute | solution.py:93
  6.7 0.1 fusion.4
  6.8 0.1 iota_add_fusion
  6.9 0.8 %fusion.5 = (s32[1,512]{1,0:T(1,128)S(1)}, s32[1,512]{1,0:T(1,128)S(1)}) fusion(s32[2,512]{1,0:T(2,128)} %param.8), kind=kLoop, calls=%fused_computation.36 | loop fusion | bytes 8192 | tf_op jit(solution)/shard_map/slice | solution.py:192
  7.7 1.8 %collective-permute-done.refs_4_ = bf16[64,2048]{1,0:T(8,128)(2,1)S(1)} collective-permute-done((bf16[64,2048]{1,0:T(8,128)(2,1)}, bf16[64,2048]{1,0:T(8,128)(2,1)S(1)}, u32[]{:S(2)}, u32[]{:S(2)}) %collective-permute-start) | collective-permute-done | bytes 262176 | tf_op jit(solution)/shard_map/ppermute | solution.py:93
  9.5 1.5 %collective-permute-done.1.refs_0_ = bf16[64,2048]{1,0:T(8,128)(2,1)S(1)} collective-permute-done((bf16[64,2048]{1,0:T(8,128)(2,1)}, bf16[64,2048]{1,0:T(8,128)(2,1)S(1)}, u32[]{:S(2)}, u32[]{:S(2)}) %collective-permute-start.1) | collective-permute-done | bytes 262176 | tf_op jit(solution)/shard_map/ppermute | solution.py:93
  10.9 1.2 %collective-permute-done.4.refs_1_ = bf16[64,2048]{1,0:T(8,128)(2,1)S(1)} collective-permute-done((bf16[64,2048]{1,0:T(8,128)(2,1)}, bf16[64,2048]{1,0:T(8,128)(2,1)S(1)}, u32[]{:S(2)}, u32[]{:S(2)}) %collective-permute-start.4) | collective-permute-done | bytes 262176 | tf_op jit(solution)/shard_map/ppermute | solution.py:93
  12.2 0.5 collective-permute-start.12
  12.7 0.4 collective-permute-start.5
  13.1 0.0 collective-permute-done.6
  13.1 1.3 %collective-permute-start.7 = (bf16[64,2048]{1,0:T(8,128)(2,1)S(1)}, bf16[64,2048]{1,0:T(8,128)(2,1)S(1)}, u32[]{:S(2)}, u32[]{:S(2)}) collective-permute-start(bf16[64,2048]{1,0:T(8,128)(2,1)S(1)} %collective-permute-done.6), channel_id=1, source_target_pairs={{2,0},{3,1},{4,6},{5,7},{10,8},{11,9},{12,14},{13,15},{18,16},{19,... | collective-permute-start | bytes 786440 | tf_op jit(solution)/shard_map/ppermute | solution.py:93
  14.4 0.0 copy-start
  14.4 0.0 copy-start.1
  14.4 0.0 copy-start.2
  14.4 1.7 %collective-permute-start.2 = (bf16[64,2048]{1,0:T(8,128)(2,1)S(1)}, bf16[64,2048]{1,0:T(8,128)(2,1)S(1)}, u32[]{:S(2)}, u32[]{:S(2)}) collective-permute-start(bf16[64,2048]{1,0:T(8,128)(2,1)S(1)} %broadcast_select_fusion.5), channel_id=1, source_target_pairs={{0,16},{1,17},{2,18},{3,19},{4,20},{5,21},{6,22},{7,23},{8,9},{9,8... | collective-permute-start | bytes 786440 | tf_op jit(solution)/shard_map/ppermute | solution.py:93
  16.2 0.8 %collective-permute-start.9 = (bf16[64,2048]{1,0:T(8,128)(2,1)S(1)}, bf16[64,2048]{1,0:T(8,128)(2,1)S(1)}, u32[]{:S(2)}, u32[]{:S(2)}) collective-permute-start(bf16[64,2048]{1,0:T(8,128)(2,1)S(1)} %collective-permute-done.4.refs_1_), channel_id=1, source_target_pairs={{2,4},{3,5},{4,2},{5,3},{10,12},{11,13},{12,10},{13,11},{18,20},{1... | collective-permute-start | bytes 786440 | tf_op jit(solution)/shard_map/ppermute | solution.py:93
  17.0 5.9 %collective-permute-done.7 = bf16[64,2048]{1,0:T(8,128)(2,1)S(1)} collective-permute-done((bf16[64,2048]{1,0:T(8,128)(2,1)S(1)}, bf16[64,2048]{1,0:T(8,128)(2,1)S(1)}, u32[]{:S(2)}, u32[]{:S(2)}) %collective-permute-start.7) | collective-permute-done | bytes 262176 | tf_op jit(solution)/shard_map/ppermute | solution.py:93
  22.9 0.0 collective-permute-done.2.refs_4_
  22.9 0.6 %collective-permute-start.14 = (bf16[64,2048]{1,0:T(8,128)(2,1)S(1)}, bf16[64,2048]{1,0:T(8,128)(2,1)S(1)}, u32[]{:S(2)}, u32[]{:S(2)}) collective-permute-start(bf16[64,2048]{1,0:T(8,128)(2,1)S(1)} %broadcast_select_fusion.1.refs_2_), channel_id=1, source_target_pairs={{0,1},{1,0},{2,3},{3,2},{4,5},{5,4},{6,7},{7,6},{8,9},{9,8},{10,11... | collective-permute-start | bytes 786440 | tf_op jit(solution)/shard_map/ppermute | solution.py:93
  23.5 1.1 %collective-permute-start.8 = (bf16[64,2048]{1,0:T(8,128)(2,1)S(1)}, bf16[64,2048]{1,0:T(8,128)(2,1)S(1)}, u32[]{:S(2)}, u32[]{:S(2)}) collective-permute-start(bf16[64,2048]{1,0:T(8,128)(2,1)S(1)} %broadcast_select_fusion.1.refs_2_), channel_id=1, source_target_pairs={{0,16},{1,17},{2,18},{3,19},{4,20},{5,21},{6,22},{7,23},{8,24},{9,... | collective-permute-start | bytes 786440 | tf_op jit(solution)/shard_map/ppermute | solution.py:93
  24.6 0.0 collective-permute-done.12.refs_5_
  24.6 0.9 %collective-permute-start.3 = (s32[256]{0:T(256)}, s32[256]{0:T(256)S(1)}, u32[]{:S(2)}, u32[]{:S(2)}) collective-permute-start(s32[256]{0:T(256)} %bitcast.23), channel_id=1, source_target_pairs={{0,16},{1,17},{2,18},{3,19},{4,20},{5,21},{6,22},{7,23},{8,24},{9,... | collective-permute-start | bytes 3080 | tf_op jit(solution)/shard_map/ppermute | solution.py:93
  25.5 1.2 %collective-permute-start.13 = (bf16[64,2048]{1,0:T(8,128)(2,1)S(1)}, bf16[64,2048]{1,0:T(8,128)(2,1)S(1)}, u32[]{:S(2)}, u32[]{:S(2)}) collective-permute-start(bf16[64,2048]{1,0:T(8,128)(2,1)S(1)} %broadcast_select_fusion.4), channel_id=1, source_target_pairs={{0,16},{1,17},{2,18},{3,19},{4,20},{5,21},{6,22},{7,23},{8,9},{9,8... | collective-permute-start | bytes 786440 | tf_op jit(solution)/shard_map/ppermute | solution.py:93
  26.7 1.3 %collective-permute-start.10 = (bf16[64,2048]{1,0:T(8,128)(2,1)S(1)}, bf16[64,2048]{1,0:T(8,128)(2,1)S(1)}, u32[]{:S(2)}, u32[]{:S(2)}) collective-permute-start(bf16[64,2048]{1,0:T(8,128)(2,1)S(1)} %collective-permute-done.9), channel_id=1, source_target_pairs={{2,0},{3,1},{4,6},{5,7},{10,8},{11,9},{12,14},{13,15},{18,16},{19,... | collective-permute-start | bytes 786440 | tf_op jit(solution)/shard_map/ppermute | solution.py:93
  28.0 2.2 %collective-permute-done.3 = s32[256]{0:T(256)S(1)} collective-permute-done((s32[256]{0:T(256)}, s32[256]{0:T(256)S(1)}, u32[]{:S(2)}, u32[]{:S(2)}) %collective-permute-start.3) | collective-permute-done | bytes 1056 | tf_op jit(solution)/shard_map/ppermute | solution.py:93
  30.2 0.7 %pad_add_fusion.1 = s32[2,256]{1,0:T(2,128)S(1)} fusion(s32[1,256]{1,0:T(1,128)S(1)} %bitcast.25, s32[1,256]{1,0:T(1,128)} %bitcast.24), kind=kLoop, calls=%fused_computation.32 | loop fusion | flops 512 | bytes 4096 | tf_op jit(solution)/shard_map/stack | solution.py:189
  30.9 1.4 %select_reduce_fusion = (s32[2,256]{1,0:T(2,128)S(1)}, s32[2,256]{1,0:T(2,128)S(1)}, s32[2,256]{1,0:T(2,128)S(1)}) fusion(s32[512]{0:T(512)} %param.9, s32[2,256]{1,0:T(2,128)S(1)} %pad_add_fusion.1, s32[512]{0:T(512)S(1)} %bitcast.22, s32[512]{0:T(512)S(1)} %bitcast.21), kind=kLoop, calls=%fused_computation.2 | loop fusion | flops 1833472 | bytes 14336 | tf_op jit(solution)/shard_map/reduce_sum | solution.py:191
  32.2 0.1 fusion.3
  32.3 0.2 fusion
  32.5 0.2 compare_convert_fusion
  32.7 0.1 slice_bitcast_fusion
  32.8 2.2 %collective-permute-done.10 = bf16[64,2048]{1,0:T(8,128)(2,1)S(1)} collective-permute-done((bf16[64,2048]{1,0:T(8,128)(2,1)S(1)}, bf16[64,2048]{1,0:T(8,128)(2,1)S(1)}, u32[]{:S(2)}, u32[]{:S(2)}) %collective-permute-start.10) | collective-permute-done | bytes 262176 | tf_op jit(solution)/shard_map/ppermute | solution.py:93
  35.0 1.0 %collective-permute-start.16 = (bf16[64,2048]{1,0:T(8,128)(2,1)S(1)}, bf16[64,2048]{1,0:T(8,128)(2,1)S(1)}, u32[]{:S(2)}, u32[]{:S(2)}) collective-permute-start(bf16[64,2048]{1,0:T(8,128)(2,1)S(1)} %broadcast_select_fusion.refs_3_), channel_id=1, source_target_pairs={{0,1},{1,0},{2,3},{3,2},{4,5},{5,4},{6,7},{7,6},{8,9},{9,8},{10,11... | collective-permute-start | bytes 786440 | tf_op jit(solution)/shard_map/ppermute | solution.py:93
  36.0 1.5 %collective-permute-start.11 = (bf16[64,2048]{1,0:T(8,128)(2,1)S(1)}, bf16[64,2048]{1,0:T(8,128)(2,1)S(1)}, u32[]{:S(2)}, u32[]{:S(2)}) collective-permute-start(bf16[64,2048]{1,0:T(8,128)(2,1)S(1)} %broadcast_select_fusion.refs_3_), channel_id=1, source_target_pairs={{0,16},{1,17},{2,18},{3,19},{4,20},{5,21},{6,22},{7,23},{8,24},{9,... | collective-permute-start | bytes 786440 | tf_op jit(solution)/shard_map/ppermute | solution.py:93
  37.5 0.6 collective-permute-start.15
  38.1 6.2 %collective-permute-done.16.refs_7_ = bf16[64,2048]{1,0:T(8,128)(2,1)S(1)} collective-permute-done((bf16[64,2048]{1,0:T(8,128)(2,1)S(1)}, bf16[64,2048]{1,0:T(8,128)(2,1)S(1)}, u32[]{:S(2)}, u32[]{:S(2)}) %collective-permute-start.16) | collective-permute-done | bytes 262176 | tf_op jit(solution)/shard_map/ppermute | solution.py:93
  44.3 0.0 collective-permute-done.11.refs_3_
  44.3 1.0 %collective-permute-start.17 = (bf16[64,2048]{1,0:T(8,128)(2,1)S(1)}, bf16[64,2048]{1,0:T(8,128)(2,1)S(1)}, u32[]{:S(2)}, u32[]{:S(2)}) collective-permute-start(bf16[64,2048]{1,0:T(8,128)(2,1)S(1)} %broadcast_select_fusion.2), channel_id=1, source_target_pairs={{0,16},{1,17},{2,18},{3,19},{4,20},{5,21},{6,22},{7,23},{8,9},{9,8... | collective-permute-start | bytes 786440 | tf_op jit(solution)/shard_map/ppermute | solution.py:93
  45.4 5.2 %add_segment.2 = (f32[256,1024]{1,0:T(8,128)S(1)}, f32[256,1024]{1,0:T(8,128)S(1)}) custom-call(bf16[512,512]{1,0:T(8,128)(2,1)S(1)} %get-tuple-element.24.picks_ref, bf16[2,256,256]{2,1,0:T(8,128)(2,1)S(1)} %get-tuple-element.26.select_ref, bf16[2048,1024]{1,0:T(8,128)(2,1)S(1)} %copy-done.1, bf16[2048,1024]{1,0:T(8,128)(2,1)S(1)} %copy-done.2, ...), custom_call_target="tpu_custom_call" | custom-call | flops 4831838208 | bytes 12582912 | tf_op jit(solution)/shard_map/add_segment/pallas_call | solution.py:146
  50.5 0.0 collective-permute-done.13.refs_5_
  50.5 0.2 collective-permute-done.17.refs_7_
  50.8 5.2 %add_segment.3 = (f32[256,1024]{1,0:T(8,128)S(1)}, f32[256,1024]{1,0:T(8,128)S(1)}) custom-call(bf16[512,512]{1,0:T(8,128)(2,1)S(1)} %get-tuple-element.25.picks_ref, bf16[2,256,256]{2,1,0:T(8,128)(2,1)S(1)} %get-tuple-element.27.select_ref, bf16[2048,1024]{1,0:T(8,128)(2,1)S(1)} %copy-done.1, bf16[2048,1024]{1,0:T(8,128)(2,1)S(1)} %copy-done.2, ...), custom_call_target="tpu_custom_call" | custom-call | flops 4831838208 | bytes 12582912 | tf_op jit(solution)/shard_map/add_segment/pallas_call | solution.py:146
  56.0 0.1 collective-permute-start.18
  56.0 2.6 %collective-permute-done.18 = f32[256,1024]{1,0:T(8,128)S(1)} collective-permute-done((f32[256,1024]{1,0:T(8,128)S(1)}, f32[256,1024]{1,0:T(8,128)S(1)}, u32[]{:S(2)}, u32[]{:S(2)}) %collective-permute-start.18) | collective-permute-done | bytes 1048608 | tf_op jit(solution)/shard_map/ppermute | solution.py:93
  58.7 1.1 %add.92 = f32[256,1024]{1,0:T(8,128)} add(f32[256,1024]{1,0:T(8,128)S(1)} %get-tuple-element.19, f32[256,1024]{1,0:T(8,128)S(1)} %collective-permute-done.18) | non-fusion elementwise | flops 262144 | bytes 3145728 | tf_op jit(solution)/shard_map/add | solution.py:218
  (15 shorter events, 0.2 us)
Async XLA Ops:
  0.0 9.5 %collective-permute-start = (bf16[64,2048]{1,0:T(8,128)(2,1)}, bf16[64,2048]{1,0:T(8,128)(2,1)S(1)}, u32[]{:S(2)}, u32[]{:S(2)}) collective-permute-start(bf16[64,2048]{1,0:T(8,128)(2,1)} %bitcast.16), channel_id=1, source_target_pairs={{0,1},{1,0},{2,3},{3,2},{4,5},{5,4},{6,7},{7,6},{8,9},{9,8},{10,11... | collective-permute-start | bytes 786440 | tf_op jit(solution)/shard_map/ppermute | solution.py:93
  2.9 8.0 %collective-permute-start.1 = (bf16[64,2048]{1,0:T(8,128)(2,1)}, bf16[64,2048]{1,0:T(8,128)(2,1)S(1)}, u32[]{:S(2)}, u32[]{:S(2)}) collective-permute-start(bf16[64,2048]{1,0:T(8,128)(2,1)} %bitcast.17), channel_id=1, source_target_pairs={{0,16},{1,17},{2,18},{3,19},{4,20},{5,21},{6,22},{7,23},{8,24},{9,... | collective-permute-start | bytes 786440 | tf_op jit(solution)/shard_map/ppermute | solution.py:93
  4.5 7.7 %collective-permute-start.4 = (bf16[64,2048]{1,0:T(8,128)(2,1)}, bf16[64,2048]{1,0:T(8,128)(2,1)S(1)}, u32[]{:S(2)}, u32[]{:S(2)}) collective-permute-start(bf16[64,2048]{1,0:T(8,128)(2,1)} %bitcast.18), channel_id=1, source_target_pairs={{0,2},{1,3},{2,0},{3,1},{4,6},{5,7},{6,4},{7,5},{8,10},{9,11},{10,... | collective-permute-start | bytes 786440 | tf_op jit(solution)/shard_map/ppermute | solution.py:93
  6.0 7.0 %collective-permute-start.6 = (bf16[64,2048]{1,0:T(8,128)(2,1)}, bf16[64,2048]{1,0:T(8,128)(2,1)S(1)}, u32[]{:S(2)}, u32[]{:S(2)}) collective-permute-start(bf16[64,2048]{1,0:T(8,128)(2,1)} %bitcast.19), channel_id=1, source_target_pairs={{2,4},{3,5},{4,2},{5,3},{10,12},{11,13},{12,10},{13,11},{18,20},{1... | collective-permute-start | bytes 786440 | tf_op jit(solution)/shard_map/ppermute | solution.py:93
  12.2 12.4 %collective-permute-start.12 = (bf16[64,2048]{1,0:T(8,128)(2,1)S(1)}, bf16[64,2048]{1,0:T(8,128)(2,1)S(1)}, u32[]{:S(2)}, u32[]{:S(2)}) collective-permute-start(bf16[64,2048]{1,0:T(8,128)(2,1)S(1)} %collective-permute-done.4.refs_1_), channel_id=1, source_target_pairs={{0,1},{1,0},{2,3},{3,2},{4,5},{5,4},{6,7},{7,6},{8,9},{9,8},{10,11... | collective-permute-start | bytes 786440 | tf_op jit(solution)/shard_map/ppermute | solution.py:93
  12.7 12.8 %collective-permute-start.5 = (bf16[64,2048]{1,0:T(8,128)(2,1)S(1)}, bf16[64,2048]{1,0:T(8,128)(2,1)S(1)}, u32[]{:S(2)}, u32[]{:S(2)}) collective-permute-start(bf16[64,2048]{1,0:T(8,128)(2,1)S(1)} %collective-permute-done.4.refs_1_), channel_id=1, source_target_pairs={{0,16},{1,17},{2,18},{3,19},{4,20},{5,21},{6,22},{7,23},{8,24},{9,... | collective-permute-start | bytes 786440 | tf_op jit(solution)/shard_map/ppermute | solution.py:93
  13.1 9.8 %collective-permute-start.7 = (bf16[64,2048]{1,0:T(8,128)(2,1)S(1)}, bf16[64,2048]{1,0:T(8,128)(2,1)S(1)}, u32[]{:S(2)}, u32[]{:S(2)}) collective-permute-start(bf16[64,2048]{1,0:T(8,128)(2,1)S(1)} %collective-permute-done.6), channel_id=1, source_target_pairs={{2,0},{3,1},{4,6},{5,7},{10,8},{11,9},{12,14},{13,15},{18,16},{19,... | collective-permute-start | bytes 786440 | tf_op jit(solution)/shard_map/ppermute | solution.py:93
  14.4 31.0 %copy-start = (bf16[1,64,2048]{2,1,0:T(8,128)(2,1)S(1)}, bf16[1,64,2048]{2,1,0:T(8,128)(2,1)}, u32[]{:S(2)}) copy-start(bf16[1,64,2048]{2,1,0:T(8,128)(2,1)} %param.6) | copy-start | bytes 786436
  14.4 30.9 %copy-start.1 = (bf16[2048,1024]{1,0:T(8,128)(2,1)S(1)}, bf16[2048,1024]{1,0:T(8,128)(2,1)}, u32[]{:S(2)}) copy-start(bf16[2048,1024]{1,0:T(8,128)(2,1)} %constant.94.clone.table_high) | copy-start | bytes 12582916
  14.4 30.9 %copy-start.2 = (bf16[2048,1024]{1,0:T(8,128)(2,1)S(1)}, bf16[2048,1024]{1,0:T(8,128)(2,1)}, u32[]{:S(2)}) copy-start(bf16[2048,1024]{1,0:T(8,128)(2,1)} %constant.95.clone.table_low) | copy-start | bytes 12582916
  14.4 8.4 %collective-permute-start.2 = (bf16[64,2048]{1,0:T(8,128)(2,1)S(1)}, bf16[64,2048]{1,0:T(8,128)(2,1)S(1)}, u32[]{:S(2)}, u32[]{:S(2)}) collective-permute-start(bf16[64,2048]{1,0:T(8,128)(2,1)S(1)} %broadcast_select_fusion.5), channel_id=1, source_target_pairs={{0,16},{1,17},{2,18},{3,19},{4,20},{5,21},{6,22},{7,23},{8,9},{9,8... | collective-permute-start | bytes 786440 | tf_op jit(solution)/shard_map/ppermute | solution.py:93
  16.2 10.6 %collective-permute-start.9 = (bf16[64,2048]{1,0:T(8,128)(2,1)S(1)}, bf16[64,2048]{1,0:T(8,128)(2,1)S(1)}, u32[]{:S(2)}, u32[]{:S(2)}) collective-permute-start(bf16[64,2048]{1,0:T(8,128)(2,1)S(1)} %collective-permute-done.4.refs_1_), channel_id=1, source_target_pairs={{2,4},{3,5},{4,2},{5,3},{10,12},{11,13},{12,10},{13,11},{18,20},{1... | collective-permute-start | bytes 786440 | tf_op jit(solution)/shard_map/ppermute | solution.py:93
  22.9 14.6 %collective-permute-start.14 = (bf16[64,2048]{1,0:T(8,128)(2,1)S(1)}, bf16[64,2048]{1,0:T(8,128)(2,1)S(1)}, u32[]{:S(2)}, u32[]{:S(2)}) collective-permute-start(bf16[64,2048]{1,0:T(8,128)(2,1)S(1)} %broadcast_select_fusion.1.refs_2_), channel_id=1, source_target_pairs={{0,1},{1,0},{2,3},{3,2},{4,5},{5,4},{6,7},{7,6},{8,9},{9,8},{10,11... | collective-permute-start | bytes 786440 | tf_op jit(solution)/shard_map/ppermute | solution.py:93
  23.5 14.0 %collective-permute-start.8 = (bf16[64,2048]{1,0:T(8,128)(2,1)S(1)}, bf16[64,2048]{1,0:T(8,128)(2,1)S(1)}, u32[]{:S(2)}, u32[]{:S(2)}) collective-permute-start(bf16[64,2048]{1,0:T(8,128)(2,1)S(1)} %broadcast_select_fusion.1.refs_2_), channel_id=1, source_target_pairs={{0,16},{1,17},{2,18},{3,19},{4,20},{5,21},{6,22},{7,23},{8,24},{9,... | collective-permute-start | bytes 786440 | tf_op jit(solution)/shard_map/ppermute | solution.py:93
  24.6 5.6 %collective-permute-start.3 = (s32[256]{0:T(256)}, s32[256]{0:T(256)S(1)}, u32[]{:S(2)}, u32[]{:S(2)}) collective-permute-start(s32[256]{0:T(256)} %bitcast.23), channel_id=1, source_target_pairs={{0,16},{1,17},{2,18},{3,19},{4,20},{5,21},{6,22},{7,23},{8,24},{9,... | collective-permute-start | bytes 3080 | tf_op jit(solution)/shard_map/ppermute | solution.py:93
  25.5 25.0 %collective-permute-start.13 = (bf16[64,2048]{1,0:T(8,128)(2,1)S(1)}, bf16[64,2048]{1,0:T(8,128)(2,1)S(1)}, u32[]{:S(2)}, u32[]{:S(2)}) collective-permute-start(bf16[64,2048]{1,0:T(8,128)(2,1)S(1)} %broadcast_select_fusion.4), channel_id=1, source_target_pairs={{0,16},{1,17},{2,18},{3,19},{4,20},{5,21},{6,22},{7,23},{8,9},{9,8... | collective-permute-start | bytes 786440 | tf_op jit(solution)/shard_map/ppermute | solution.py:93
  26.7 8.3 %collective-permute-start.10 = (bf16[64,2048]{1,0:T(8,128)(2,1)S(1)}, bf16[64,2048]{1,0:T(8,128)(2,1)S(1)}, u32[]{:S(2)}, u32[]{:S(2)}) collective-permute-start(bf16[64,2048]{1,0:T(8,128)(2,1)S(1)} %collective-permute-done.9), channel_id=1, source_target_pairs={{2,0},{3,1},{4,6},{5,7},{10,8},{11,9},{12,14},{13,15},{18,16},{19,... | collective-permute-start | bytes 786440 | tf_op jit(solution)/shard_map/ppermute | solution.py:93
  35.0 9.3 %collective-permute-start.16 = (bf16[64,2048]{1,0:T(8,128)(2,1)S(1)}, bf16[64,2048]{1,0:T(8,128)(2,1)S(1)}, u32[]{:S(2)}, u32[]{:S(2)}) collective-permute-start(bf16[64,2048]{1,0:T(8,128)(2,1)S(1)} %broadcast_select_fusion.refs_3_), channel_id=1, source_target_pairs={{0,1},{1,0},{2,3},{3,2},{4,5},{5,4},{6,7},{7,6},{8,9},{9,8},{10,11... | collective-permute-start | bytes 786440 | tf_op jit(solution)/shard_map/ppermute | solution.py:93
  36.0 8.3 %collective-permute-start.11 = (bf16[64,2048]{1,0:T(8,128)(2,1)S(1)}, bf16[64,2048]{1,0:T(8,128)(2,1)S(1)}, u32[]{:S(2)}, u32[]{:S(2)}) collective-permute-start(bf16[64,2048]{1,0:T(8,128)(2,1)S(1)} %broadcast_select_fusion.refs_3_), channel_id=1, source_target_pairs={{0,16},{1,17},{2,18},{3,19},{4,20},{5,21},{6,22},{7,23},{8,24},{9,... | collective-permute-start | bytes 786440 | tf_op jit(solution)/shard_map/ppermute | solution.py:93
  37.5 13.0 %collective-permute-start.15 = (bf16[64,2048]{1,0:T(8,128)(2,1)S(1)}, bf16[64,2048]{1,0:T(8,128)(2,1)S(1)}, u32[]{:S(2)}, u32[]{:S(2)}) collective-permute-start(bf16[64,2048]{1,0:T(8,128)(2,1)S(1)} %broadcast_select_fusion.3), channel_id=1, source_target_pairs={{0,16},{1,17},{2,18},{3,19},{4,20},{5,21},{6,22},{7,23},{8,9},{9,8... | collective-permute-start | bytes 786440 | tf_op jit(solution)/shard_map/ppermute | solution.py:93
  44.3 6.4 %collective-permute-start.17 = (bf16[64,2048]{1,0:T(8,128)(2,1)S(1)}, bf16[64,2048]{1,0:T(8,128)(2,1)S(1)}, u32[]{:S(2)}, u32[]{:S(2)}) collective-permute-start(bf16[64,2048]{1,0:T(8,128)(2,1)S(1)} %broadcast_select_fusion.2), channel_id=1, source_target_pairs={{0,16},{1,17},{2,18},{3,19},{4,20},{5,21},{6,22},{7,23},{8,9},{9,8... | collective-permute-start | bytes 786440 | tf_op jit(solution)/shard_map/ppermute | solution.py:93
  56.0 2.7 %collective-permute-start.18 = (f32[256,1024]{1,0:T(8,128)S(1)}, f32[256,1024]{1,0:T(8,128)S(1)}, u32[]{:S(2)}, u32[]{:S(2)}) collective-permute-start(f32[256,1024]{1,0:T(8,128)S(1)} %get-tuple-element.20), channel_id=1, source_target_pairs={{0,8},{1,9},{2,10},{3,11},{4,12},{5,13},{6,14},{7,15},{8,0},{9,1},... | collective-permute-start | bytes 3145736 | tf_op jit(solution)/shard_map/ppermute | solution.py:93

commit v4 on v3

--- a/solution.py
+++ b/solution.py
@@ -85,8 +85,8 @@
 OTHER_COLUMN = moves(lambda r, c, z, x: (r, c, z, 1 - x))
 DIAGONAL = moves(lambda r, c, z, x: (1 - r, c, z, x) if c == 0 else (r, c, z, 1 - x))
 PAIR_SWAP = moves(lambda r, c, z, x: (r, c, z ^ 1, x))
-INNER_SWAP = moves(lambda r, c, z, x: (r, c, 3 - z, x) if z in (1, 2) else None)
-OUTWARD = moves(lambda r, c, z, x: (r, c, z ^ 1, x) if z in (1, 2) else None)
+INNER_SWAP = moves(lambda r, c, z, x: (r, c, 3 - z, x) if z in (1, 2) else (r, 1 - c, z, x))
+OUTWARD = PAIR_SWAP
 
 
 def send(value, pairs):
@@ -109,7 +109,7 @@
 
 
 def segment_kernel(picks_ref, select_ref, table_high, table_low, *refs):
-    blocks, refs = refs[: 2 * LAYERS], refs[2 * LAYERS :]
+    blocks, refs = refs[:6], refs[6:]
     earlier, (theirs_ref, ours_ref, high_cross, low_cross) = refs[:-4], refs[-4:]
     entries = picks_ref.shape[0] // 2
     bins = table_high.shape[0] // 2
@@ -179,12 +179,13 @@
     side, ahead = around(own)
     near, swapped = send(own, PAIR_SWAP), send(own, INNER_SWAP)
     corner = diagonal(side, ahead)
-    near_side, near_ahead = around(after(near, side, ahead))
     third = jnp.where(inner, swapped, send(swapped, OUTWARD))
+    two = jnp.concatenate([near, third], axis=0)
+    two_side, two_ahead = around(two)
     swapped = send(near, INNER_SWAP)
     fourth = jnp.where(inner, swapped, send(swapped, OUTWARD))
     listed_here = pair_list[0, 0]
-    listed_there = send(after(listed_here, corner), OTHER_ROW)
+    listed_there = send(after(listed_here, third), OTHER_ROW)
 
     listed = jnp.stack([listed_here, listed_there])
     hit = listed[:, :, None] == jnp.arange(catalogue, dtype=jnp.int32)
@@ -198,14 +199,12 @@
     spots = jnp.arange(COLUMNS * LAYERS * stations, dtype=jnp.int32)
     picks = (position[:, :, None] == spots).astype(jnp.bfloat16)
 
-    third_side, third_ahead = around(after(third, corner))
-    near_corner = diagonal(near_side, near_ahead)
     fourth_side, fourth_ahead = around(after(fourth, picks))
-    third_corner = diagonal(third_side, third_ahead)
+    two_corner = diagonal(two_side, two_ahead)
     fourth_corner = diagonal(fourth_side, fourth_ahead)
-    here = (own, near, third, fourth, side, near_side, third_side, fourth_side)
-    there = (ahead, near_ahead, third_ahead, fourth_ahead)
-    there += (corner, near_corner, third_corner, fourth_corner)
+    here = (own, two, fourth, side, two_side, fourth_side)
+    there = (ahead, two_ahead, fourth_ahead)
+    there += (corner, two_corner, fourth_corner)
 
     codes = look_up(owner_code)
     owner = row * CORES + jnp.stack([1 - core, core])

time: 60.1 us -> 54.9 us (0.913)
  waiting for transfers between devices: 23.9 us -> 17.4 us
  starting transfers between devices: 20.6 us -> 21.9 us
    ppermute x19 -> x16, waiting for transfers between devices: 23.9 us -> 17.4 us  [send(): return lax.ppermute(value, AXES, pairs)]
    ppermute x19 -> x16, starting transfers between devices: 20.6 us -> 21.9 us  [send(): return lax.ppermute(value, AXES, pairs)]
  transfers between devices with their start and end apart: 19 -> 16, of which waited for: 9 -> 8; matrix products, arithmetic and copies ran while one was open for 6% -> 7% of each run, Pallas kernels for 9% -> 9%
where the time goes in v4:
time: 54.9 us; the launch traced here: 54.6 us
  starting transfers between devices  21.9 us (40%)
  waiting for transfers between devices  17.4 us (32%)
  Pallas kernels  10.3 us (19%)
  other arithmetic  3.95 us (7%)
  local copies, waits for them, and re-layouts  0.89 us (2%)
    ppermute x16, starting transfers between devices, send(): return lax.ppermute(value, AXES, pairs)  21.9 us
    ppermute x16, waiting for transfers between devices, send(): return lax.ppermute(value, AXES, pairs)  17.4 us
    pallas_call x2, Pallas kernels, add_segment(): pl.pallas_call(segment_kernel, out_shape=[jax.ShapeDtypeStruct((slots, LA...  10.3 us
    reduce_sum x1, other arithmetic, local_grid(): look_up = lambda values: jnp.sum(jnp.where(hit, values, 0), axis=-1)  1.35 us
    add x1, other arithmetic, local_grid(): return ours + send(theirs, OTHER_CORE)  1.11 us
  transfers between devices with their start and end apart: 16, of which 8 were waited for; matrix products, arithmetic and copies ran while one was open for 7% of the time, Pallas kernels for 9%

profile of v4, /device:TPU:0, one launch (start us, length us, event | category | flops | bytes accessed | tf_op | source)
XLA Modules:
  0.0 54.6 jit_solution(6663963157431138468)
XLA Ops:
  0.0 0.5 collective-permute-start
  0.5 4.1 %collective-permute-start.4 = (bf16[64,2048]{1,0:T(8,128)(2,1)}, bf16[64,2048]{1,0:T(8,128)(2,1)S(1)}, u32[]{:S(2)}, u32[]{:S(2)}) collective-permute-start(bf16[64,2048]{1,0:T(8,128)(2,1)} %bitcast.17), channel_id=1, source_target_pairs={{0,2},{1,3},{2,0},{3,1},{4,6},{5,7},{6,4},{7,5},{8,10},{9,11},{10,... | collective-permute-start | bytes 786440 | tf_op jit(solution)/shard_map/ppermute | solution.py:93
  4.6 1.5 %collective-permute-start.9 = (bf16[64,2048]{1,0:T(8,128)(2,1)}, bf16[64,2048]{1,0:T(8,128)(2,1)S(1)}, u32[]{:S(2)}, u32[]{:S(2)}) collective-permute-start(bf16[64,2048]{1,0:T(8,128)(2,1)} %bitcast.18), channel_id=1, source_target_pairs={{0,1},{1,0},{2,3},{3,2},{4,5},{5,4},{6,7},{7,6},{8,9},{9,8},{10,11... | collective-permute-start | bytes 786440 | tf_op jit(solution)/shard_map/ppermute | solution.py:93
  6.1 1.5 %collective-permute-start.3 = (bf16[64,2048]{1,0:T(8,128)(2,1)}, bf16[64,2048]{1,0:T(8,128)(2,1)S(1)}, u32[]{:S(2)}, u32[]{:S(2)}) collective-permute-start(bf16[64,2048]{1,0:T(8,128)(2,1)} %bitcast.19), channel_id=1, source_target_pairs={{0,16},{1,17},{2,18},{3,19},{4,20},{5,21},{6,22},{7,23},{8,24},{9,... | collective-permute-start | bytes 786440 | tf_op jit(solution)/shard_map/ppermute | solution.py:93
  7.6 0.1 fusion.4
  7.7 0.1 iota_add_fusion
  7.8 0.8 %fusion.5 = (s32[1,512]{1,0:T(1,128)S(1)}, s32[1,512]{1,0:T(1,128)S(1)}) fusion(s32[2,512]{1,0:T(2,128)} %param.8), kind=kLoop, calls=%fused_computation.36 | loop fusion | bytes 8192 | tf_op jit(solution)/shard_map/slice | solution.py:193
  8.5 0.0 collective-permute-done
  8.5 2.7 %collective-permute-start.1 = (bf16[64,2048]{1,0:T(8,128)(2,1)S(1)}, bf16[64,2048]{1,0:T(8,128)(2,1)S(1)}, u32[]{:S(2)}, u32[]{:S(2)}) collective-permute-start(bf16[64,2048]{1,0:T(8,128)(2,1)S(1)} %collective-permute-done), channel_id=1, source_target_pairs={{0,2},{1,3},{2,0},{3,1},{4,6},{5,7},{6,4},{7,5},{8,10},{9,11},{10,... | collective-permute-start | bytes 786440 | tf_op jit(solution)/shard_map/ppermute | solution.py:93
  11.3 1.0 %collective-permute-done.9.refs_3_ = bf16[64,2048]{1,0:T(8,128)(2,1)S(1)} collective-permute-done((bf16[64,2048]{1,0:T(8,128)(2,1)}, bf16[64,2048]{1,0:T(8,128)(2,1)S(1)}, u32[]{:S(2)}, u32[]{:S(2)}) %collective-permute-start.9) | collective-permute-done | bytes 262176 | tf_op jit(solution)/shard_map/ppermute | solution.py:93
  12.3 1.2 %collective-permute-done.3.refs_0_ = bf16[64,2048]{1,0:T(8,128)(2,1)S(1)} collective-permute-done((bf16[64,2048]{1,0:T(8,128)(2,1)}, bf16[64,2048]{1,0:T(8,128)(2,1)S(1)}, u32[]{:S(2)}, u32[]{:S(2)}) %collective-permute-start.3) | collective-permute-done | bytes 262176 | tf_op jit(solution)/shard_map/ppermute | solution.py:93
  13.5 1.6 %collective-permute-start.10 = (bf16[64,2048]{1,0:T(8,128)(2,1)S(1)}, bf16[64,2048]{1,0:T(8,128)(2,1)S(1)}, u32[]{:S(2)}, u32[]{:S(2)}) collective-permute-start(bf16[64,2048]{1,0:T(8,128)(2,1)S(1)} %broadcast_select_fusion.2), channel_id=1, source_target_pairs={{0,16},{1,17},{2,18},{3,19},{4,20},{5,21},{6,22},{7,23},{8,9},{9,8... | collective-permute-start | bytes 786440 | tf_op jit(solution)/shard_map/ppermute | solution.py:93
  15.1 0.0 collective-permute-done.4
  15.1 0.0 collective-permute-start.6
  15.1 1.6 %collective-permute-done.1 = bf16[64,2048]{1,0:T(8,128)(2,1)S(1)} collective-permute-done((bf16[64,2048]{1,0:T(8,128)(2,1)S(1)}, bf16[64,2048]{1,0:T(8,128)(2,1)S(1)}, u32[]{:S(2)}, u32[]{:S(2)}) %collective-permute-start.1) | collective-permute-done | bytes 262176 | tf_op jit(solution)/shard_map/ppermute | solution.py:93
  16.7 1.6 %collective-permute-start.2 = (s32[256]{0:T(256)}, s32[256]{0:T(256)S(1)}, u32[]{:S(2)}, u32[]{:S(2)}) collective-permute-start(s32[256]{0:T(256)} %bitcast.23), channel_id=1, source_target_pairs={{0,16},{1,17},{2,18},{3,19},{4,20},{5,21},{6,22},{7,23},{8,24},{9,... | collective-permute-start | bytes 3080 | tf_op jit(solution)/shard_map/ppermute | solution.py:93
  18.4 0.0 copy-start
  18.4 0.0 copy-start.1
  18.4 1.6 %collective-permute-start.11 = (bf16[128,2048]{1,0:T(8,128)(2,1)S(1)}, bf16[128,2048]{1,0:T(8,128)(2,1)S(1)}, u32[]{:S(2)}, u32[]{:S(2)}) collective-permute-start(bf16[128,2048]{1,0:T(8,128)(2,1)S(1)} %pad_maximum_fusion.refs_1_), channel_id=1, source_target_pairs={{0,1},{1,0},{2,3},{3,2},{4,5},{5,4},{6,7},{7,6},{8,9},{9,8},{10,11... | collective-permute-start | bytes 1572872 | tf_op jit(solution)/shard_map/ppermute | solution.py:93
  20.0 0.5 collective-permute-start.5
  20.5 0.0 collective-permute-done.6
  20.5 1.7 %collective-permute-start.7 = (bf16[64,2048]{1,0:T(8,128)(2,1)S(1)}, bf16[64,2048]{1,0:T(8,128)(2,1)S(1)}, u32[]{:S(2)}, u32[]{:S(2)}) collective-permute-start(bf16[64,2048]{1,0:T(8,128)(2,1)S(1)} %collective-permute-done.6), channel_id=1, source_target_pairs={{0,2},{1,3},{2,0},{3,1},{4,6},{5,7},{6,4},{7,5},{8,10},{9,11},{10,... | collective-permute-start | bytes 786440 | tf_op jit(solution)/shard_map/ppermute | solution.py:93
  22.2 0.0 collective-permute-done.2
  22.2 0.7 %pad_add_fusion.1 = s32[2,256]{1,0:T(2,128)S(1)} fusion(s32[1,256]{1,0:T(1,128)S(1)} %bitcast.25, s32[1,256]{1,0:T(1,128)} %bitcast.24), kind=kLoop, calls=%fused_computation.32 | loop fusion | flops 512 | bytes 4096 | tf_op jit(solution)/shard_map/stack | solution.py:190
  22.9 1.4 %select_reduce_fusion = (s32[2,256]{1,0:T(2,128)S(1)}, s32[2,256]{1,0:T(2,128)S(1)}, s32[2,256]{1,0:T(2,128)S(1)}) fusion(s32[512]{0:T(512)} %param.9, s32[2,256]{1,0:T(2,128)S(1)} %pad_add_fusion.1, s32[512]{0:T(512)S(1)} %bitcast.22, s32[512]{0:T(512)S(1)} %bitcast.21), kind=kLoop, calls=%fused_computation.2 | loop fusion | flops 1833472 | bytes 14336 | tf_op jit(solution)/shard_map/reduce_sum | solution.py:192
  24.3 0.1 fusion.3
  24.3 0.2 fusion
  24.6 0.1 slice_bitcast_fusion
  24.6 0.2 compare_convert_fusion
  24.8 2.0 %collective-permute-done.7 = bf16[64,2048]{1,0:T(8,128)(2,1)S(1)} collective-permute-done((bf16[64,2048]{1,0:T(8,128)(2,1)S(1)}, bf16[64,2048]{1,0:T(8,128)(2,1)S(1)}, u32[]{:S(2)}, u32[]{:S(2)}) %collective-permute-start.7) | collective-permute-done | bytes 262176 | tf_op jit(solution)/shard_map/ppermute | solution.py:93
  26.9 1.3 %collective-permute-start.13 = (bf16[64,2048]{1,0:T(8,128)(2,1)S(1)}, bf16[64,2048]{1,0:T(8,128)(2,1)S(1)}, u32[]{:S(2)}, u32[]{:S(2)}) collective-permute-start(bf16[64,2048]{1,0:T(8,128)(2,1)S(1)} %broadcast_select_fusion.3.refs_2_), channel_id=1, source_target_pairs={{0,1},{1,0},{2,3},{3,2},{4,5},{5,4},{6,7},{7,6},{8,9},{9,8},{10,11... | collective-permute-start | bytes 786440 | tf_op jit(solution)/shard_map/ppermute | solution.py:93
  28.2 2.6 %collective-permute-start.8 = (bf16[64,2048]{1,0:T(8,128)(2,1)S(1)}, bf16[64,2048]{1,0:T(8,128)(2,1)S(1)}, u32[]{:S(2)}, u32[]{:S(2)}) collective-permute-start(bf16[64,2048]{1,0:T(8,128)(2,1)S(1)} %broadcast_select_fusion.3.refs_2_), channel_id=1, source_target_pairs={{0,16},{1,17},{2,18},{3,19},{4,20},{5,21},{6,22},{7,23},{8,24},{9,... | collective-permute-start | bytes 786440 | tf_op jit(solution)/shard_map/ppermute | solution.py:93
  30.8 2.6 %collective-permute-done.11.refs_4_ = bf16[128,2048]{1,0:T(8,128)(2,1)S(1)} collective-permute-done((bf16[128,2048]{1,0:T(8,128)(2,1)S(1)}, bf16[128,2048]{1,0:T(8,128)(2,1)S(1)}, u32[]{:S(2)}, u32[]{:S(2)}) %collective-permute-start.11) | collective-permute-done | bytes 524320 | tf_op jit(solution)/shard_map/ppermute | solution.py:93
  33.3 0.0 collective-permute-done.5.refs_1_
  33.3 0.1 broadcast_select_fusion
  33.4 0.5 collective-permute-start.12
  33.9 5.1 %collective-permute-done.13.refs_5_ = bf16[64,2048]{1,0:T(8,128)(2,1)S(1)} collective-permute-done((bf16[64,2048]{1,0:T(8,128)(2,1)S(1)}, bf16[64,2048]{1,0:T(8,128)(2,1)S(1)}, u32[]{:S(2)}, u32[]{:S(2)}) %collective-permute-start.13) | collective-permute-done | bytes 262176 | tf_op jit(solution)/shard_map/ppermute | solution.py:93
  38.9 0.0 collective-permute-done.8.refs_2_
  39.0 0.1 collective-permute-start.14
  39.1 0.0 copy-done.2
  39.1 5.2 %add_segment.2 = (f32[256,1024]{1,0:T(8,128)S(1)}, f32[256,1024]{1,0:T(8,128)S(1)}) custom-call(bf16[512,512]{1,0:T(8,128)(2,1)S(1)} %get-tuple-element.20.picks_ref, bf16[2,256,256]{2,1,0:T(8,128)(2,1)S(1)} %get-tuple-element.22.select_ref, bf16[2048,1024]{1,0:T(8,128)(2,1)S(1)} %copy-done.1, bf16[2048,1024]{1,0:T(8,128)(2,1)S(1)} %copy-done.2, ...), custom_call_target="tpu_custom_call" | custom-call | flops 4831838208 | bytes 12582912 | tf_op jit(solution)/shard_map/add_segment/pallas_call | solution.py:146
  44.3 0.0 collective-permute-done.10.refs_3_
  44.3 1.3 %collective-permute-done.14.refs_5_ = bf16[64,2048]{1,0:T(8,128)(2,1)S(1)} collective-permute-done((bf16[64,2048]{1,0:T(8,128)(2,1)S(1)}, bf16[64,2048]{1,0:T(8,128)(2,1)S(1)}, u32[]{:S(2)}, u32[]{:S(2)}) %collective-permute-start.14) | collective-permute-done | bytes 262176 | tf_op jit(solution)/shard_map/ppermute | solution.py:93
  45.6 0.0 collective-permute-done.12.refs_4_
  45.6 5.2 %add_segment.3 = (f32[256,1024]{1,0:T(8,128)S(1)}, f32[256,1024]{1,0:T(8,128)S(1)}) custom-call(bf16[512,512]{1,0:T(8,128)(2,1)S(1)} %get-tuple-element.21.picks_ref, bf16[2,256,256]{2,1,0:T(8,128)(2,1)S(1)} %get-tuple-element.23.select_ref, bf16[2048,1024]{1,0:T(8,128)(2,1)S(1)} %copy-done.1, bf16[2048,1024]{1,0:T(8,128)(2,1)S(1)} %copy-done.2, ...), custom_call_target="tpu_custom_call" | custom-call | flops 4831838208 | bytes 12582912 | tf_op jit(solution)/shard_map/add_segment/pallas_call | solution.py:146
  50.8 0.1 collective-permute-start.15
  50.9 2.6 %collective-permute-done.15 = f32[256,1024]{1,0:T(8,128)S(1)} collective-permute-done((f32[256,1024]{1,0:T(8,128)S(1)}, f32[256,1024]{1,0:T(8,128)S(1)}, u32[]{:S(2)}, u32[]{:S(2)}) %collective-permute-start.15) | collective-permute-done | bytes 1048608 | tf_op jit(solution)/shard_map/ppermute | solution.py:93
  53.5 1.1 %add.92 = f32[256,1024]{1,0:T(8,128)} add(f32[256,1024]{1,0:T(8,128)S(1)} %get-tuple-element.15, f32[256,1024]{1,0:T(8,128)S(1)} %collective-permute-done.15) | non-fusion elementwise | flops 262144 | bytes 3145728 | tf_op jit(solution)/shard_map/add | solution.py:217
  (9 shorter events, 0.2 us)
Async XLA Ops:
  0.0 8.5 %collective-permute-start = (bf16[64,2048]{1,0:T(8,128)(2,1)}, bf16[64,2048]{1,0:T(8,128)(2,1)S(1)}, u32[]{:S(2)}, u32[]{:S(2)}) collective-permute-start(bf16[64,2048]{1,0:T(8,128)(2,1)} %bitcast.16), channel_id=1, source_target_pairs={{0,8},{1,9},{2,4},{3,5},{4,2},{5,3},{6,14},{7,15},{8,0},{9,1},{10,... | collective-permute-start | bytes 786440 | tf_op jit(solution)/shard_map/ppermute | solution.py:93
  0.5 14.7 %collective-permute-start.4 = (bf16[64,2048]{1,0:T(8,128)(2,1)}, bf16[64,2048]{1,0:T(8,128)(2,1)S(1)}, u32[]{:S(2)}, u32[]{:S(2)}) collective-permute-start(bf16[64,2048]{1,0:T(8,128)(2,1)} %bitcast.17), channel_id=1, source_target_pairs={{0,2},{1,3},{2,0},{3,1},{4,6},{5,7},{6,4},{7,5},{8,10},{9,11},{10,... | collective-permute-start | bytes 786440 | tf_op jit(solution)/shard_map/ppermute | solution.py:93
  4.6 7.7 %collective-permute-start.9 = (bf16[64,2048]{1,0:T(8,128)(2,1)}, bf16[64,2048]{1,0:T(8,128)(2,1)S(1)}, u32[]{:S(2)}, u32[]{:S(2)}) collective-permute-start(bf16[64,2048]{1,0:T(8,128)(2,1)} %bitcast.18), channel_id=1, source_target_pairs={{0,1},{1,0},{2,3},{3,2},{4,5},{5,4},{6,7},{7,6},{8,9},{9,8},{10,11... | collective-permute-start | bytes 786440 | tf_op jit(solution)/shard_map/ppermute | solution.py:93
  6.1 7.4 %collective-permute-start.3 = (bf16[64,2048]{1,0:T(8,128)(2,1)}, bf16[64,2048]{1,0:T(8,128)(2,1)S(1)}, u32[]{:S(2)}, u32[]{:S(2)}) collective-permute-start(bf16[64,2048]{1,0:T(8,128)(2,1)} %bitcast.19), channel_id=1, source_target_pairs={{0,16},{1,17},{2,18},{3,19},{4,20},{5,21},{6,22},{7,23},{8,24},{9,... | collective-permute-start | bytes 786440 | tf_op jit(solution)/shard_map/ppermute | solution.py:93
  8.5 8.2 %collective-permute-start.1 = (bf16[64,2048]{1,0:T(8,128)(2,1)S(1)}, bf16[64,2048]{1,0:T(8,128)(2,1)S(1)}, u32[]{:S(2)}, u32[]{:S(2)}) collective-permute-start(bf16[64,2048]{1,0:T(8,128)(2,1)S(1)} %collective-permute-done), channel_id=1, source_target_pairs={{0,2},{1,3},{2,0},{3,1},{4,6},{5,7},{6,4},{7,5},{8,10},{9,11},{10,... | collective-permute-start | bytes 786440 | tf_op jit(solution)/shard_map/ppermute | solution.py:93
  13.5 30.7 %collective-permute-start.10 = (bf16[64,2048]{1,0:T(8,128)(2,1)S(1)}, bf16[64,2048]{1,0:T(8,128)(2,1)S(1)}, u32[]{:S(2)}, u32[]{:S(2)}) collective-permute-start(bf16[64,2048]{1,0:T(8,128)(2,1)S(1)} %broadcast_select_fusion.2), channel_id=1, source_target_pairs={{0,16},{1,17},{2,18},{3,19},{4,20},{5,21},{6,22},{7,23},{8,9},{9,8... | collective-permute-start | bytes 786440 | tf_op jit(solution)/shard_map/ppermute | solution.py:93
  15.1 5.3 %collective-permute-start.6 = (bf16[64,2048]{1,0:T(8,128)(2,1)S(1)}, bf16[64,2048]{1,0:T(8,128)(2,1)S(1)}, u32[]{:S(2)}, u32[]{:S(2)}) collective-permute-start(bf16[64,2048]{1,0:T(8,128)(2,1)S(1)} %collective-permute-done.4), channel_id=1, source_target_pairs={{0,8},{1,9},{2,4},{3,5},{4,2},{5,3},{6,14},{7,15},{8,0},{9,1},{10,... | collective-permute-start | bytes 786440 | tf_op jit(solution)/shard_map/ppermute | solution.py:93
  16.7 5.5 %collective-permute-start.2 = (s32[256]{0:T(256)}, s32[256]{0:T(256)S(1)}, u32[]{:S(2)}, u32[]{:S(2)}) collective-permute-start(s32[256]{0:T(256)} %bitcast.23), channel_id=1, source_target_pairs={{0,16},{1,17},{2,18},{3,19},{4,20},{5,21},{6,22},{7,23},{8,24},{9,... | collective-permute-start | bytes 3080 | tf_op jit(solution)/shard_map/ppermute | solution.py:93
  18.3 20.7 %copy-start.2 = (bf16[2048,1024]{1,0:T(8,128)(2,1)S(1)}, bf16[2048,1024]{1,0:T(8,128)(2,1)}, u32[]{:S(2)}) copy-start(bf16[2048,1024]{1,0:T(8,128)(2,1)} %constant.95.clone.table_low) | copy-start | bytes 12582916
  18.4 20.7 %copy-start = (bf16[1,64,2048]{2,1,0:T(8,128)(2,1)S(1)}, bf16[1,64,2048]{2,1,0:T(8,128)(2,1)}, u32[]{:S(2)}) copy-start(bf16[1,64,2048]{2,1,0:T(8,128)(2,1)} %param.6) | copy-start | bytes 786436
  18.4 20.7 %copy-start.1 = (bf16[2048,1024]{1,0:T(8,128)(2,1)S(1)}, bf16[2048,1024]{1,0:T(8,128)(2,1)}, u32[]{:S(2)}) copy-start(bf16[2048,1024]{1,0:T(8,128)(2,1)} %constant.94.clone.table_high) | copy-start | bytes 12582916
  18.4 14.9 %collective-permute-start.11 = (bf16[128,2048]{1,0:T(8,128)(2,1)S(1)}, bf16[128,2048]{1,0:T(8,128)(2,1)S(1)}, u32[]{:S(2)}, u32[]{:S(2)}) collective-permute-start(bf16[128,2048]{1,0:T(8,128)(2,1)S(1)} %pad_maximum_fusion.refs_1_), channel_id=1, source_target_pairs={{0,1},{1,0},{2,3},{3,2},{4,5},{5,4},{6,7},{7,6},{8,9},{9,8},{10,11... | collective-permute-start | bytes 1572872 | tf_op jit(solution)/shard_map/ppermute | solution.py:93
  20.0 13.4 %collective-permute-start.5 = (bf16[128,2048]{1,0:T(8,128)(2,1)S(1)}, bf16[128,2048]{1,0:T(8,128)(2,1)S(1)}, u32[]{:S(2)}, u32[]{:S(2)}) collective-permute-start(bf16[128,2048]{1,0:T(8,128)(2,1)S(1)} %pad_maximum_fusion.refs_1_), channel_id=1, source_target_pairs={{0,16},{1,17},{2,18},{3,19},{4,20},{5,21},{6,22},{7,23},{8,24},{9,... | collective-permute-start | bytes 1572872 | tf_op jit(solution)/shard_map/ppermute | solution.py:93
  20.5 6.4 %collective-permute-start.7 = (bf16[64,2048]{1,0:T(8,128)(2,1)S(1)}, bf16[64,2048]{1,0:T(8,128)(2,1)S(1)}, u32[]{:S(2)}, u32[]{:S(2)}) collective-permute-start(bf16[64,2048]{1,0:T(8,128)(2,1)S(1)} %collective-permute-done.6), channel_id=1, source_target_pairs={{0,2},{1,3},{2,0},{3,1},{4,6},{5,7},{6,4},{7,5},{8,10},{9,11},{10,... | collective-permute-start | bytes 786440 | tf_op jit(solution)/shard_map/ppermute | solution.py:93
  26.9 12.1 %collective-permute-start.13 = (bf16[64,2048]{1,0:T(8,128)(2,1)S(1)}, bf16[64,2048]{1,0:T(8,128)(2,1)S(1)}, u32[]{:S(2)}, u32[]{:S(2)}) collective-permute-start(bf16[64,2048]{1,0:T(8,128)(2,1)S(1)} %broadcast_select_fusion.3.refs_2_), channel_id=1, source_target_pairs={{0,1},{1,0},{2,3},{3,2},{4,5},{5,4},{6,7},{7,6},{8,9},{9,8},{10,11... | collective-permute-start | bytes 786440 | tf_op jit(solution)/shard_map/ppermute | solution.py:93
  28.2 10.8 %collective-permute-start.8 = (bf16[64,2048]{1,0:T(8,128)(2,1)S(1)}, bf16[64,2048]{1,0:T(8,128)(2,1)S(1)}, u32[]{:S(2)}, u32[]{:S(2)}) collective-permute-start(bf16[64,2048]{1,0:T(8,128)(2,1)S(1)} %broadcast_select_fusion.3.refs_2_), channel_id=1, source_target_pairs={{0,16},{1,17},{2,18},{3,19},{4,20},{5,21},{6,22},{7,23},{8,24},{9,... | collective-permute-start | bytes 786440 | tf_op jit(solution)/shard_map/ppermute | solution.py:93
  33.4 12.2 %collective-permute-start.12 = (bf16[128,2048]{1,0:T(8,128)(2,1)S(1)}, bf16[128,2048]{1,0:T(8,128)(2,1)S(1)}, u32[]{:S(2)}, u32[]{:S(2)}) collective-permute-start(bf16[128,2048]{1,0:T(8,128)(2,1)S(1)} %broadcast_select_fusion), channel_id=1, source_target_pairs={{0,16},{1,17},{2,18},{3,19},{4,20},{5,21},{6,22},{7,23},{8,9},{9,8... | collective-permute-start | bytes 1572872 | tf_op jit(solution)/shard_map/ppermute | solution.py:93
  39.0 6.6 %collective-permute-start.14 = (bf16[64,2048]{1,0:T(8,128)(2,1)S(1)}, bf16[64,2048]{1,0:T(8,128)(2,1)S(1)}, u32[]{:S(2)}, u32[]{:S(2)}) collective-permute-start(bf16[64,2048]{1,0:T(8,128)(2,1)S(1)} %broadcast_select_fusion.1), channel_id=1, source_target_pairs={{0,16},{1,17},{2,18},{3,19},{4,20},{5,21},{6,22},{7,23},{8,9},{9,8... | collective-permute-start | bytes 786440 | tf_op jit(solution)/shard_map/ppermute | solution.py:93
  50.8 2.7 %collective-permute-start.15 = (f32[256,1024]{1,0:T(8,128)S(1)}, f32[256,1024]{1,0:T(8,128)S(1)}, u32[]{:S(2)}, u32[]{:S(2)}) collective-permute-start(f32[256,1024]{1,0:T(8,128)S(1)} %get-tuple-element.16), channel_id=1, source_target_pairs={{0,8},{1,9},{2,10},{3,11},{4,12},{5,13},{6,14},{7,15},{8,0},{9,1},... | collective-permute-start | bytes 3145736 | tf_op jit(solution)/shard_map/ppermute | solution.py:93

commit v5 on v4

--- a/solution.py
+++ b/solution.py
@@ -94,27 +94,40 @@
 
 
 def split_table(bins):
-    index = np.arange(bins)[:, None] * (np.arange(LAGS)[None, :] - LAGS // 2) % (2 * bins)
+    index = np.arange(bins)[:, None] * np.arange(LAGS // 2)[None, :] % (2 * bins)
     angle = index * (np.pi / bins)
-    rows = np.concatenate([np.cos(angle), -np.sin(angle)]) / np.sqrt(bins)
+    rows = np.concatenate([np.cos(angle), np.sin(angle)]) / np.sqrt(bins)
     rows = rows.astype(np.float32)
     high = rows.astype(jnp.bfloat16)
     low = (rows - high.astype(np.float32)).astype(jnp.bfloat16)
     return jnp.asarray(high), jnp.asarray(low)
 
 
+def first_lag(bins):
+    index = np.arange(bins) * (LAGS // 2) % (2 * bins)
+    angle = index * (np.pi / bins)
+    return jnp.asarray(np.stack([np.cos(angle), np.sin(angle)]) / np.sqrt(bins), jnp.float32)
+
+
+def backwards():
+    half = LAGS // 2
+    return jnp.asarray(np.arange(half)[:, None] == -np.arange(half)[None, :] % half, jnp.bfloat16)
+
+
 def two_parts(value):
     high = value.astype(jnp.bfloat16)
     return high, (value - high.astype(jnp.float32)).astype(jnp.bfloat16)
 
 
-def segment_kernel(picks_ref, select_ref, table_high, table_low, *refs):
+def segment_kernel(picks_ref, select_ref, table_high, table_low, first_ref, back_ref, *refs):
     blocks, refs = refs[:6], refs[6:]
     earlier, (theirs_ref, ours_ref, high_cross, low_cross) = refs[:-4], refs[-4:]
     entries = picks_ref.shape[0] // 2
     bins = table_high.shape[0] // 2
     dot = functools.partial(jnp.dot, preferred_element_type=jnp.float32)
 
+    half = LAGS // 2
+    first = jnp.zeros((entries, 1), jnp.float32)
     for at in range(0, bins, BLOCK):
         real, imag = slice(at, at + BLOCK), slice(bins + at, bins + at + BLOCK)
         stations = jnp.concatenate(
@@ -123,16 +136,25 @@
         both = dot(picks_ref[...], stations)
         real_a, imag_a = both[:entries, :BLOCK], both[:entries, BLOCK:]
         real_b, imag_b = both[entries:, :BLOCK], both[entries:, BLOCK:]
-        for value, columns in (
-            (real_a * real_b + imag_a * imag_b, real),
-            (real_a * imag_b - imag_a * real_b, imag),
-        ):
-            high_cross[:, columns], low_cross[:, columns] = two_parts(value)
-
-    lags = dot(high_cross[...], table_high[...])
-    lags += dot(low_cross[...], table_high[...])
-    lags += dot(high_cross[...], table_low[...])
-    high, low = two_parts(lags)
+        real_c = real_a * real_b + imag_a * imag_b
+        imag_c = real_a * imag_b - imag_a * real_b
+        high_cross[:, real], low_cross[:, real] = two_parts(real_c)
+        high_cross[:, imag], low_cross[:, imag] = two_parts(imag_c)
+        terms = real_c * first_ref[0:1, real] + imag_c * first_ref[1:2, real]
+        first += jnp.sum(terms, axis=1, keepdims=True)
+
+    even, odd = (
+        dot(high_cross[:, part], table_high[part, :])
+        + dot(low_cross[:, part], table_high[part, :])
+        + dot(high_cross[:, part], table_low[part, :])
+        for part in (slice(0, bins), slice(bins, 2 * bins))
+    )
+    column = lax.broadcasted_iota(jnp.int32, even.shape, 1)
+    before = jnp.where(column == 0, first, even + odd)
+    high, low = (
+        jnp.concatenate([dot(early, back_ref[...]).astype(jnp.bfloat16), late], axis=1)
+        for early, late in zip(two_parts(before), two_parts(even - odd))
+    )
     for part, out_ref in enumerate((theirs_ref, ours_ref)):
         slots = dot(select_ref[part], high) + dot(select_ref[part], low)
         out_ref[...] = slots + earlier[part][...] if earlier else slots
@@ -141,7 +163,7 @@
 def add_segment(picks, select, table, blocks, earlier=()):
     entries, (_, slots, _) = picks.shape[0] // 2, select.shape
     bins = table[0].shape[0] // 2
-    operands = [picks, select, *table, *blocks, *earlier]
+    operands = [picks, select, *table, first_lag(bins), backwards(), *blocks, *earlier]
     in_vmem = pl.BlockSpec(memory_space=pltpu.VMEM)
     return pl.pallas_call(
         segment_kernel,
@@ -151,7 +173,8 @@
         scratch_shapes=[pltpu.VMEM((entries, 2 * bins), jnp.bfloat16)] * 2,
         compiler_params=pltpu.CompilerParams(vmem_limit_bytes=24 * 1024 * 1024),
         cost_estimate=pl.CostEstimate(
-            flops=4 * entries * (bins * (3 * LAGS + 2 * picks.shape[1]) + 2 * slots * LAGS),
+            flops=2 * entries * LAGS * (3 * bins + LAGS // 2 + 4 * slots)
+            + 8 * entries * bins * picks.shape[1],
             bytes_accessed=8 * bins * (LAGS + picks.shape[1]),
             transcendentals=0,
         ),

time: 54.9 us -> 53.7 us (0.978)
  waiting for transfers between devices: 17.4 us -> 19.7 us
  Pallas kernels: 10.3 us -> 8.12 us
  other arithmetic: 3.95 us -> 2.61 us
    ppermute x16, waiting for transfers between devices: 17.4 us -> 19.7 us  [send(): return lax.ppermute(value, AXES, pairs)]
    pallas_call x2, Pallas kernels: 10.3 us -> 8.12 us  [add_segment(): pl.pallas_call(segment_kernel, out_shape=[jax.ShapeDtypeStruct((slots, LA...]
    another operation x1, other arithmetic: 0.69 us -> 0.01 us  [local_grid(): listed = jnp.stack([listed_here, listed_there])]
    reduce_sum x1, other arithmetic: 1.35 us -> 0.68 us  [local_grid(): look_up = lambda values: jnp.sum(jnp.where(hit, values, 0), axis=-1)]
  transfers between devices with their start and end apart: 16 -> 16, of which waited for: 8 -> 8; matrix products, arithmetic and copies ran while one was open for 7% -> 4% of each run, Pallas kernels for 9% -> 8%
where the time goes in v5:
time: 53.7 us; the launch traced here: 53.5 us
  starting transfers between devices  22 us (41%)
  waiting for transfers between devices  19.7 us (37%)
  Pallas kernels  8.12 us (15%)
  other arithmetic  2.61 us (5%)
  local copies, waits for them, and re-layouts  0.91 us (2%)
    ppermute x16, starting transfers between devices, send(): return lax.ppermute(value, AXES, pairs)  22 us
    ppermute x16, waiting for transfers between devices, send(): return lax.ppermute(value, AXES, pairs)  19.7 us
    pallas_call x2, Pallas kernels, add_segment(): pl.pallas_call(segment_kernel, out_shape=[jax.ShapeDtypeStruct((slots, LA...  8.12 us
    add x1, other arithmetic, local_grid(): return ours + send(theirs, OTHER_CORE)  1.12 us
  transfers between devices with their start and end apart: 16, of which 8 were waited for; matrix products, arithmetic and copies ran while one was open for 4% of the time, Pallas kernels for 8%

profile of v5, /device:TPU:0, one launch (start us, length us, event | category | flops | bytes accessed | tf_op | source)
XLA Modules:
  0.0 53.5 jit_solution(17202192271072959387)
XLA Ops:
  0.0 0.5 collective-permute-start
  0.5 4.1 %collective-permute-start.4 = (bf16[64,2048]{1,0:T(8,128)(2,1)}, bf16[64,2048]{1,0:T(8,128)(2,1)S(1)}, u32[]{:S(2)}, u32[]{:S(2)}) collective-permute-start(bf16[64,2048]{1,0:T(8,128)(2,1)} %bitcast.17), channel_id=1, source_target_pairs={{0,2},{1,3},{2,0},{3,1},{4,6},{5,7},{6,4},{7,5},{8,10},{9,11},{10,... | collective-permute-start | bytes 786440 | tf_op jit(solution)/shard_map/ppermute | solution.py:93
  4.6 1.5 %collective-permute-start.9 = (bf16[64,2048]{1,0:T(8,128)(2,1)}, bf16[64,2048]{1,0:T(8,128)(2,1)S(1)}, u32[]{:S(2)}, u32[]{:S(2)}) collective-permute-start(bf16[64,2048]{1,0:T(8,128)(2,1)} %bitcast.18), channel_id=1, source_target_pairs={{0,1},{1,0},{2,3},{3,2},{4,5},{5,4},{6,7},{7,6},{8,9},{9,8},{10,11... | collective-permute-start | bytes 786440 | tf_op jit(solution)/shard_map/ppermute | solution.py:93
  6.1 1.5 %collective-permute-start.3 = (bf16[64,2048]{1,0:T(8,128)(2,1)}, bf16[64,2048]{1,0:T(8,128)(2,1)S(1)}, u32[]{:S(2)}, u32[]{:S(2)}) collective-permute-start(bf16[64,2048]{1,0:T(8,128)(2,1)} %bitcast.19), channel_id=1, source_target_pairs={{0,16},{1,17},{2,18},{3,19},{4,20},{5,21},{6,22},{7,23},{8,24},{9,... | collective-permute-start | bytes 786440 | tf_op jit(solution)/shard_map/ppermute | solution.py:93
  7.6 0.1 fusion.4
  7.7 0.1 iota_add_fusion
  7.8 0.8 %fusion.5 = (s32[1,512]{1,0:T(1,128)S(1)}, s32[1,512]{1,0:T(1,128)S(1)}) fusion(s32[2,512]{1,0:T(2,128)} %param.12), kind=kLoop, calls=%fused_computation.36 | loop fusion | bytes 8192 | tf_op jit(solution)/shard_map/slice | solution.py:216
  8.5 0.0 collective-permute-done
  8.5 2.7 %collective-permute-start.1 = (bf16[64,2048]{1,0:T(8,128)(2,1)S(1)}, bf16[64,2048]{1,0:T(8,128)(2,1)S(1)}, u32[]{:S(2)}, u32[]{:S(2)}) collective-permute-start(bf16[64,2048]{1,0:T(8,128)(2,1)S(1)} %collective-permute-done), channel_id=1, source_target_pairs={{0,2},{1,3},{2,0},{3,1},{4,6},{5,7},{6,4},{7,5},{8,10},{9,11},{10,... | collective-permute-start | bytes 786440 | tf_op jit(solution)/shard_map/ppermute | solution.py:93
  11.3 1.0 %collective-permute-done.9.refs_3_ = bf16[64,2048]{1,0:T(8,128)(2,1)S(1)} collective-permute-done((bf16[64,2048]{1,0:T(8,128)(2,1)}, bf16[64,2048]{1,0:T(8,128)(2,1)S(1)}, u32[]{:S(2)}, u32[]{:S(2)}) %collective-permute-start.9) | collective-permute-done | bytes 262176 | tf_op jit(solution)/shard_map/ppermute | solution.py:93
  12.3 1.2 %collective-permute-done.3.refs_0_ = bf16[64,2048]{1,0:T(8,128)(2,1)S(1)} collective-permute-done((bf16[64,2048]{1,0:T(8,128)(2,1)}, bf16[64,2048]{1,0:T(8,128)(2,1)S(1)}, u32[]{:S(2)}, u32[]{:S(2)}) %collective-permute-start.3) | collective-permute-done | bytes 262176 | tf_op jit(solution)/shard_map/ppermute | solution.py:93
  13.5 1.6 %collective-permute-start.10 = (bf16[64,2048]{1,0:T(8,128)(2,1)S(1)}, bf16[64,2048]{1,0:T(8,128)(2,1)S(1)}, u32[]{:S(2)}, u32[]{:S(2)}) collective-permute-start(bf16[64,2048]{1,0:T(8,128)(2,1)S(1)} %broadcast_select_fusion.2), channel_id=1, source_target_pairs={{0,16},{1,17},{2,18},{3,19},{4,20},{5,21},{6,22},{7,23},{8,9},{9,8... | collective-permute-start | bytes 786440 | tf_op jit(solution)/shard_map/ppermute | solution.py:93
  15.1 0.0 collective-permute-done.4
  15.1 0.0 collective-permute-start.6
  15.1 1.6 %collective-permute-done.1 = bf16[64,2048]{1,0:T(8,128)(2,1)S(1)} collective-permute-done((bf16[64,2048]{1,0:T(8,128)(2,1)S(1)}, bf16[64,2048]{1,0:T(8,128)(2,1)S(1)}, u32[]{:S(2)}, u32[]{:S(2)}) %collective-permute-start.1) | collective-permute-done | bytes 262176 | tf_op jit(solution)/shard_map/ppermute | solution.py:93
  16.8 1.6 %collective-permute-start.2 = (s32[256]{0:T(256)}, s32[256]{0:T(256)S(1)}, u32[]{:S(2)}, u32[]{:S(2)}) collective-permute-start(s32[256]{0:T(256)} %bitcast.23), channel_id=1, source_target_pairs={{0,16},{1,17},{2,18},{3,19},{4,20},{5,21},{6,22},{7,23},{8,24},{9,... | collective-permute-start | bytes 3080 | tf_op jit(solution)/shard_map/ppermute | solution.py:93
  18.4 1.6 %collective-permute-start.11 = (bf16[128,2048]{1,0:T(8,128)(2,1)S(1)}, bf16[128,2048]{1,0:T(8,128)(2,1)S(1)}, u32[]{:S(2)}, u32[]{:S(2)}) collective-permute-start(bf16[128,2048]{1,0:T(8,128)(2,1)S(1)} %pad_maximum_fusion.refs_1_), channel_id=1, source_target_pairs={{0,1},{1,0},{2,3},{3,2},{4,5},{5,4},{6,7},{7,6},{8,9},{9,8},{10,11... | collective-permute-start | bytes 1572872 | tf_op jit(solution)/shard_map/ppermute | solution.py:93
  19.9 0.5 collective-permute-start.5
  20.4 0.0 collective-permute-done.6
  20.5 1.7 %collective-permute-start.7 = (bf16[64,2048]{1,0:T(8,128)(2,1)S(1)}, bf16[64,2048]{1,0:T(8,128)(2,1)S(1)}, u32[]{:S(2)}, u32[]{:S(2)}) collective-permute-start(bf16[64,2048]{1,0:T(8,128)(2,1)S(1)} %collective-permute-done.6), channel_id=1, source_target_pairs={{0,2},{1,3},{2,0},{3,1},{4,6},{5,7},{6,4},{7,5},{8,10},{9,11},{10,... | collective-permute-start | bytes 786440 | tf_op jit(solution)/shard_map/ppermute | solution.py:93
  22.2 0.0 collective-permute-done.2
  22.2 0.7 %select_reduce_fusion = (s32[2,256]{1,0:T(2,128)S(1)}, s32[2,256]{1,0:T(2,128)S(1)}, s32[2,256]{1,0:T(2,128)S(1)}) fusion(s32[512]{0:T(512)S(1)} %copy-done.5, s32[2,256]{1,0:T(2,128)S(1)} %pad_add_fusion.1, s32[512]{0:T(512)S(1)} %bitcast.22, s32[512]{0:T(512)S(1)} %bitcast.21), kind=kLoop, calls=%fused_computation.2 | loop fusion | flops 1833472 | bytes 14336 | tf_op jit(solution)/shard_map/reduce_sum | solution.py:215
  22.9 0.1 fusion.3
  23.0 0.2 fusion
  23.2 0.0 copy-start.3
  23.2 0.1 slice_bitcast_fusion
  23.3 0.0 copy-start.2
  23.3 0.2 compare_convert_fusion
  23.5 0.0 copy-start
  23.5 0.0 copy-start.1
  23.5 0.0 copy-start.4
  23.5 3.3 %collective-permute-done.7 = bf16[64,2048]{1,0:T(8,128)(2,1)S(1)} collective-permute-done((bf16[64,2048]{1,0:T(8,128)(2,1)S(1)}, bf16[64,2048]{1,0:T(8,128)(2,1)S(1)}, u32[]{:S(2)}, u32[]{:S(2)}) %collective-permute-start.7) | collective-permute-done | bytes 262176 | tf_op jit(solution)/shard_map/ppermute | solution.py:93
  26.9 1.2 %collective-permute-start.13 = (bf16[64,2048]{1,0:T(8,128)(2,1)S(1)}, bf16[64,2048]{1,0:T(8,128)(2,1)S(1)}, u32[]{:S(2)}, u32[]{:S(2)}) collective-permute-start(bf16[64,2048]{1,0:T(8,128)(2,1)S(1)} %broadcast_select_fusion.3.refs_2_), channel_id=1, source_target_pairs={{0,1},{1,0},{2,3},{3,2},{4,5},{5,4},{6,7},{7,6},{8,9},{9,8},{10,11... | collective-permute-start | bytes 786440 | tf_op jit(solution)/shard_map/ppermute | solution.py:93
  28.0 2.6 %collective-permute-start.8 = (bf16[64,2048]{1,0:T(8,128)(2,1)S(1)}, bf16[64,2048]{1,0:T(8,128)(2,1)S(1)}, u32[]{:S(2)}, u32[]{:S(2)}) collective-permute-start(bf16[64,2048]{1,0:T(8,128)(2,1)S(1)} %broadcast_select_fusion.3.refs_2_), channel_id=1, source_target_pairs={{0,16},{1,17},{2,18},{3,19},{4,20},{5,21},{6,22},{7,23},{8,24},{9,... | collective-permute-start | bytes 786440 | tf_op jit(solution)/shard_map/ppermute | solution.py:93
  30.6 2.7 %collective-permute-done.11.refs_4_ = bf16[128,2048]{1,0:T(8,128)(2,1)S(1)} collective-permute-done((bf16[128,2048]{1,0:T(8,128)(2,1)S(1)}, bf16[128,2048]{1,0:T(8,128)(2,1)S(1)}, u32[]{:S(2)}, u32[]{:S(2)}) %collective-permute-start.11) | collective-permute-done | bytes 524320 | tf_op jit(solution)/shard_map/ppermute | solution.py:93
  33.3 0.0 collective-permute-done.5.refs_1_
  33.3 0.1 broadcast_select_fusion
  33.4 0.8 %collective-permute-start.12 = (bf16[128,2048]{1,0:T(8,128)(2,1)S(1)}, bf16[128,2048]{1,0:T(8,128)(2,1)S(1)}, u32[]{:S(2)}, u32[]{:S(2)}) collective-permute-start(bf16[128,2048]{1,0:T(8,128)(2,1)S(1)} %broadcast_select_fusion), channel_id=1, source_target_pairs={{0,16},{1,17},{2,18},{3,19},{4,20},{5,21},{6,22},{7,23},{8,9},{9,8... | collective-permute-start | bytes 1572872 | tf_op jit(solution)/shard_map/ppermute | solution.py:93
  34.1 4.8 %collective-permute-done.13.refs_5_ = bf16[64,2048]{1,0:T(8,128)(2,1)S(1)} collective-permute-done((bf16[64,2048]{1,0:T(8,128)(2,1)S(1)}, bf16[64,2048]{1,0:T(8,128)(2,1)S(1)}, u32[]{:S(2)}, u32[]{:S(2)}) %collective-permute-start.13) | collective-permute-done | bytes 262176 | tf_op jit(solution)/shard_map/ppermute | solution.py:93
  38.9 0.0 collective-permute-done.8.refs_2_
  39.0 0.1 collective-permute-start.14
  39.1 4.0 %add_segment.2 = (f32[256,1024]{1,0:T(8,128)S(1)}, f32[256,1024]{1,0:T(8,128)S(1)}) custom-call(bf16[512,512]{1,0:T(8,128)(2,1)S(1)} %get-tuple-element.20.picks_ref, bf16[2,256,256]{2,1,0:T(8,128)(2,1)S(1)} %get-tuple-element.22.select_ref, bf16[2048,512]{1,0:T(8,128)(2,1)S(1)} %copy-done.1, bf16[2048,512]{1,0:T(8,128)(2,1)S(1)} %copy-done.2, ...), custom_call_target="tpu_custom_call" | custom-call | flops 3489660928 | bytes 12582912 | tf_op jit(solution)/shard_map/add_segment/pallas_call | solution.py:168
  43.1 0.0 collective-permute-done.10.refs_3_
  43.2 2.4 %collective-permute-done.14.refs_5_ = bf16[64,2048]{1,0:T(8,128)(2,1)S(1)} collective-permute-done((bf16[64,2048]{1,0:T(8,128)(2,1)S(1)}, bf16[64,2048]{1,0:T(8,128)(2,1)S(1)}, u32[]{:S(2)}, u32[]{:S(2)}) %collective-permute-start.14) | collective-permute-done | bytes 262176 | tf_op jit(solution)/shard_map/ppermute | solution.py:93
  45.6 4.1 %add_segment.3 = (f32[256,1024]{1,0:T(8,128)S(1)}, f32[256,1024]{1,0:T(8,128)S(1)}) custom-call(bf16[512,512]{1,0:T(8,128)(2,1)S(1)} %get-tuple-element.21.picks_ref, bf16[2,256,256]{2,1,0:T(8,128)(2,1)S(1)} %get-tuple-element.23.select_ref, bf16[2048,512]{1,0:T(8,128)(2,1)S(1)} %copy-done.1, bf16[2048,512]{1,0:T(8,128)(2,1)S(1)} %copy-done.2, ...), custom_call_target="tpu_custom_call" | custom-call | flops 3489660928 | bytes 12582912 | tf_op jit(solution)/shard_map/add_segment/pallas_call | solution.py:168
  49.7 0.1 collective-permute-start.15
  49.7 2.6 %collective-permute-done.15 = f32[256,1024]{1,0:T(8,128)S(1)} collective-permute-done((f32[256,1024]{1,0:T(8,128)S(1)}, f32[256,1024]{1,0:T(8,128)S(1)}, u32[]{:S(2)}, u32[]{:S(2)}) %collective-permute-start.15) | collective-permute-done | bytes 1048608 | tf_op jit(solution)/shard_map/ppermute | solution.py:93
  52.4 1.1 %add.92 = f32[256,1024]{1,0:T(8,128)} add(f32[256,1024]{1,0:T(8,128)S(1)} %get-tuple-element.15, f32[256,1024]{1,0:T(8,128)S(1)} %collective-permute-done.15) | non-fusion elementwise | flops 262144 | bytes 3145728 | tf_op jit(solution)/shard_map/add | solution.py:240
  (17 shorter events, 0.2 us)
Async XLA Ops:
  0.0 22.2 %copy-start.6 = (s32[1,1,256]{2,1,0:T(1,128)S(1)}, s32[1,1,256]{2,1,0:T(1,128)}, u32[]{:S(2)}) copy-start(s32[1,1,256]{2,1,0:T(1,128)} %param.11) | copy-start | bytes 3076
  0.0 22.2 %copy-start.5 = (s32[512]{0:T(512)S(1)}, s32[512]{0:T(512)}, u32[]{:S(2)}) copy-start(s32[512]{0:T(512)} %param.13) | copy-start | bytes 6148
  0.0 8.5 %collective-permute-start = (bf16[64,2048]{1,0:T(8,128)(2,1)}, bf16[64,2048]{1,0:T(8,128)(2,1)S(1)}, u32[]{:S(2)}, u32[]{:S(2)}) collective-permute-start(bf16[64,2048]{1,0:T(8,128)(2,1)} %bitcast.16), channel_id=1, source_target_pairs={{0,8},{1,9},{2,4},{3,5},{4,2},{5,3},{6,14},{7,15},{8,0},{9,1},{10,... | collective-permute-start | bytes 786440 | tf_op jit(solution)/shard_map/ppermute | solution.py:93
  0.5 14.7 %collective-permute-start.4 = (bf16[64,2048]{1,0:T(8,128)(2,1)}, bf16[64,2048]{1,0:T(8,128)(2,1)S(1)}, u32[]{:S(2)}, u32[]{:S(2)}) collective-permute-start(bf16[64,2048]{1,0:T(8,128)(2,1)} %bitcast.17), channel_id=1, source_target_pairs={{0,2},{1,3},{2,0},{3,1},{4,6},{5,7},{6,4},{7,5},{8,10},{9,11},{10,... | collective-permute-start | bytes 786440 | tf_op jit(solution)/shard_map/ppermute | solution.py:93
  4.6 7.7 %collective-permute-start.9 = (bf16[64,2048]{1,0:T(8,128)(2,1)}, bf16[64,2048]{1,0:T(8,128)(2,1)S(1)}, u32[]{:S(2)}, u32[]{:S(2)}) collective-permute-start(bf16[64,2048]{1,0:T(8,128)(2,1)} %bitcast.18), channel_id=1, source_target_pairs={{0,1},{1,0},{2,3},{3,2},{4,5},{5,4},{6,7},{7,6},{8,9},{9,8},{10,11... | collective-permute-start | bytes 786440 | tf_op jit(solution)/shard_map/ppermute | solution.py:93
  6.1 7.4 %collective-permute-start.3 = (bf16[64,2048]{1,0:T(8,128)(2,1)}, bf16[64,2048]{1,0:T(8,128)(2,1)S(1)}, u32[]{:S(2)}, u32[]{:S(2)}) collective-permute-start(bf16[64,2048]{1,0:T(8,128)(2,1)} %bitcast.19), channel_id=1, source_target_pairs={{0,16},{1,17},{2,18},{3,19},{4,20},{5,21},{6,22},{7,23},{8,24},{9,... | collective-permute-start | bytes 786440 | tf_op jit(solution)/shard_map/ppermute | solution.py:93
  8.5 8.2 %collective-permute-start.1 = (bf16[64,2048]{1,0:T(8,128)(2,1)S(1)}, bf16[64,2048]{1,0:T(8,128)(2,1)S(1)}, u32[]{:S(2)}, u32[]{:S(2)}) collective-permute-start(bf16[64,2048]{1,0:T(8,128)(2,1)S(1)} %collective-permute-done), channel_id=1, source_target_pairs={{0,2},{1,3},{2,0},{3,1},{4,6},{5,7},{6,4},{7,5},{8,10},{9,11},{10,... | collective-permute-start | bytes 786440 | tf_op jit(solution)/shard_map/ppermute | solution.py:93
  13.5 29.6 %collective-permute-start.10 = (bf16[64,2048]{1,0:T(8,128)(2,1)S(1)}, bf16[64,2048]{1,0:T(8,128)(2,1)S(1)}, u32[]{:S(2)}, u32[]{:S(2)}) collective-permute-start(bf16[64,2048]{1,0:T(8,128)(2,1)S(1)} %broadcast_select_fusion.2), channel_id=1, source_target_pairs={{0,16},{1,17},{2,18},{3,19},{4,20},{5,21},{6,22},{7,23},{8,9},{9,8... | collective-permute-start | bytes 786440 | tf_op jit(solution)/shard_map/ppermute | solution.py:93
  15.1 5.3 %collective-permute-start.6 = (bf16[64,2048]{1,0:T(8,128)(2,1)S(1)}, bf16[64,2048]{1,0:T(8,128)(2,1)S(1)}, u32[]{:S(2)}, u32[]{:S(2)}) collective-permute-start(bf16[64,2048]{1,0:T(8,128)(2,1)S(1)} %collective-permute-done.4), channel_id=1, source_target_pairs={{0,8},{1,9},{2,4},{3,5},{4,2},{5,3},{6,14},{7,15},{8,0},{9,1},{10,... | collective-permute-start | bytes 786440 | tf_op jit(solution)/shard_map/ppermute | solution.py:93
  16.8 5.4 %collective-permute-start.2 = (s32[256]{0:T(256)}, s32[256]{0:T(256)S(1)}, u32[]{:S(2)}, u32[]{:S(2)}) collective-permute-start(s32[256]{0:T(256)} %bitcast.23), channel_id=1, source_target_pairs={{0,16},{1,17},{2,18},{3,19},{4,20},{5,21},{6,22},{7,23},{8,24},{9,... | collective-permute-start | bytes 3080 | tf_op jit(solution)/shard_map/ppermute | solution.py:93
  18.4 14.9 %collective-permute-start.11 = (bf16[128,2048]{1,0:T(8,128)(2,1)S(1)}, bf16[128,2048]{1,0:T(8,128)(2,1)S(1)}, u32[]{:S(2)}, u32[]{:S(2)}) collective-permute-start(bf16[128,2048]{1,0:T(8,128)(2,1)S(1)} %pad_maximum_fusion.refs_1_), channel_id=1, source_target_pairs={{0,1},{1,0},{2,3},{3,2},{4,5},{5,4},{6,7},{7,6},{8,9},{9,8},{10,11... | collective-permute-start | bytes 1572872 | tf_op jit(solution)/shard_map/ppermute | solution.py:93
  19.9 13.4 %collective-permute-start.5 = (bf16[128,2048]{1,0:T(8,128)(2,1)S(1)}, bf16[128,2048]{1,0:T(8,128)(2,1)S(1)}, u32[]{:S(2)}, u32[]{:S(2)}) collective-permute-start(bf16[128,2048]{1,0:T(8,128)(2,1)S(1)} %pad_maximum_fusion.refs_1_), channel_id=1, source_target_pairs={{0,16},{1,17},{2,18},{3,19},{4,20},{5,21},{6,22},{7,23},{8,24},{9,... | collective-permute-start | bytes 1572872 | tf_op jit(solution)/shard_map/ppermute | solution.py:93
  20.5 6.4 %collective-permute-start.7 = (bf16[64,2048]{1,0:T(8,128)(2,1)S(1)}, bf16[64,2048]{1,0:T(8,128)(2,1)S(1)}, u32[]{:S(2)}, u32[]{:S(2)}) collective-permute-start(bf16[64,2048]{1,0:T(8,128)(2,1)S(1)} %collective-permute-done.6), channel_id=1, source_target_pairs={{0,2},{1,3},{2,0},{3,1},{4,6},{5,7},{6,4},{7,5},{8,10},{9,11},{10,... | collective-permute-start | bytes 786440 | tf_op jit(solution)/shard_map/ppermute | solution.py:93
  23.2 15.9 %copy-start.3 = (bf16[512,512]{1,0:T(8,128)(2,1)S(1)}, bf16[512,512]{1,0:T(8,128)(2,1)}, u32[]{:S(2)}) copy-start(bf16[512,512]{1,0:T(8,128)(2,1)} %constant.101.clone.back_ref) | copy-start | bytes 1572868
  23.3 15.8 %copy-start.2 = (bf16[2048,512]{1,0:T(8,128)(2,1)S(1)}, bf16[2048,512]{1,0:T(8,128)(2,1)}, u32[]{:S(2)}) copy-start(bf16[2048,512]{1,0:T(8,128)(2,1)} %constant.99.clone.table_low) | copy-start | bytes 6291460
  23.5 15.6 %copy-start = (bf16[1,64,2048]{2,1,0:T(8,128)(2,1)S(1)}, bf16[1,64,2048]{2,1,0:T(8,128)(2,1)}, u32[]{:S(2)}) copy-start(bf16[1,64,2048]{2,1,0:T(8,128)(2,1)} %param.10) | copy-start | bytes 786436
  23.5 15.6 %copy-start.1 = (bf16[2048,512]{1,0:T(8,128)(2,1)S(1)}, bf16[2048,512]{1,0:T(8,128)(2,1)}, u32[]{:S(2)}) copy-start(bf16[2048,512]{1,0:T(8,128)(2,1)} %constant.98.clone.table_high) | copy-start | bytes 6291460
  23.5 15.6 %copy-start.4 = (f32[2,1024]{1,0:T(2,128)S(1)}, f32[2,1024]{1,0:T(2,128)}, u32[]{:S(2)}) copy-start(f32[2,1024]{1,0:T(2,128)} %constant.100.clone.first_ref) | copy-start | bytes 24580
  26.9 12.1 %collective-permute-start.13 = (bf16[64,2048]{1,0:T(8,128)(2,1)S(1)}, bf16[64,2048]{1,0:T(8,128)(2,1)S(1)}, u32[]{:S(2)}, u32[]{:S(2)}) collective-permute-start(bf16[64,2048]{1,0:T(8,128)(2,1)S(1)} %broadcast_select_fusion.3.refs_2_), channel_id=1, source_target_pairs={{0,1},{1,0},{2,3},{3,2},{4,5},{5,4},{6,7},{7,6},{8,9},{9,8},{10,11... | collective-permute-start | bytes 786440 | tf_op jit(solution)/shard_map/ppermute | solution.py:93
  28.0 10.9 %collective-permute-start.8 = (bf16[64,2048]{1,0:T(8,128)(2,1)S(1)}, bf16[64,2048]{1,0:T(8,128)(2,1)S(1)}, u32[]{:S(2)}, u32[]{:S(2)}) collective-permute-start(bf16[64,2048]{1,0:T(8,128)(2,1)S(1)} %broadcast_select_fusion.3.refs_2_), channel_id=1, source_target_pairs={{0,16},{1,17},{2,18},{3,19},{4,20},{5,21},{6,22},{7,23},{8,24},{9,... | collective-permute-start | bytes 786440 | tf_op jit(solution)/shard_map/ppermute | solution.py:93
  33.4 12.2 %collective-permute-start.12 = (bf16[128,2048]{1,0:T(8,128)(2,1)S(1)}, bf16[128,2048]{1,0:T(8,128)(2,1)S(1)}, u32[]{:S(2)}, u32[]{:S(2)}) collective-permute-start(bf16[128,2048]{1,0:T(8,128)(2,1)S(1)} %broadcast_select_fusion), channel_id=1, source_target_pairs={{0,16},{1,17},{2,18},{3,19},{4,20},{5,21},{6,22},{7,23},{8,9},{9,8... | collective-permute-start | bytes 1572872 | tf_op jit(solution)/shard_map/ppermute | solution.py:93
  39.0 6.6 %collective-permute-start.14 = (bf16[64,2048]{1,0:T(8,128)(2,1)S(1)}, bf16[64,2048]{1,0:T(8,128)(2,1)S(1)}, u32[]{:S(2)}, u32[]{:S(2)}) collective-permute-start(bf16[64,2048]{1,0:T(8,128)(2,1)S(1)} %broadcast_select_fusion.1), channel_id=1, source_target_pairs={{0,16},{1,17},{2,18},{3,19},{4,20},{5,21},{6,22},{7,23},{8,9},{9,8... | collective-permute-start | bytes 786440 | tf_op jit(solution)/shard_map/ppermute | solution.py:93
  49.7 2.7 %collective-permute-start.15 = (f32[256,1024]{1,0:T(8,128)S(1)}, f32[256,1024]{1,0:T(8,128)S(1)}, u32[]{:S(2)}, u32[]{:S(2)}) collective-permute-start(f32[256,1024]{1,0:T(8,128)S(1)} %get-tuple-element.16), channel_id=1, source_target_pairs={{0,8},{1,9},{2,10},{3,11},{4,12},{5,13},{6,14},{7,15},{8,0},{9,1},... | collective-permute-start | bytes 3145736 | tf_op jit(solution)/shard_map/ppermute | solution.py:93

commit v6 on v5

--- a/solution.py
+++ b/solution.py
@@ -119,9 +119,9 @@
     return high, (value - high.astype(jnp.float32)).astype(jnp.bfloat16)
 
 
-def segment_kernel(picks_ref, select_ref, table_high, table_low, first_ref, back_ref, *refs):
-    blocks, refs = refs[:6], refs[6:]
-    earlier, (theirs_ref, ours_ref, high_cross, low_cross) = refs[:-4], refs[-4:]
+def segment_kernel(count, rows, picks_ref, select_ref, table_high, table_low, first_ref, back_ref, *refs):
+    blocks, refs = refs[:count], refs[count:]
+    earlier, (theirs_ref, high_ref, low_ref, high_cross, low_cross) = refs[:-5], refs[-5:]
     entries = picks_ref.shape[0] // 2
     bins = table_high.shape[0] // 2
     dot = functools.partial(jnp.dot, preferred_element_type=jnp.float32)
@@ -131,7 +131,11 @@
     for at in range(0, bins, BLOCK):
         real, imag = slice(at, at + BLOCK), slice(bins + at, bins + at + BLOCK)
         stations = jnp.concatenate(
-            [jnp.concatenate([ref[:, real], ref[:, imag]], axis=1) for ref in blocks], axis=0
+            [
+                jnp.concatenate([ref[:many, real], ref[:many, imag]], axis=1)
+                for ref, many in zip(blocks, rows)
+            ],
+            axis=0,
         )
         both = dot(picks_ref[...], stations)
         real_a, imag_a = both[:entries, :BLOCK], both[:entries, BLOCK:]
@@ -155,31 +159,58 @@
         jnp.concatenate([dot(early, back_ref[...]).astype(jnp.bfloat16), late], axis=1)
         for early, late in zip(two_parts(before), two_parts(even - odd))
     )
-    for part, out_ref in enumerate((theirs_ref, ours_ref)):
-        slots = dot(select_ref[part], high) + dot(select_ref[part], low)
-        out_ref[...] = slots + earlier[part][...] if earlier else slots
-
-
-def add_segment(picks, select, table, blocks, earlier=()):
-    entries, (_, slots, _) = picks.shape[0] // 2, select.shape
+    high_ref[...], low_ref[...] = high, low
+    slots = dot(select_ref[...], high) + dot(select_ref[...], low)
+    theirs_ref[...] = slots + earlier[0][...] if earlier else slots
+
+
+def slots_kernel(select_ref, *refs):
+    parts, out_ref = refs[:-1], refs[-1]
+    out_ref[...] = sum(
+        jnp.dot(select_ref[at // 2], part[...], preferred_element_type=jnp.float32)
+        for at, part in enumerate(parts)
+    )
+
+
+def add_segment(picks, select, table, blocks, stations, earlier=()):
+    entries, slots = picks.shape[0] // 2, select.shape[0]
+    rows = [block.shape[0] // stations * stations for block in blocks]
     bins = table[0].shape[0] // 2
     operands = [picks, select, *table, first_lag(bins), backwards(), *blocks, *earlier]
     in_vmem = pl.BlockSpec(memory_space=pltpu.VMEM)
     return pl.pallas_call(
-        segment_kernel,
-        out_shape=[jax.ShapeDtypeStruct((slots, LAGS), jnp.float32)] * 2,
+        functools.partial(segment_kernel, len(blocks), rows),
+        out_shape=[jax.ShapeDtypeStruct((slots, LAGS), jnp.float32)]
+        + [jax.ShapeDtypeStruct((entries, LAGS), jnp.bfloat16)] * 2,
         in_specs=[in_vmem] * len(operands),
-        out_specs=[in_vmem] * 2,
+        out_specs=[in_vmem] * 3,
         scratch_shapes=[pltpu.VMEM((entries, 2 * bins), jnp.bfloat16)] * 2,
         compiler_params=pltpu.CompilerParams(vmem_limit_bytes=24 * 1024 * 1024),
         cost_estimate=pl.CostEstimate(
-            flops=2 * entries * LAGS * (3 * bins + LAGS // 2 + 4 * slots)
+            flops=2 * entries * LAGS * (3 * bins + LAGS // 2 + 2 * slots)
             + 8 * entries * bins * picks.shape[1],
             bytes_accessed=8 * bins * (LAGS + picks.shape[1]),
             transcendentals=0,
         ),
         name="add_segment",
     )(*operands)
+
+
+def add_slots(select, parts):
+    in_vmem = pl.BlockSpec(memory_space=pltpu.VMEM)
+    return pl.pallas_call(
+        slots_kernel,
+        out_shape=jax.ShapeDtypeStruct((select.shape[1], LAGS), jnp.float32),
+        in_specs=[in_vmem] * (1 + len(parts)),
+        out_specs=in_vmem,
+        compiler_params=pltpu.CompilerParams(vmem_limit_bytes=16 * 1024 * 1024),
+        cost_estimate=pl.CostEstimate(
+            flops=2 * len(parts) * parts[0].size * select.shape[1],
+            bytes_accessed=4 * len(parts) * parts[0].size,
+            transcendentals=0,
+        ),
+        name="add_slots",
+    )(select, *parts)
 
 
 def local_grid(spectra, pair_list, pair_stations, owner_code):
@@ -198,16 +229,18 @@
     def diagonal(side, ahead):
         return send(jnp.where(core == 0, side, ahead), DIAGONAL)
 
+    listed_here = pair_list[0, 0]
     inner = (layer == 1) | (layer == 2)
     side, ahead = around(own)
-    near, swapped = send(own, PAIR_SWAP), send(own, INNER_SWAP)
-    corner = diagonal(side, ahead)
-    third = jnp.where(inner, swapped, send(swapped, OUTWARD))
+    near, m1 = send(own, PAIR_SWAP), send(own, INNER_SWAP)
+    l1 = send(m1, OUTWARD)
+    third = jnp.where(inner, m1, l1)
+    m2 = send(near, INNER_SWAP)
+    corner = send(jnp.where(core == 0, side, ahead), DIAGONAL)
     two = jnp.concatenate([near, third], axis=0)
     two_side, two_ahead = around(two)
-    swapped = send(near, INNER_SWAP)
-    fourth = jnp.where(inner, swapped, send(swapped, OUTWARD))
-    listed_here = pair_list[0, 0]
+    l2 = send(m2, OUTWARD)
+    fourth = jnp.where(inner, m2, l2)
     listed_there = send(after(listed_here, third), OTHER_ROW)
 
     listed = jnp.stack([listed_here, listed_there])
@@ -223,11 +256,13 @@
     picks = (position[:, :, None] == spots).astype(jnp.bfloat16)
 
     fourth_side, fourth_ahead = around(after(fourth, picks))
-    two_corner = diagonal(two_side, two_ahead)
-    fourth_corner = diagonal(fourth_side, fourth_ahead)
+    inward = send(after(corner, third), INNER_SWAP)
+    outward = send(after(jnp.concatenate([corner, inward], axis=0), fourth), OUTWARD)
+    near_corner = outward[:stations]
+    third_corner = jnp.where(inner, inward, outward[stations:])
+    fourth_corner = send(jnp.where(core == 0, fourth_side, fourth_ahead), DIAGONAL)
     here = (own, two, fourth, side, two_side, fourth_side)
-    there = (ahead, two_ahead, fourth_ahead)
-    there += (corner, two_corner, fourth_corner)
+    there = (ahead, two_ahead, fourth_ahead, corner, near_corner, third_corner, fourth_corner)
 
     codes = look_up(owner_code)
     owner = row * CORES + jnp.stack([1 - core, core])
@@ -235,8 +270,9 @@
     select = (slots[:, :, None] == codes[:, None, None, :]).astype(jnp.bfloat16)
 
     table = split_table(bins)
-    sums = add_segment(picks[0], select[0], table, here)
-    theirs, ours = add_segment(picks[1], select[1], table, there, sums)
+    theirs, *first_parts = add_segment(picks[0], select[0, 0], table, here, stations)
+    theirs, *parts = add_segment(picks[1], select[1, 0], table, there, stations, [theirs])
+    ours = add_slots(select[:, 1], first_parts + parts)
     return ours + send(theirs, OTHER_CORE)
 
 

time: 53.7 us -> 51.5 us (0.959)
  waiting for transfers between devices: 19.7 us -> 15.7 us
  starting transfers between devices: 22 us -> 23.5 us
    ppermute x16 -> x17, waiting for transfers between devices: 19.7 us -> 15.7 us  [send(): return lax.ppermute(value, AXES, pairs)]
    ppermute x16 -> x17, starting transfers between devices: 22 us -> 23.5 us  [send(): return lax.ppermute(value, AXES, pairs)]
    pallas_call x2 -> x3, Pallas kernels: 8.12 us -> 8.3 us  [the longest x2 7.59 us: add_segment(): pl.pallas_call(functools.partial(segment_kernel, len(blocks), rows), out_...]
  transfers between devices with their start and end apart: 16 -> 17, of which waited for: 8 -> 9; matrix products, arithmetic and copies ran while one was open for 4% -> 5% of each run, Pallas kernels for 8% -> 9%
where the time goes in v6:
time: 51.5 us; the launch traced here: 51.3 us
  starting transfers between devices  23.5 us (46%)
  waiting for transfers between devices  15.7 us (30%)
  Pallas kernels  8.3 us (16%)
  other arithmetic  2.64 us (5%)
  local copies, waits for them, and re-layouts  0.91 us (2%)
    ppermute x17, starting transfers between devices, send(): return lax.ppermute(value, AXES, pairs)  23.5 us
    ppermute x17, waiting for transfers between devices, send(): return lax.ppermute(value, AXES, pairs)  15.7 us
    pallas_call x2, Pallas kernels, add_segment(): pl.pallas_call(functools.partial(segment_kernel, len(blocks), rows), out_...  7.59 us
    add x1, other arithmetic, local_grid(): return ours + send(theirs, OTHER_CORE)  1.12 us
  transfers between devices with their start and end apart: 17, of which 9 were waited for; matrix products, arithmetic and copies ran while one was open for 5% of the time, Pallas kernels for 9%

profile of v6, /device:TPU:0, one launch (start us, length us, event | category | flops | bytes accessed | tf_op | source)
XLA Modules:
  0.0 51.3 jit_solution(9260355522889007538)
XLA Ops:
  0.0 0.5 collective-permute-start
  0.5 4.1 %collective-permute-start.3 = (bf16[64,2048]{1,0:T(8,128)(2,1)}, bf16[64,2048]{1,0:T(8,128)(2,1)S(1)}, u32[]{:S(2)}, u32[]{:S(2)}) collective-permute-start(bf16[64,2048]{1,0:T(8,128)(2,1)} %bitcast.19), channel_id=1, source_target_pairs={{0,2},{1,3},{2,0},{3,1},{4,6},{5,7},{6,4},{7,5},{8,10},{9,11},{10,... | collective-permute-start | bytes 786440 | tf_op jit(solution)/shard_map/ppermute | solution.py:93
  4.6 1.5 %collective-permute-start.6 = (bf16[64,2048]{1,0:T(8,128)(2,1)}, bf16[64,2048]{1,0:T(8,128)(2,1)S(1)}, u32[]{:S(2)}, u32[]{:S(2)}) collective-permute-start(bf16[64,2048]{1,0:T(8,128)(2,1)} %bitcast.20), channel_id=1, source_target_pairs={{0,1},{1,0},{2,3},{3,2},{4,5},{5,4},{6,7},{7,6},{8,9},{9,8},{10,11... | collective-permute-start | bytes 786440 | tf_op jit(solution)/shard_map/ppermute | solution.py:93
  6.1 1.5 %collective-permute-start.9 = (bf16[64,2048]{1,0:T(8,128)(2,1)}, bf16[64,2048]{1,0:T(8,128)(2,1)S(1)}, u32[]{:S(2)}, u32[]{:S(2)}) collective-permute-start(bf16[64,2048]{1,0:T(8,128)(2,1)} %bitcast.21), channel_id=1, source_target_pairs={{0,16},{1,17},{2,18},{3,19},{4,20},{5,21},{6,22},{7,23},{8,24},{9,... | collective-permute-start | bytes 786440 | tf_op jit(solution)/shard_map/ppermute | solution.py:93
  7.6 0.1 fusion.4
  7.7 0.1 iota_add_fusion
  7.8 0.8 %fusion.5 = (s32[1,512]{1,0:T(1,128)S(1)}, s32[1,512]{1,0:T(1,128)S(1)}) fusion(s32[2,512]{1,0:T(2,128)} %param.12), kind=kLoop, calls=%fused_computation.38 | loop fusion | bytes 8192 | tf_op jit(solution)/shard_map/slice | solution.py:249
  8.5 0.0 collective-permute-done
  8.5 2.7 %collective-permute-start.1 = (bf16[64,2048]{1,0:T(8,128)(2,1)S(1)}, bf16[64,2048]{1,0:T(8,128)(2,1)S(1)}, u32[]{:S(2)}, u32[]{:S(2)}) collective-permute-start(bf16[64,2048]{1,0:T(8,128)(2,1)S(1)} %collective-permute-done), channel_id=1, source_target_pairs={{0,2},{1,3},{2,0},{3,1},{4,6},{5,7},{6,4},{7,5},{8,10},{9,11},{10,... | collective-permute-start | bytes 786440 | tf_op jit(solution)/shard_map/ppermute | solution.py:93
  11.3 1.0 %collective-permute-done.6.refs_3_ = bf16[64,2048]{1,0:T(8,128)(2,1)S(1)} collective-permute-done((bf16[64,2048]{1,0:T(8,128)(2,1)}, bf16[64,2048]{1,0:T(8,128)(2,1)S(1)}, u32[]{:S(2)}, u32[]{:S(2)}) %collective-permute-start.6) | collective-permute-done | bytes 262176 | tf_op jit(solution)/shard_map/ppermute | solution.py:93
  12.3 1.2 %collective-permute-done.9.refs_0_ = bf16[64,2048]{1,0:T(8,128)(2,1)S(1)} collective-permute-done((bf16[64,2048]{1,0:T(8,128)(2,1)}, bf16[64,2048]{1,0:T(8,128)(2,1)S(1)}, u32[]{:S(2)}, u32[]{:S(2)}) %collective-permute-start.9) | collective-permute-done | bytes 262176 | tf_op jit(solution)/shard_map/ppermute | solution.py:93
  13.5 1.6 %collective-permute-start.12 = (bf16[64,2048]{1,0:T(8,128)(2,1)S(1)}, bf16[64,2048]{1,0:T(8,128)(2,1)S(1)}, u32[]{:S(2)}, u32[]{:S(2)}) collective-permute-start(bf16[64,2048]{1,0:T(8,128)(2,1)S(1)} %broadcast_select_fusion.1), channel_id=1, source_target_pairs={{0,16},{1,17},{2,18},{3,19},{4,20},{5,21},{6,22},{7,23},{8,9},{9,8... | collective-permute-start | bytes 786440 | tf_op jit(solution)/shard_map/ppermute | solution.py:93
  15.1 0.0 collective-permute-done.3
  15.1 0.0 collective-permute-start.4
  15.1 1.6 %collective-permute-done.1 = bf16[64,2048]{1,0:T(8,128)(2,1)S(1)} collective-permute-done((bf16[64,2048]{1,0:T(8,128)(2,1)S(1)}, bf16[64,2048]{1,0:T(8,128)(2,1)S(1)}, u32[]{:S(2)}, u32[]{:S(2)}) %collective-permute-start.1) | collective-permute-done | bytes 262176 | tf_op jit(solution)/shard_map/ppermute | solution.py:93
  16.8 1.6 %collective-permute-start.2 = (s32[256]{0:T(256)}, s32[256]{0:T(256)S(1)}, u32[]{:S(2)}, u32[]{:S(2)}) collective-permute-start(s32[256]{0:T(256)} %bitcast.25), channel_id=1, source_target_pairs={{0,16},{1,17},{2,18},{3,19},{4,20},{5,21},{6,22},{7,23},{8,24},{9,... | collective-permute-start | bytes 3080 | tf_op jit(solution)/shard_map/ppermute | solution.py:93
  18.4 1.6 %collective-permute-start.7 = (bf16[128,2048]{1,0:T(8,128)(2,1)S(1)}, bf16[128,2048]{1,0:T(8,128)(2,1)S(1)}, u32[]{:S(2)}, u32[]{:S(2)}) collective-permute-start(bf16[128,2048]{1,0:T(8,128)(2,1)S(1)} %pad_maximum_fusion.refs_1_), channel_id=1, source_target_pairs={{0,1},{1,0},{2,3},{3,2},{4,5},{5,4},{6,7},{7,6},{8,9},{9,8},{10,11... | collective-permute-start | bytes 1572872 | tf_op jit(solution)/shard_map/ppermute | solution.py:93
  19.9 0.5 collective-permute-start.10
  20.4 0.0 collective-permute-done.12.refs_3_
  20.5 0.0 collective-permute-start.13
  20.5 0.0 collective-permute-done.4
  20.5 3.3 %collective-permute-start.5 = (bf16[64,2048]{1,0:T(8,128)(2,1)S(1)}, bf16[64,2048]{1,0:T(8,128)(2,1)S(1)}, u32[]{:S(2)}, u32[]{:S(2)}) collective-permute-start(bf16[64,2048]{1,0:T(8,128)(2,1)S(1)} %collective-permute-done.4), channel_id=1, source_target_pairs={{0,2},{1,3},{2,0},{3,1},{4,6},{5,7},{6,4},{7,5},{8,10},{9,11},{10,... | collective-permute-start | bytes 786440 | tf_op jit(solution)/shard_map/ppermute | solution.py:93
  23.8 0.0 collective-permute-done.2
  23.8 0.7 %select_reduce_fusion.1 = (s32[2,256]{1,0:T(2,128)S(1)}, s32[2,256]{1,0:T(2,128)S(1)}, s32[2,256]{1,0:T(2,128)S(1)}) fusion(s32[512]{0:T(512)S(1)} %bitcast.24, s32[2,256]{1,0:T(2,128)S(1)} %pad_add_fusion.1, s32[512]{0:T(512)S(1)} %bitcast.23, s32[512]{0:T(512)S(1)} %copy-done.5), kind=kLoop, calls=%fused_computation.3 | loop fusion | flops 1833472 | bytes 14336 | tf_op jit(solution)/shard_map/reduce_sum | solution.py:248
  24.5 0.2 fusion
  24.8 0.2 compare_convert_fusion
  24.9 0.0 copy-start.2
  24.9 0.1 slice_bitcast_fusion
  25.0 0.0 copy-start
  25.0 0.0 copy-start.1
  25.0 0.0 copy-start.3
  25.1 0.0 copy-start.4
  25.1 4.1 %collective-permute-done.5 = bf16[64,2048]{1,0:T(8,128)(2,1)S(1)} collective-permute-done((bf16[64,2048]{1,0:T(8,128)(2,1)S(1)}, bf16[64,2048]{1,0:T(8,128)(2,1)S(1)}, u32[]{:S(2)}, u32[]{:S(2)}) %collective-permute-start.5) | collective-permute-done | bytes 262176 | tf_op jit(solution)/shard_map/ppermute | solution.py:93
  29.2 0.6 %collective-permute-start.8 = (bf16[64,2048]{1,0:T(8,128)(2,1)S(1)}, bf16[64,2048]{1,0:T(8,128)(2,1)S(1)}, u32[]{:S(2)}, u32[]{:S(2)}) collective-permute-start(bf16[64,2048]{1,0:T(8,128)(2,1)S(1)} %broadcast_select_fusion.2.refs_2_), channel_id=1, source_target_pairs={{0,1},{1,0},{2,3},{3,2},{4,5},{5,4},{6,7},{7,6},{8,9},{9,8},{10,11... | collective-permute-start | bytes 786440 | tf_op jit(solution)/shard_map/ppermute | solution.py:93
  29.8 1.5 %collective-permute-start.11 = (bf16[64,2048]{1,0:T(8,128)(2,1)S(1)}, bf16[64,2048]{1,0:T(8,128)(2,1)S(1)}, u32[]{:S(2)}, u32[]{:S(2)}) collective-permute-start(bf16[64,2048]{1,0:T(8,128)(2,1)S(1)} %broadcast_select_fusion.2.refs_2_), channel_id=1, source_target_pairs={{0,16},{1,17},{2,18},{3,19},{4,20},{5,21},{6,22},{7,23},{8,24},{9,... | collective-permute-start | bytes 786440 | tf_op jit(solution)/shard_map/ppermute | solution.py:93
  31.4 1.1 %collective-permute-start.14 = (bf16[128,2048]{1,0:T(8,128)(2,1)S(1)}, bf16[128,2048]{1,0:T(8,128)(2,1)S(1)}, u32[]{:S(2)}, u32[]{:S(2)}) collective-permute-start(bf16[128,2048]{1,0:T(8,128)(2,1)S(1)} %pad_maximum_fusion.1), channel_id=1, source_target_pairs={{0,2},{1,3},{2,0},{3,1},{4,6},{5,7},{6,4},{7,5},{8,10},{9,11},{10,... | collective-permute-start | bytes 1572872 | tf_op jit(solution)/shard_map/ppermute | solution.py:93
  32.5 3.4 %collective-permute-done.8.refs_5_ = bf16[64,2048]{1,0:T(8,128)(2,1)S(1)} collective-permute-done((bf16[64,2048]{1,0:T(8,128)(2,1)S(1)}, bf16[64,2048]{1,0:T(8,128)(2,1)S(1)}, u32[]{:S(2)}, u32[]{:S(2)}) %collective-permute-start.8) | collective-permute-done | bytes 262176 | tf_op jit(solution)/shard_map/ppermute | solution.py:93
  35.9 1.2 %collective-permute-done.11.refs_2_ = bf16[64,2048]{1,0:T(8,128)(2,1)S(1)} collective-permute-done((bf16[64,2048]{1,0:T(8,128)(2,1)S(1)}, bf16[64,2048]{1,0:T(8,128)(2,1)S(1)}, u32[]{:S(2)}, u32[]{:S(2)}) %collective-permute-start.11) | collective-permute-done | bytes 262176 | tf_op jit(solution)/shard_map/ppermute | solution.py:93
  37.2 1.3 %collective-permute-start.15 = (bf16[64,2048]{1,0:T(8,128)(2,1)S(1)}, bf16[64,2048]{1,0:T(8,128)(2,1)S(1)}, u32[]{:S(2)}, u32[]{:S(2)}) collective-permute-start(bf16[64,2048]{1,0:T(8,128)(2,1)S(1)} %broadcast_select_fusion), channel_id=1, source_target_pairs={{0,16},{1,17},{2,18},{3,19},{4,20},{5,21},{6,22},{7,23},{8,9},{9,8... | collective-permute-start | bytes 786440 | tf_op jit(solution)/shard_map/ppermute | solution.py:93
  38.5 0.0 collective-permute-done.7.refs_4_
  38.5 3.8 %add_segment.2 = (f32[256,1024]{1,0:T(8,128)S(1)}, bf16[256,1024]{1,0:T(8,128)(2,1)S(1)}, bf16[256,1024]{1,0:T(8,128)(2,1)S(1)}) custom-call(bf16[512,512]{1,0:T(8,128)(2,1)S(1)} %get-tuple-element.29.picks_ref, bf16[256,256]{1,0:T(8,128)(2,1)S(1)} %get-tuple-element.33.select_ref, bf16[2048,512]{1,0:T(8,128)(2,1)S(1)} %copy-done.1, ...), custom_call_target="tpu_custom_call" | custom-call | flops 3221225472 | bytes 12582912 | tf_op jit(solution)/shard_map/add_segment/pallas_call | solution.py:181
  42.3 0.9 %collective-permute-done.14 = bf16[128,2048]{1,0:T(8,128)(2,1)S(1)} collective-permute-done((bf16[128,2048]{1,0:T(8,128)(2,1)S(1)}, bf16[128,2048]{1,0:T(8,128)(2,1)S(1)}, u32[]{:S(2)}, u32[]{:S(2)}) %collective-permute-start.14) | collective-permute-done | bytes 524320 | tf_op jit(solution)/shard_map/ppermute | solution.py:93
  43.3 0.3 collective-permute-done.15.refs_6_
  43.6 3.8 %add_segment.3 = (f32[256,1024]{1,0:T(8,128)S(1)}, bf16[256,1024]{1,0:T(8,128)(2,1)S(1)}, bf16[256,1024]{1,0:T(8,128)(2,1)S(1)}) custom-call(bf16[512,512]{1,0:T(8,128)(2,1)S(1)} %get-tuple-element.28.picks_ref, bf16[256,256]{1,0:T(8,128)(2,1)S(1)} %get-tuple-element.32.select_ref, bf16[2048,512]{1,0:T(8,128)(2,1)S(1)} %copy-done.1, ...), custom_call_target="tpu_custom_call" | custom-call | flops 3221225472 | bytes 12582912 | tf_op jit(solution)/shard_map/add_segment/pallas_call | solution.py:181
  47.4 0.1 collective-permute-start.16
  47.5 0.7 %add_slots.1 = f32[256,1024]{1,0:T(8,128)S(1)} custom-call(bf16[2,256,256]{2,1,0:T(8,128)(2,1)S(1)} %slice_bitcast_fusion.2.select_ref, bf16[256,1024]{1,0:T(8,128)(2,1)S(1)} %get-tuple-element.17.refs_0_, bf16[256,1024]{1,0:T(8,128)(2,1)S(1)} %get-tuple-element.18.refs_1_, bf16[256,1024]{1,0:T(8,128)(2,1)S(1)} %get-tuple-element.22.refs_2_, ...), custom_call_target="tpu_custom_call" | custom-call | flops 536870912 | bytes 4194304 | tf_op jit(solution)/shard_map/add_slots/pallas_call | solution.py:201
  48.3 1.9 %collective-permute-done.16 = f32[256,1024]{1,0:T(8,128)S(1)} collective-permute-done((f32[256,1024]{1,0:T(8,128)S(1)}, f32[256,1024]{1,0:T(8,128)S(1)}, u32[]{:S(2)}, u32[]{:S(2)}) %collective-permute-start.16) | collective-permute-done | bytes 1048608 | tf_op jit(solution)/shard_map/ppermute | solution.py:93
  50.2 1.1 %add.92 = f32[256,1024]{1,0:T(8,128)} add(f32[256,1024]{1,0:T(8,128)S(1)} %add_slots.1, f32[256,1024]{1,0:T(8,128)S(1)} %collective-permute-done.16) | non-fusion elementwise | flops 262144 | bytes 3145728 | tf_op jit(solution)/shard_map/add | solution.py:276
  (22 shorter events, 0.4 us)
Async XLA Ops:
  0.0 23.8 %copy-start.6 = (s32[1,1,256]{2,1,0:T(1,128)S(1)}, s32[1,1,256]{2,1,0:T(1,128)}, u32[]{:S(2)}) copy-start(s32[1,1,256]{2,1,0:T(1,128)} %param.11) | copy-start | bytes 3076
  0.0 23.8 %copy-start.5 = (s32[512]{0:T(512)S(1)}, s32[512]{0:T(512)}, u32[]{:S(2)}) copy-start(s32[512]{0:T(512)} %param.13) | copy-start | bytes 6148
  0.0 8.5 %collective-permute-start = (bf16[64,2048]{1,0:T(8,128)(2,1)}, bf16[64,2048]{1,0:T(8,128)(2,1)S(1)}, u32[]{:S(2)}, u32[]{:S(2)}) collective-permute-start(bf16[64,2048]{1,0:T(8,128)(2,1)} %bitcast.18), channel_id=1, source_target_pairs={{0,8},{1,9},{2,4},{3,5},{4,2},{5,3},{6,14},{7,15},{8,0},{9,1},{10,... | collective-permute-start | bytes 786440 | tf_op jit(solution)/shard_map/ppermute | solution.py:93
  0.5 14.7 %collective-permute-start.3 = (bf16[64,2048]{1,0:T(8,128)(2,1)}, bf16[64,2048]{1,0:T(8,128)(2,1)S(1)}, u32[]{:S(2)}, u32[]{:S(2)}) collective-permute-start(bf16[64,2048]{1,0:T(8,128)(2,1)} %bitcast.19), channel_id=1, source_target_pairs={{0,2},{1,3},{2,0},{3,1},{4,6},{5,7},{6,4},{7,5},{8,10},{9,11},{10,... | collective-permute-start | bytes 786440 | tf_op jit(solution)/shard_map/ppermute | solution.py:93
  4.6 7.7 %collective-permute-start.6 = (bf16[64,2048]{1,0:T(8,128)(2,1)}, bf16[64,2048]{1,0:T(8,128)(2,1)S(1)}, u32[]{:S(2)}, u32[]{:S(2)}) collective-permute-start(bf16[64,2048]{1,0:T(8,128)(2,1)} %bitcast.20), channel_id=1, source_target_pairs={{0,1},{1,0},{2,3},{3,2},{4,5},{5,4},{6,7},{7,6},{8,9},{9,8},{10,11... | collective-permute-start | bytes 786440 | tf_op jit(solution)/shard_map/ppermute | solution.py:93
  6.1 7.4 %collective-permute-start.9 = (bf16[64,2048]{1,0:T(8,128)(2,1)}, bf16[64,2048]{1,0:T(8,128)(2,1)S(1)}, u32[]{:S(2)}, u32[]{:S(2)}) collective-permute-start(bf16[64,2048]{1,0:T(8,128)(2,1)} %bitcast.21), channel_id=1, source_target_pairs={{0,16},{1,17},{2,18},{3,19},{4,20},{5,21},{6,22},{7,23},{8,24},{9,... | collective-permute-start | bytes 786440 | tf_op jit(solution)/shard_map/ppermute | solution.py:93
  8.5 8.2 %collective-permute-start.1 = (bf16[64,2048]{1,0:T(8,128)(2,1)S(1)}, bf16[64,2048]{1,0:T(8,128)(2,1)S(1)}, u32[]{:S(2)}, u32[]{:S(2)}) collective-permute-start(bf16[64,2048]{1,0:T(8,128)(2,1)S(1)} %collective-permute-done), channel_id=1, source_target_pairs={{0,2},{1,3},{2,0},{3,1},{4,6},{5,7},{6,4},{7,5},{8,10},{9,11},{10,... | collective-permute-start | bytes 786440 | tf_op jit(solution)/shard_map/ppermute | solution.py:93
  13.5 6.9 %collective-permute-start.12 = (bf16[64,2048]{1,0:T(8,128)(2,1)S(1)}, bf16[64,2048]{1,0:T(8,128)(2,1)S(1)}, u32[]{:S(2)}, u32[]{:S(2)}) collective-permute-start(bf16[64,2048]{1,0:T(8,128)(2,1)S(1)} %broadcast_select_fusion.1), channel_id=1, source_target_pairs={{0,16},{1,17},{2,18},{3,19},{4,20},{5,21},{6,22},{7,23},{8,9},{9,8... | collective-permute-start | bytes 786440 | tf_op jit(solution)/shard_map/ppermute | solution.py:93
  15.1 5.3 %collective-permute-start.4 = (bf16[64,2048]{1,0:T(8,128)(2,1)S(1)}, bf16[64,2048]{1,0:T(8,128)(2,1)S(1)}, u32[]{:S(2)}, u32[]{:S(2)}) collective-permute-start(bf16[64,2048]{1,0:T(8,128)(2,1)S(1)} %collective-permute-done.3), channel_id=1, source_target_pairs={{0,8},{1,9},{2,4},{3,5},{4,2},{5,3},{6,14},{7,15},{8,0},{9,1},{10,... | collective-permute-start | bytes 786440 | tf_op jit(solution)/shard_map/ppermute | solution.py:93
  16.8 7.0 %collective-permute-start.2 = (s32[256]{0:T(256)}, s32[256]{0:T(256)S(1)}, u32[]{:S(2)}, u32[]{:S(2)}) collective-permute-start(s32[256]{0:T(256)} %bitcast.25), channel_id=1, source_target_pairs={{0,16},{1,17},{2,18},{3,19},{4,20},{5,21},{6,22},{7,23},{8,24},{9,... | collective-permute-start | bytes 3080 | tf_op jit(solution)/shard_map/ppermute | solution.py:93
  18.4 20.1 %collective-permute-start.7 = (bf16[128,2048]{1,0:T(8,128)(2,1)S(1)}, bf16[128,2048]{1,0:T(8,128)(2,1)S(1)}, u32[]{:S(2)}, u32[]{:S(2)}) collective-permute-start(bf16[128,2048]{1,0:T(8,128)(2,1)S(1)} %pad_maximum_fusion.refs_1_), channel_id=1, source_target_pairs={{0,1},{1,0},{2,3},{3,2},{4,5},{5,4},{6,7},{7,6},{8,9},{9,8},{10,11... | collective-permute-start | bytes 1572872 | tf_op jit(solution)/shard_map/ppermute | solution.py:93
  19.9 23.3 %collective-permute-start.10 = (bf16[128,2048]{1,0:T(8,128)(2,1)S(1)}, bf16[128,2048]{1,0:T(8,128)(2,1)S(1)}, u32[]{:S(2)}, u32[]{:S(2)}) collective-permute-start(bf16[128,2048]{1,0:T(8,128)(2,1)S(1)} %pad_maximum_fusion.refs_1_), channel_id=1, source_target_pairs={{0,16},{1,17},{2,18},{3,19},{4,20},{5,21},{6,22},{7,23},{8,24},{9,... | collective-permute-start | bytes 1572872 | tf_op jit(solution)/shard_map/ppermute | solution.py:93
  20.5 10.9 %collective-permute-start.13 = (bf16[64,2048]{1,0:T(8,128)(2,1)S(1)}, bf16[64,2048]{1,0:T(8,128)(2,1)S(1)}, u32[]{:S(2)}, u32[]{:S(2)}) collective-permute-start(bf16[64,2048]{1,0:T(8,128)(2,1)S(1)} %collective-permute-done.12.refs_3_), channel_id=1, source_target_pairs={{0,8},{1,9},{2,4},{3,5},{4,2},{5,3},{6,14},{7,15},{8,0},{9,1},{10,... | collective-permute-start | bytes 786440 | tf_op jit(solution)/shard_map/ppermute | solution.py:93
  20.5 8.7 %collective-permute-start.5 = (bf16[64,2048]{1,0:T(8,128)(2,1)S(1)}, bf16[64,2048]{1,0:T(8,128)(2,1)S(1)}, u32[]{:S(2)}, u32[]{:S(2)}) collective-permute-start(bf16[64,2048]{1,0:T(8,128)(2,1)S(1)} %collective-permute-done.4), channel_id=1, source_target_pairs={{0,2},{1,3},{2,0},{3,1},{4,6},{5,7},{6,4},{7,5},{8,10},{9,11},{10,... | collective-permute-start | bytes 786440 | tf_op jit(solution)/shard_map/ppermute | solution.py:93
  24.9 13.6 %copy-start.2 = (bf16[2048,512]{1,0:T(8,128)(2,1)S(1)}, bf16[2048,512]{1,0:T(8,128)(2,1)}, u32[]{:S(2)}) copy-start(bf16[2048,512]{1,0:T(8,128)(2,1)} %constant.99.clone.table_low) | copy-start | bytes 6291460
  25.0 13.5 %copy-start = (bf16[1,64,2048]{2,1,0:T(8,128)(2,1)S(1)}, bf16[1,64,2048]{2,1,0:T(8,128)(2,1)}, u32[]{:S(2)}) copy-start(bf16[1,64,2048]{2,1,0:T(8,128)(2,1)} %param.10) | copy-start | bytes 786436
  25.0 13.5 %copy-start.1 = (bf16[2048,512]{1,0:T(8,128)(2,1)S(1)}, bf16[2048,512]{1,0:T(8,128)(2,1)}, u32[]{:S(2)}) copy-start(bf16[2048,512]{1,0:T(8,128)(2,1)} %constant.98.clone.table_high) | copy-start | bytes 6291460
  25.0 13.5 %copy-start.3 = (bf16[512,512]{1,0:T(8,128)(2,1)S(1)}, bf16[512,512]{1,0:T(8,128)(2,1)}, u32[]{:S(2)}) copy-start(bf16[512,512]{1,0:T(8,128)(2,1)} %constant.101.clone.back_ref) | copy-start | bytes 1572868
  25.1 13.5 %copy-start.4 = (f32[2,1024]{1,0:T(2,128)S(1)}, f32[2,1024]{1,0:T(2,128)}, u32[]{:S(2)}) copy-start(f32[2,1024]{1,0:T(2,128)} %constant.100.clone.first_ref) | copy-start | bytes 24580
  29.2 6.7 %collective-permute-start.8 = (bf16[64,2048]{1,0:T(8,128)(2,1)S(1)}, bf16[64,2048]{1,0:T(8,128)(2,1)S(1)}, u32[]{:S(2)}, u32[]{:S(2)}) collective-permute-start(bf16[64,2048]{1,0:T(8,128)(2,1)S(1)} %broadcast_select_fusion.2.refs_2_), channel_id=1, source_target_pairs={{0,1},{1,0},{2,3},{3,2},{4,5},{5,4},{6,7},{7,6},{8,9},{9,8},{10,11... | collective-permute-start | bytes 786440 | tf_op jit(solution)/shard_map/ppermute | solution.py:93
  29.8 7.3 %collective-permute-start.11 = (bf16[64,2048]{1,0:T(8,128)(2,1)S(1)}, bf16[64,2048]{1,0:T(8,128)(2,1)S(1)}, u32[]{:S(2)}, u32[]{:S(2)}) collective-permute-start(bf16[64,2048]{1,0:T(8,128)(2,1)S(1)} %broadcast_select_fusion.2.refs_2_), channel_id=1, source_target_pairs={{0,16},{1,17},{2,18},{3,19},{4,20},{5,21},{6,22},{7,23},{8,24},{9,... | collective-permute-start | bytes 786440 | tf_op jit(solution)/shard_map/ppermute | solution.py:93
  31.4 11.8 %collective-permute-start.14 = (bf16[128,2048]{1,0:T(8,128)(2,1)S(1)}, bf16[128,2048]{1,0:T(8,128)(2,1)S(1)}, u32[]{:S(2)}, u32[]{:S(2)}) collective-permute-start(bf16[128,2048]{1,0:T(8,128)(2,1)S(1)} %pad_maximum_fusion.1), channel_id=1, source_target_pairs={{0,2},{1,3},{2,0},{3,1},{4,6},{5,7},{6,4},{7,5},{8,10},{9,11},{10,... | collective-permute-start | bytes 1572872 | tf_op jit(solution)/shard_map/ppermute | solution.py:93
  37.2 6.4 %collective-permute-start.15 = (bf16[64,2048]{1,0:T(8,128)(2,1)S(1)}, bf16[64,2048]{1,0:T(8,128)(2,1)S(1)}, u32[]{:S(2)}, u32[]{:S(2)}) collective-permute-start(bf16[64,2048]{1,0:T(8,128)(2,1)S(1)} %broadcast_select_fusion), channel_id=1, source_target_pairs={{0,16},{1,17},{2,18},{3,19},{4,20},{5,21},{6,22},{7,23},{8,9},{9,8... | collective-permute-start | bytes 786440 | tf_op jit(solution)/shard_map/ppermute | solution.py:93
  47.4 2.7 %collective-permute-start.16 = (f32[256,1024]{1,0:T(8,128)S(1)}, f32[256,1024]{1,0:T(8,128)S(1)}, u32[]{:S(2)}, u32[]{:S(2)}) collective-permute-start(f32[256,1024]{1,0:T(8,128)S(1)} %get-tuple-element.24), channel_id=1, source_target_pairs={{0,8},{1,9},{2,10},{3,11},{4,12},{5,13},{6,14},{7,15},{8,0},{9,1},... | collective-permute-start | bytes 3145736 | tf_op jit(solution)/shard_map/ppermute | solution.py:93

commit v7 on v6

--- a/solution.py
+++ b/solution.py
@@ -126,8 +126,7 @@
     bins = table_high.shape[0] // 2
     dot = functools.partial(jnp.dot, preferred_element_type=jnp.float32)
 
-    half = LAGS // 2
-    first = jnp.zeros((entries, 1), jnp.float32)
+    first = jnp.zeros((entries, BLOCK), jnp.float32)
     for at in range(0, bins, BLOCK):
         real, imag = slice(at, at + BLOCK), slice(bins + at, bins + at + BLOCK)
         stations = jnp.concatenate(
@@ -144,8 +143,7 @@
         imag_c = real_a * imag_b - imag_a * real_b
         high_cross[:, real], low_cross[:, real] = two_parts(real_c)
         high_cross[:, imag], low_cross[:, imag] = two_parts(imag_c)
-        terms = real_c * first_ref[0:1, real] + imag_c * first_ref[1:2, real]
-        first += jnp.sum(terms, axis=1, keepdims=True)
+        first += real_c * first_ref[0:1, real] + imag_c * first_ref[1:2, real]
 
     even, odd = (
         dot(high_cross[:, part], table_high[part, :])
@@ -154,7 +152,7 @@
         for part in (slice(0, bins), slice(bins, 2 * bins))
     )
     column = lax.broadcasted_iota(jnp.int32, even.shape, 1)
-    before = jnp.where(column == 0, first, even + odd)
+    before = jnp.where(column == 0, jnp.sum(first, axis=1, keepdims=True), even + odd)
     high, low = (
         jnp.concatenate([dot(early, back_ref[...]).astype(jnp.bfloat16), late], axis=1)
         for early, late in zip(two_parts(before), two_parts(even - odd))
@@ -232,15 +230,13 @@
     listed_here = pair_list[0, 0]
     inner = (layer == 1) | (layer == 2)
     side, ahead = around(own)
-    near, m1 = send(own, PAIR_SWAP), send(own, INNER_SWAP)
-    l1 = send(m1, OUTWARD)
-    third = jnp.where(inner, m1, l1)
-    m2 = send(near, INNER_SWAP)
-    corner = send(jnp.where(core == 0, side, ahead), DIAGONAL)
+    near, swapped = send(own, PAIR_SWAP), send(own, INNER_SWAP)
+    third = jnp.where(inner, swapped, send(swapped, OUTWARD))
+    swapped = send(near, INNER_SWAP)
+    corner = diagonal(side, ahead)
     two = jnp.concatenate([near, third], axis=0)
     two_side, two_ahead = around(two)
-    l2 = send(m2, OUTWARD)
-    fourth = jnp.where(inner, m2, l2)
+    fourth = jnp.where(inner, swapped, send(swapped, OUTWARD))
     listed_there = send(after(listed_here, third), OTHER_ROW)
 
     listed = jnp.stack([listed_here, listed_there])
@@ -260,7 +256,7 @@
     outward = send(after(jnp.concatenate([corner, inward], axis=0), fourth), OUTWARD)
     near_corner = outward[:stations]
     third_corner = jnp.where(inner, inward, outward[stations:])
-    fourth_corner = send(jnp.where(core == 0, fourth_side, fourth_ahead), DIAGONAL)
+    fourth_corner = diagonal(fourth_side, fourth_ahead)
     here = (own, two, fourth, side, two_side, fourth_side)
     there = (ahead, two_ahead, fourth_ahead, corner, near_corner, third_corner, fourth_corner)
 

time: 51.5 us -> 51.4 us (level)
  no operation moved by 1% of the time
where the time goes in v7:
time: 51.4 us; the launch traced here: 51.2 us
  starting transfers between devices  23.5 us (46%)
  waiting for transfers between devices  15.8 us (31%)
  Pallas kernels  8.13 us (16%)
  other arithmetic  2.64 us (5%)
  local copies, waits for them, and re-layouts  0.91 us (2%)
    ppermute x17, starting transfers between devices, send(): return lax.ppermute(value, AXES, pairs)  23.5 us
    ppermute x17, waiting for transfers between devices, send(): return lax.ppermute(value, AXES, pairs)  15.8 us
    pallas_call x2, Pallas kernels, add_segment(): pl.pallas_call(functools.partial(segment_kernel, len(blocks), rows), out_...  7.41 us
    add x1, other arithmetic, local_grid(): return ours + send(theirs, OTHER_CORE)  1.12 us
  transfers between devices with their start and end apart: 17, of which 9 were waited for; matrix products, arithmetic and copies ran while one was open for 5% of the time, Pallas kernels for 9%

profile of v7, /device:TPU:0, one launch (start us, length us, event | category | flops | bytes accessed | tf_op | source)
XLA Modules:
  0.0 51.2 jit_solution(3609468960757659831)
XLA Ops:
  0.0 0.5 collective-permute-start
  0.5 4.1 %collective-permute-start.3 = (bf16[64,2048]{1,0:T(8,128)(2,1)}, bf16[64,2048]{1,0:T(8,128)(2,1)S(1)}, u32[]{:S(2)}, u32[]{:S(2)}) collective-permute-start(bf16[64,2048]{1,0:T(8,128)(2,1)} %bitcast.19), channel_id=1, source_target_pairs={{0,2},{1,3},{2,0},{3,1},{4,6},{5,7},{6,4},{7,5},{8,10},{9,11},{10,... | collective-permute-start | bytes 786440 | tf_op jit(solution)/shard_map/ppermute | solution.py:93
  4.6 1.5 %collective-permute-start.6 = (bf16[64,2048]{1,0:T(8,128)(2,1)}, bf16[64,2048]{1,0:T(8,128)(2,1)S(1)}, u32[]{:S(2)}, u32[]{:S(2)}) collective-permute-start(bf16[64,2048]{1,0:T(8,128)(2,1)} %bitcast.20), channel_id=1, source_target_pairs={{0,1},{1,0},{2,3},{3,2},{4,5},{5,4},{6,7},{7,6},{8,9},{9,8},{10,11... | collective-permute-start | bytes 786440 | tf_op jit(solution)/shard_map/ppermute | solution.py:93
  6.1 1.5 %collective-permute-start.9 = (bf16[64,2048]{1,0:T(8,128)(2,1)}, bf16[64,2048]{1,0:T(8,128)(2,1)S(1)}, u32[]{:S(2)}, u32[]{:S(2)}) collective-permute-start(bf16[64,2048]{1,0:T(8,128)(2,1)} %bitcast.21), channel_id=1, source_target_pairs={{0,16},{1,17},{2,18},{3,19},{4,20},{5,21},{6,22},{7,23},{8,24},{9,... | collective-permute-start | bytes 786440 | tf_op jit(solution)/shard_map/ppermute | solution.py:93
  7.6 0.1 fusion.4
  7.7 0.1 iota_add_fusion
  7.8 0.8 %fusion.5 = (s32[1,512]{1,0:T(1,128)S(1)}, s32[1,512]{1,0:T(1,128)S(1)}) fusion(s32[2,512]{1,0:T(2,128)} %param.12), kind=kLoop, calls=%fused_computation.38 | loop fusion | bytes 8192 | tf_op jit(solution)/shard_map/slice | solution.py:245
  8.5 0.0 collective-permute-done
  8.5 2.7 %collective-permute-start.1 = (bf16[64,2048]{1,0:T(8,128)(2,1)S(1)}, bf16[64,2048]{1,0:T(8,128)(2,1)S(1)}, u32[]{:S(2)}, u32[]{:S(2)}) collective-permute-start(bf16[64,2048]{1,0:T(8,128)(2,1)S(1)} %collective-permute-done), channel_id=1, source_target_pairs={{0,2},{1,3},{2,0},{3,1},{4,6},{5,7},{6,4},{7,5},{8,10},{9,11},{10,... | collective-permute-start | bytes 786440 | tf_op jit(solution)/shard_map/ppermute | solution.py:93
  11.3 1.0 %collective-permute-done.6.refs_3_ = bf16[64,2048]{1,0:T(8,128)(2,1)S(1)} collective-permute-done((bf16[64,2048]{1,0:T(8,128)(2,1)}, bf16[64,2048]{1,0:T(8,128)(2,1)S(1)}, u32[]{:S(2)}, u32[]{:S(2)}) %collective-permute-start.6) | collective-permute-done | bytes 262176 | tf_op jit(solution)/shard_map/ppermute | solution.py:93
  12.3 1.2 %collective-permute-done.9.refs_0_ = bf16[64,2048]{1,0:T(8,128)(2,1)S(1)} collective-permute-done((bf16[64,2048]{1,0:T(8,128)(2,1)}, bf16[64,2048]{1,0:T(8,128)(2,1)S(1)}, u32[]{:S(2)}, u32[]{:S(2)}) %collective-permute-start.9) | collective-permute-done | bytes 262176 | tf_op jit(solution)/shard_map/ppermute | solution.py:93
  13.5 1.6 %collective-permute-start.12 = (bf16[64,2048]{1,0:T(8,128)(2,1)S(1)}, bf16[64,2048]{1,0:T(8,128)(2,1)S(1)}, u32[]{:S(2)}, u32[]{:S(2)}) collective-permute-start(bf16[64,2048]{1,0:T(8,128)(2,1)S(1)} %broadcast_select_fusion.1), channel_id=1, source_target_pairs={{0,16},{1,17},{2,18},{3,19},{4,20},{5,21},{6,22},{7,23},{8,9},{9,8... | collective-permute-start | bytes 786440 | tf_op jit(solution)/shard_map/ppermute | solution.py:93
  15.1 0.0 collective-permute-done.3
  15.1 0.0 collective-permute-start.4
  15.1 1.6 %collective-permute-done.1 = bf16[64,2048]{1,0:T(8,128)(2,1)S(1)} collective-permute-done((bf16[64,2048]{1,0:T(8,128)(2,1)S(1)}, bf16[64,2048]{1,0:T(8,128)(2,1)S(1)}, u32[]{:S(2)}, u32[]{:S(2)}) %collective-permute-start.1) | collective-permute-done | bytes 262176 | tf_op jit(solution)/shard_map/ppermute | solution.py:93
  16.8 1.6 %collective-permute-start.2 = (s32[256]{0:T(256)}, s32[256]{0:T(256)S(1)}, u32[]{:S(2)}, u32[]{:S(2)}) collective-permute-start(s32[256]{0:T(256)} %bitcast.25), channel_id=1, source_target_pairs={{0,16},{1,17},{2,18},{3,19},{4,20},{5,21},{6,22},{7,23},{8,24},{9,... | collective-permute-start | bytes 3080 | tf_op jit(solution)/shard_map/ppermute | solution.py:93
  18.4 1.6 %collective-permute-start.7 = (bf16[128,2048]{1,0:T(8,128)(2,1)S(1)}, bf16[128,2048]{1,0:T(8,128)(2,1)S(1)}, u32[]{:S(2)}, u32[]{:S(2)}) collective-permute-start(bf16[128,2048]{1,0:T(8,128)(2,1)S(1)} %pad_maximum_fusion.refs_1_), channel_id=1, source_target_pairs={{0,1},{1,0},{2,3},{3,2},{4,5},{5,4},{6,7},{7,6},{8,9},{9,8},{10,11... | collective-permute-start | bytes 1572872 | tf_op jit(solution)/shard_map/ppermute | solution.py:93
  19.9 0.5 collective-permute-start.10
  20.4 0.0 collective-permute-done.12.refs_3_
  20.5 0.0 collective-permute-start.13
  20.5 0.0 collective-permute-done.4
  20.5 3.3 %collective-permute-start.5 = (bf16[64,2048]{1,0:T(8,128)(2,1)S(1)}, bf16[64,2048]{1,0:T(8,128)(2,1)S(1)}, u32[]{:S(2)}, u32[]{:S(2)}) collective-permute-start(bf16[64,2048]{1,0:T(8,128)(2,1)S(1)} %collective-permute-done.4), channel_id=1, source_target_pairs={{0,2},{1,3},{2,0},{3,1},{4,6},{5,7},{6,4},{7,5},{8,10},{9,11},{10,... | collective-permute-start | bytes 786440 | tf_op jit(solution)/shard_map/ppermute | solution.py:93
  23.8 0.7 %select_reduce_fusion.1 = (s32[2,256]{1,0:T(2,128)S(1)}, s32[2,256]{1,0:T(2,128)S(1)}, s32[2,256]{1,0:T(2,128)S(1)}) fusion(s32[512]{0:T(512)S(1)} %bitcast.24, s32[2,256]{1,0:T(2,128)S(1)} %pad_add_fusion.1, s32[512]{0:T(512)S(1)} %bitcast.23, s32[512]{0:T(512)S(1)} %copy-done.5), kind=kLoop, calls=%fused_computation.3 | loop fusion | flops 1833472 | bytes 14336 | tf_op jit(solution)/shard_map/reduce_sum | solution.py:244
  24.5 0.2 fusion
  24.8 0.2 compare_convert_fusion
  24.9 0.0 copy-start.2
  24.9 0.1 slice_bitcast_fusion
  25.0 0.0 copy-start
  25.0 0.0 copy-start.1
  25.0 0.0 copy-start.3
  25.1 0.0 copy-start.4
  25.1 4.1 %collective-permute-done.5 = bf16[64,2048]{1,0:T(8,128)(2,1)S(1)} collective-permute-done((bf16[64,2048]{1,0:T(8,128)(2,1)S(1)}, bf16[64,2048]{1,0:T(8,128)(2,1)S(1)}, u32[]{:S(2)}, u32[]{:S(2)}) %collective-permute-start.5) | collective-permute-done | bytes 262176 | tf_op jit(solution)/shard_map/ppermute | solution.py:93
  29.2 0.6 %collective-permute-start.8 = (bf16[64,2048]{1,0:T(8,128)(2,1)S(1)}, bf16[64,2048]{1,0:T(8,128)(2,1)S(1)}, u32[]{:S(2)}, u32[]{:S(2)}) collective-permute-start(bf16[64,2048]{1,0:T(8,128)(2,1)S(1)} %broadcast_select_fusion.2.refs_2_), channel_id=1, source_target_pairs={{0,1},{1,0},{2,3},{3,2},{4,5},{5,4},{6,7},{7,6},{8,9},{9,8},{10,11... | collective-permute-start | bytes 786440 | tf_op jit(solution)/shard_map/ppermute | solution.py:93
  29.8 1.5 %collective-permute-start.11 = (bf16[64,2048]{1,0:T(8,128)(2,1)S(1)}, bf16[64,2048]{1,0:T(8,128)(2,1)S(1)}, u32[]{:S(2)}, u32[]{:S(2)}) collective-permute-start(bf16[64,2048]{1,0:T(8,128)(2,1)S(1)} %broadcast_select_fusion.2.refs_2_), channel_id=1, source_target_pairs={{0,16},{1,17},{2,18},{3,19},{4,20},{5,21},{6,22},{7,23},{8,24},{9,... | collective-permute-start | bytes 786440 | tf_op jit(solution)/shard_map/ppermute | solution.py:93
  31.4 1.1 %collective-permute-start.14 = (bf16[128,2048]{1,0:T(8,128)(2,1)S(1)}, bf16[128,2048]{1,0:T(8,128)(2,1)S(1)}, u32[]{:S(2)}, u32[]{:S(2)}) collective-permute-start(bf16[128,2048]{1,0:T(8,128)(2,1)S(1)} %pad_maximum_fusion.1), channel_id=1, source_target_pairs={{0,2},{1,3},{2,0},{3,1},{4,6},{5,7},{6,4},{7,5},{8,10},{9,11},{10,... | collective-permute-start | bytes 1572872 | tf_op jit(solution)/shard_map/ppermute | solution.py:93
  32.5 3.4 %collective-permute-done.8.refs_5_ = bf16[64,2048]{1,0:T(8,128)(2,1)S(1)} collective-permute-done((bf16[64,2048]{1,0:T(8,128)(2,1)S(1)}, bf16[64,2048]{1,0:T(8,128)(2,1)S(1)}, u32[]{:S(2)}, u32[]{:S(2)}) %collective-permute-start.8) | collective-permute-done | bytes 262176 | tf_op jit(solution)/shard_map/ppermute | solution.py:93
  35.9 1.2 %collective-permute-done.11.refs_2_ = bf16[64,2048]{1,0:T(8,128)(2,1)S(1)} collective-permute-done((bf16[64,2048]{1,0:T(8,128)(2,1)S(1)}, bf16[64,2048]{1,0:T(8,128)(2,1)S(1)}, u32[]{:S(2)}, u32[]{:S(2)}) %collective-permute-start.11) | collective-permute-done | bytes 262176 | tf_op jit(solution)/shard_map/ppermute | solution.py:93
  37.2 1.3 %collective-permute-start.15 = (bf16[64,2048]{1,0:T(8,128)(2,1)S(1)}, bf16[64,2048]{1,0:T(8,128)(2,1)S(1)}, u32[]{:S(2)}, u32[]{:S(2)}) collective-permute-start(bf16[64,2048]{1,0:T(8,128)(2,1)S(1)} %broadcast_select_fusion), channel_id=1, source_target_pairs={{0,16},{1,17},{2,18},{3,19},{4,20},{5,21},{6,22},{7,23},{8,9},{9,8... | collective-permute-start | bytes 786440 | tf_op jit(solution)/shard_map/ppermute | solution.py:93
  38.5 0.0 collective-permute-done.7.refs_4_
  38.5 3.7 %add_segment.2 = (f32[256,1024]{1,0:T(8,128)S(1)}, bf16[256,1024]{1,0:T(8,128)(2,1)S(1)}, bf16[256,1024]{1,0:T(8,128)(2,1)S(1)}) custom-call(bf16[512,512]{1,0:T(8,128)(2,1)S(1)} %get-tuple-element.29.picks_ref, bf16[256,256]{1,0:T(8,128)(2,1)S(1)} %get-tuple-element.33.select_ref, bf16[2048,512]{1,0:T(8,128)(2,1)S(1)} %copy-done.1, ...), custom_call_target="tpu_custom_call" | custom-call | flops 3221225472 | bytes 12582912 | tf_op jit(solution)/shard_map/add_segment/pallas_call | solution.py:179
  42.2 1.0 %collective-permute-done.14 = bf16[128,2048]{1,0:T(8,128)(2,1)S(1)} collective-permute-done((bf16[128,2048]{1,0:T(8,128)(2,1)S(1)}, bf16[128,2048]{1,0:T(8,128)(2,1)S(1)}, u32[]{:S(2)}, u32[]{:S(2)}) %collective-permute-start.14) | collective-permute-done | bytes 524320 | tf_op jit(solution)/shard_map/ppermute | solution.py:93
  43.3 0.0 collective-permute-done.10.refs_1_
  43.3 0.3 collective-permute-done.15.refs_6_
  43.6 3.7 %add_segment.3 = (f32[256,1024]{1,0:T(8,128)S(1)}, bf16[256,1024]{1,0:T(8,128)(2,1)S(1)}, bf16[256,1024]{1,0:T(8,128)(2,1)S(1)}) custom-call(bf16[512,512]{1,0:T(8,128)(2,1)S(1)} %get-tuple-element.28.picks_ref, bf16[256,256]{1,0:T(8,128)(2,1)S(1)} %get-tuple-element.32.select_ref, bf16[2048,512]{1,0:T(8,128)(2,1)S(1)} %copy-done.1, ...), custom_call_target="tpu_custom_call" | custom-call | flops 3221225472 | bytes 12582912 | tf_op jit(solution)/shard_map/add_segment/pallas_call | solution.py:179
  47.3 0.1 collective-permute-start.16
  47.5 0.7 %add_slots.1 = f32[256,1024]{1,0:T(8,128)S(1)} custom-call(bf16[2,256,256]{2,1,0:T(8,128)(2,1)S(1)} %slice_bitcast_fusion.2.select_ref, bf16[256,1024]{1,0:T(8,128)(2,1)S(1)} %get-tuple-element.17.refs_0_, bf16[256,1024]{1,0:T(8,128)(2,1)S(1)} %get-tuple-element.18.refs_1_, bf16[256,1024]{1,0:T(8,128)(2,1)S(1)} %get-tuple-element.22.refs_2_, ...), custom_call_target="tpu_custom_call" | custom-call | flops 536870912 | bytes 4194304 | tf_op jit(solution)/shard_map/add_slots/pallas_call | solution.py:199
  48.2 1.9 %collective-permute-done.16 = f32[256,1024]{1,0:T(8,128)S(1)} collective-permute-done((f32[256,1024]{1,0:T(8,128)S(1)}, f32[256,1024]{1,0:T(8,128)S(1)}, u32[]{:S(2)}, u32[]{:S(2)}) %collective-permute-start.16) | collective-permute-done | bytes 1048608 | tf_op jit(solution)/shard_map/ppermute | solution.py:93
  50.1 1.1 %add.92 = f32[256,1024]{1,0:T(8,128)} add(f32[256,1024]{1,0:T(8,128)S(1)} %add_slots.1, f32[256,1024]{1,0:T(8,128)S(1)} %collective-permute-done.16) | non-fusion elementwise | flops 262144 | bytes 3145728 | tf_op jit(solution)/shard_map/add | solution.py:272
  (22 shorter events, 0.4 us)
Async XLA Ops:
  0.0 23.8 %copy-start.6 = (s32[1,1,256]{2,1,0:T(1,128)S(1)}, s32[1,1,256]{2,1,0:T(1,128)}, u32[]{:S(2)}) copy-start(s32[1,1,256]{2,1,0:T(1,128)} %param.11) | copy-start | bytes 3076
  0.0 23.8 %copy-start.5 = (s32[512]{0:T(512)S(1)}, s32[512]{0:T(512)}, u32[]{:S(2)}) copy-start(s32[512]{0:T(512)} %param.13) | copy-start | bytes 6148
  0.0 8.5 %collective-permute-start = (bf16[64,2048]{1,0:T(8,128)(2,1)}, bf16[64,2048]{1,0:T(8,128)(2,1)S(1)}, u32[]{:S(2)}, u32[]{:S(2)}) collective-permute-start(bf16[64,2048]{1,0:T(8,128)(2,1)} %bitcast.18), channel_id=1, source_target_pairs={{0,8},{1,9},{2,4},{3,5},{4,2},{5,3},{6,14},{7,15},{8,0},{9,1},{10,... | collective-permute-start | bytes 786440 | tf_op jit(solution)/shard_map/ppermute | solution.py:93
  0.5 14.7 %collective-permute-start.3 = (bf16[64,2048]{1,0:T(8,128)(2,1)}, bf16[64,2048]{1,0:T(8,128)(2,1)S(1)}, u32[]{:S(2)}, u32[]{:S(2)}) collective-permute-start(bf16[64,2048]{1,0:T(8,128)(2,1)} %bitcast.19), channel_id=1, source_target_pairs={{0,2},{1,3},{2,0},{3,1},{4,6},{5,7},{6,4},{7,5},{8,10},{9,11},{10,... | collective-permute-start | bytes 786440 | tf_op jit(solution)/shard_map/ppermute | solution.py:93
  4.6 7.7 %collective-permute-start.6 = (bf16[64,2048]{1,0:T(8,128)(2,1)}, bf16[64,2048]{1,0:T(8,128)(2,1)S(1)}, u32[]{:S(2)}, u32[]{:S(2)}) collective-permute-start(bf16[64,2048]{1,0:T(8,128)(2,1)} %bitcast.20), channel_id=1, source_target_pairs={{0,1},{1,0},{2,3},{3,2},{4,5},{5,4},{6,7},{7,6},{8,9},{9,8},{10,11... | collective-permute-start | bytes 786440 | tf_op jit(solution)/shard_map/ppermute | solution.py:93
  6.1 7.4 %collective-permute-start.9 = (bf16[64,2048]{1,0:T(8,128)(2,1)}, bf16[64,2048]{1,0:T(8,128)(2,1)S(1)}, u32[]{:S(2)}, u32[]{:S(2)}) collective-permute-start(bf16[64,2048]{1,0:T(8,128)(2,1)} %bitcast.21), channel_id=1, source_target_pairs={{0,16},{1,17},{2,18},{3,19},{4,20},{5,21},{6,22},{7,23},{8,24},{9,... | collective-permute-start | bytes 786440 | tf_op jit(solution)/shard_map/ppermute | solution.py:93
  8.5 8.2 %collective-permute-start.1 = (bf16[64,2048]{1,0:T(8,128)(2,1)S(1)}, bf16[64,2048]{1,0:T(8,128)(2,1)S(1)}, u32[]{:S(2)}, u32[]{:S(2)}) collective-permute-start(bf16[64,2048]{1,0:T(8,128)(2,1)S(1)} %collective-permute-done), channel_id=1, source_target_pairs={{0,2},{1,3},{2,0},{3,1},{4,6},{5,7},{6,4},{7,5},{8,10},{9,11},{10,... | collective-permute-start | bytes 786440 | tf_op jit(solution)/shard_map/ppermute | solution.py:93
  13.5 6.9 %collective-permute-start.12 = (bf16[64,2048]{1,0:T(8,128)(2,1)S(1)}, bf16[64,2048]{1,0:T(8,128)(2,1)S(1)}, u32[]{:S(2)}, u32[]{:S(2)}) collective-permute-start(bf16[64,2048]{1,0:T(8,128)(2,1)S(1)} %broadcast_select_fusion.1), channel_id=1, source_target_pairs={{0,16},{1,17},{2,18},{3,19},{4,20},{5,21},{6,22},{7,23},{8,9},{9,8... | collective-permute-start | bytes 786440 | tf_op jit(solution)/shard_map/ppermute | solution.py:93
  15.1 5.3 %collective-permute-start.4 = (bf16[64,2048]{1,0:T(8,128)(2,1)S(1)}, bf16[64,2048]{1,0:T(8,128)(2,1)S(1)}, u32[]{:S(2)}, u32[]{:S(2)}) collective-permute-start(bf16[64,2048]{1,0:T(8,128)(2,1)S(1)} %collective-permute-done.3), channel_id=1, source_target_pairs={{0,8},{1,9},{2,4},{3,5},{4,2},{5,3},{6,14},{7,15},{8,0},{9,1},{10,... | collective-permute-start | bytes 786440 | tf_op jit(solution)/shard_map/ppermute | solution.py:93
  16.8 7.0 %collective-permute-start.2 = (s32[256]{0:T(256)}, s32[256]{0:T(256)S(1)}, u32[]{:S(2)}, u32[]{:S(2)}) collective-permute-start(s32[256]{0:T(256)} %bitcast.25), channel_id=1, source_target_pairs={{0,16},{1,17},{2,18},{3,19},{4,20},{5,21},{6,22},{7,23},{8,24},{9,... | collective-permute-start | bytes 3080 | tf_op jit(solution)/shard_map/ppermute | solution.py:93
  18.4 20.1 %collective-permute-start.7 = (bf16[128,2048]{1,0:T(8,128)(2,1)S(1)}, bf16[128,2048]{1,0:T(8,128)(2,1)S(1)}, u32[]{:S(2)}, u32[]{:S(2)}) collective-permute-start(bf16[128,2048]{1,0:T(8,128)(2,1)S(1)} %pad_maximum_fusion.refs_1_), channel_id=1, source_target_pairs={{0,1},{1,0},{2,3},{3,2},{4,5},{5,4},{6,7},{7,6},{8,9},{9,8},{10,11... | collective-permute-start | bytes 1572872 | tf_op jit(solution)/shard_map/ppermute | solution.py:93
  19.9 23.3 %collective-permute-start.10 = (bf16[128,2048]{1,0:T(8,128)(2,1)S(1)}, bf16[128,2048]{1,0:T(8,128)(2,1)S(1)}, u32[]{:S(2)}, u32[]{:S(2)}) collective-permute-start(bf16[128,2048]{1,0:T(8,128)(2,1)S(1)} %pad_maximum_fusion.refs_1_), channel_id=1, source_target_pairs={{0,16},{1,17},{2,18},{3,19},{4,20},{5,21},{6,22},{7,23},{8,24},{9,... | collective-permute-start | bytes 1572872 | tf_op jit(solution)/shard_map/ppermute | solution.py:93
  20.5 10.9 %collective-permute-start.13 = (bf16[64,2048]{1,0:T(8,128)(2,1)S(1)}, bf16[64,2048]{1,0:T(8,128)(2,1)S(1)}, u32[]{:S(2)}, u32[]{:S(2)}) collective-permute-start(bf16[64,2048]{1,0:T(8,128)(2,1)S(1)} %collective-permute-done.12.refs_3_), channel_id=1, source_target_pairs={{0,8},{1,9},{2,4},{3,5},{4,2},{5,3},{6,14},{7,15},{8,0},{9,1},{10,... | collective-permute-start | bytes 786440 | tf_op jit(solution)/shard_map/ppermute | solution.py:93
  20.5 8.7 %collective-permute-start.5 = (bf16[64,2048]{1,0:T(8,128)(2,1)S(1)}, bf16[64,2048]{1,0:T(8,128)(2,1)S(1)}, u32[]{:S(2)}, u32[]{:S(2)}) collective-permute-start(bf16[64,2048]{1,0:T(8,128)(2,1)S(1)} %collective-permute-done.4), channel_id=1, source_target_pairs={{0,2},{1,3},{2,0},{3,1},{4,6},{5,7},{6,4},{7,5},{8,10},{9,11},{10,... | collective-permute-start | bytes 786440 | tf_op jit(solution)/shard_map/ppermute | solution.py:93
  24.9 13.6 %copy-start.2 = (bf16[2048,512]{1,0:T(8,128)(2,1)S(1)}, bf16[2048,512]{1,0:T(8,128)(2,1)}, u32[]{:S(2)}) copy-start(bf16[2048,512]{1,0:T(8,128)(2,1)} %constant.99.clone.table_low) | copy-start | bytes 6291460
  25.0 13.5 %copy-start = (bf16[1,64,2048]{2,1,0:T(8,128)(2,1)S(1)}, bf16[1,64,2048]{2,1,0:T(8,128)(2,1)}, u32[]{:S(2)}) copy-start(bf16[1,64,2048]{2,1,0:T(8,128)(2,1)} %param.10) | copy-start | bytes 786436
  25.0 13.5 %copy-start.1 = (bf16[2048,512]{1,0:T(8,128)(2,1)S(1)}, bf16[2048,512]{1,0:T(8,128)(2,1)}, u32[]{:S(2)}) copy-start(bf16[2048,512]{1,0:T(8,128)(2,1)} %constant.98.clone.table_high) | copy-start | bytes 6291460
  25.0 13.5 %copy-start.3 = (bf16[512,512]{1,0:T(8,128)(2,1)S(1)}, bf16[512,512]{1,0:T(8,128)(2,1)}, u32[]{:S(2)}) copy-start(bf16[512,512]{1,0:T(8,128)(2,1)} %constant.101.clone.back_ref) | copy-start | bytes 1572868
  25.1 13.5 %copy-start.4 = (f32[2,1024]{1,0:T(2,128)S(1)}, f32[2,1024]{1,0:T(2,128)}, u32[]{:S(2)}) copy-start(f32[2,1024]{1,0:T(2,128)} %constant.100.clone.first_ref) | copy-start | bytes 24580
  29.2 6.7 %collective-permute-start.8 = (bf16[64,2048]{1,0:T(8,128)(2,1)S(1)}, bf16[64,2048]{1,0:T(8,128)(2,1)S(1)}, u32[]{:S(2)}, u32[]{:S(2)}) collective-permute-start(bf16[64,2048]{1,0:T(8,128)(2,1)S(1)} %broadcast_select_fusion.2.refs_2_), channel_id=1, source_target_pairs={{0,1},{1,0},{2,3},{3,2},{4,5},{5,4},{6,7},{7,6},{8,9},{9,8},{10,11... | collective-permute-start | bytes 786440 | tf_op jit(solution)/shard_map/ppermute | solution.py:93
  29.8 7.3 %collective-permute-start.11 = (bf16[64,2048]{1,0:T(8,128)(2,1)S(1)}, bf16[64,2048]{1,0:T(8,128)(2,1)S(1)}, u32[]{:S(2)}, u32[]{:S(2)}) collective-permute-start(bf16[64,2048]{1,0:T(8,128)(2,1)S(1)} %broadcast_select_fusion.2.refs_2_), channel_id=1, source_target_pairs={{0,16},{1,17},{2,18},{3,19},{4,20},{5,21},{6,22},{7,23},{8,24},{9,... | collective-permute-start | bytes 786440 | tf_op jit(solution)/shard_map/ppermute | solution.py:93
  31.4 11.8 %collective-permute-start.14 = (bf16[128,2048]{1,0:T(8,128)(2,1)S(1)}, bf16[128,2048]{1,0:T(8,128)(2,1)S(1)}, u32[]{:S(2)}, u32[]{:S(2)}) collective-permute-start(bf16[128,2048]{1,0:T(8,128)(2,1)S(1)} %pad_maximum_fusion.1), channel_id=1, source_target_pairs={{0,2},{1,3},{2,0},{3,1},{4,6},{5,7},{6,4},{7,5},{8,10},{9,11},{10,... | collective-permute-start | bytes 1572872 | tf_op jit(solution)/shard_map/ppermute | solution.py:93
  37.2 6.4 %collective-permute-start.15 = (bf16[64,2048]{1,0:T(8,128)(2,1)S(1)}, bf16[64,2048]{1,0:T(8,128)(2,1)S(1)}, u32[]{:S(2)}, u32[]{:S(2)}) collective-permute-start(bf16[64,2048]{1,0:T(8,128)(2,1)S(1)} %broadcast_select_fusion), channel_id=1, source_target_pairs={{0,16},{1,17},{2,18},{3,19},{4,20},{5,21},{6,22},{7,23},{8,9},{9,8... | collective-permute-start | bytes 786440 | tf_op jit(solution)/shard_map/ppermute | solution.py:93
  47.3 2.7 %collective-permute-start.16 = (f32[256,1024]{1,0:T(8,128)S(1)}, f32[256,1024]{1,0:T(8,128)S(1)}, u32[]{:S(2)}, u32[]{:S(2)}) collective-permute-start(f32[256,1024]{1,0:T(8,128)S(1)} %get-tuple-element.24), channel_id=1, source_target_pairs={{0,8},{1,9},{2,10},{3,11},{4,12},{5,13},{6,14},{7,15},{8,0},{9,1},... | collective-permute-start | bytes 3145736 | tf_op jit(solution)/shard_map/ppermute | solution.py:93
